TPU v7x, 512 devices: a whole 4x8x8 slice. The times are simulated.
512 devices in a mesh: gx: 16 (over z, y_lo), gy: 8 (over y_hi, core), gz: 4 (over x).
Axes of the slice: x: 4, y: 8 (y_hi: 4, y_lo: 2; y = y_hi * 2 + y_lo), z: 8, core: 2. Of those that a mesh axis runs over, the one named last changes fastest.
Arguments:
- features: bfloat16 [32, 64, 32, 512], P(None, 'gx', 'gy', 'gz'), may hold values from -6 to 6
- cotangent: bfloat16 [32, 64, 32, 512], P(None, 'gx', 'gy', 'gz'), may hold values from -6 to 6
- w_fine_in: bfloat16 [27, 32, 32], replicated, may hold values from -0.21875 to 0.21875
- w_coarse_in: bfloat16 [27, 32, 128], replicated, may hold values from -0.21875 to 0.21875
- w_coarse_mid: bfloat16 [27, 128, 128], replicated, may hold values from -0.109375 to 0.109375
- w_lift: bfloat16 [128, 32], replicated, may hold values from -0.5 to 0.5
- w_fine_out: bfloat16 [27, 32, 32], replicated, may hold values from -0.21875 to 0.21875
Outputs:
- output: bfloat16 [32, 64, 32, 512], P(None, 'gx', 'gy', 'gz')
- grad_input: bfloat16 [32, 64, 32, 512], P(None, 'gx', 'gy', 'gz')
- grad_fine_in: float32 [27, 32, 32], P(None, 'gx', ('gy', 'gz'))
- grad_coarse_in: float32 [27, 32, 128], P(None, 'gx', ('gy', 'gz'))
- grad_coarse_mid: float32 [27, 128, 128], P(None, 'gx', ('gy', 'gz'))
- grad_lift: float32 [128, 32], P('gx', ('gy', 'gz'))
- grad_fine_out: float32 [27, 32, 32], P(None, 'gx', ('gy', 'gz'))
All inputs are finite; a program needn't handle non-finite values.
Results may differ from a plain program's by a relative error of at most 0.02.
Values may be sent and summed in bfloat16 or wider, within the bound.
No kernel may reach another device: no remote copies, remote signals or barrier semaphores. Data moves between devices by JAX's collectives and lax.ppermute only.
A program may use at most 128 MiB of HBM per device.

v0:
```python
import math

import jax
import jax.numpy as jnp
from jax import lax
from jax.sharding import Mesh
from jax.sharding import PartitionSpec as P

GX = ("gx_0", "gx_1")


def extended(cells, sides, width):
    for axis, dim in sides:
        count = lax.axis_size(axis)
        ends = count - 1
        head = lax.slice_in_dim(cells, 0, width, axis=dim)
        tail = lax.slice_in_dim(cells, cells.shape[dim] - width, cells.shape[dim], axis=dim)
        cells = jnp.concatenate(
            [
                lax.ppermute(tail, axis, [(i, (i + 1) % count) for i in range(ends)]),
                cells,
                lax.ppermute(head, axis, [((i + 1) % count, i) for i in range(ends)]),
            ],
            axis=dim,
        )
    return cells


def scatter_axes(shard, axes, dim):
    for axis in axes:
        shard = lax.psum_scatter(shard, axis, scatter_dimension=dim, tiled=True)
    return shard


def split_up(shard, dim, size):
    before, after = (shard.shape[:dim], shard.shape[dim + 1 :])
    return jnp.moveaxis(shard.reshape(*before, size, -1, *after), dim, 0)


def summed_on_arrival(shard, axis, dim):
    pieces = split_up(shard, dim, lax.axis_size(axis))
    arrived = lax.all_to_all(pieces, axis, split_axis=0, concat_axis=0, tiled=True)
    return arrived.sum(axis=0)


def silu_slope(values):
    sigma = jax.nn.sigmoid(values)
    return sigma * (1.0 + values * (1.0 - sigma))


def conv_valid(padded, weight):
    kernel = weight.reshape(3, 3, 3, weight.shape[1], weight.shape[2])
    result = lax.conv_general_dilated(
        padded[None],
        kernel,
        (1, 1, 1),
        "VALID",
        dimension_numbers=("NCDHW", "DHWIO", "NCDHW"),
        preferred_element_type=jnp.float32,
    )
    return result[0]


def flipped(weight):
    return jnp.flip(weight, 0).transpose(0, 2, 1)


def tap_grad_direct(padded, grad):
    depth = padded.shape[1] - 2
    height = padded.shape[2] - 2
    length = padded.shape[3] - 2
    flat_grad = grad.reshape(grad.shape[0], -1)
    blocks = []
    for tap in range(27):
        shift_x, shift_y, shift_z = (tap // 9, tap // 3 % 3, tap % 3)
        window = padded[
            :, shift_x : shift_x + depth, shift_y : shift_y + height, shift_z : shift_z + length
        ].reshape(padded.shape[0], -1)
        blocks.append(
            lax.dot_general(
                window, flat_grad, (((1,), (1,)), ((), ())), preferred_element_type=jnp.float32
            )
        )
    return jnp.stack(blocks)


def pool_blocks(field):
    chans, depth, height, length = field.shape
    grouped = field.astype(jnp.float32).reshape(
        chans, depth // 4, 4, height // 4, 4, length // 4, 4
    )
    return grouped.sum(axis=(2, 4, 6))


def spread_up(field):
    chans, depth, height, length = field.shape
    grown = jnp.broadcast_to(
        field[:, :, None, :, None, :, None], (chans, depth, 4, height, 4, length, 4)
    )
    return grown.reshape(chans, depth * 4, height * 4, length * 4)


def fine_rim(field):
    return extended(field, ((GX, 1), ("gy", 2), ("gz", 3)), 1)


def coarse_rim(field):
    return extended(field, ((GX, 1), ("gy", 2), ("gz", 3)), 1)


def reduce_joint(partials):
    count_x = lax.axis_size(GX)
    count_yz = lax.axis_size("gy") * lax.axis_size("gz")
    packed = []
    shapes = []
    for partial_value in partials:
        taps, rows, cols = partial_value.shape
        shapes.append((taps, rows // count_x, cols // count_yz))
        blocks = partial_value.reshape(taps, count_x, rows // count_x, count_yz, cols // count_yz)
        packed.append(blocks.transpose(1, 3, 0, 2, 4).reshape(count_x, count_yz, -1))
    joint = jnp.concatenate(packed, axis=2)
    joint = scatter_axes(joint, GX, 0)
    joint = summed_on_arrival(joint, ("gy", "gz"), 1)
    flat = joint[0, 0]
    results = []
    offset = 0
    for shape in shapes:
        span = shape[0] * shape[1] * shape[2]
        results.append(flat[offset : offset + span].reshape(shape))
        offset = offset + span
    return results


def shards(features, cotangent, w_fine_in, w_coarse_in, w_coarse_mid, w_lift, w_fine_out):
    depth, height, length = (features.shape[1], features.shape[2], features.shape[3])
    whole_cells = (
        depth * lax.axis_size(GX) * height * lax.axis_size("gy") * length * lax.axis_size("gz")
    )
    scale = 1.0 / math.sqrt(whole_cells)
    padded_in = fine_rim(features)
    z_first = conv_valid(padded_in, w_fine_in)
    act_first = jax.nn.silu(z_first).astype(jnp.bfloat16)
    pooled = (pool_blocks(act_first) / 64.0).astype(jnp.bfloat16)
    pooled_pad = coarse_rim(pooled)
    z_second = conv_valid(pooled_pad, w_coarse_in)
    act_second = jax.nn.silu(z_second).astype(jnp.bfloat16)
    second_pad = coarse_rim(act_second)
    z_third = conv_valid(second_pad, w_coarse_mid)
    act_third = jax.nn.silu(z_third).astype(jnp.bfloat16)
    lifted = lax.dot_general(
        w_lift, act_third, (((0,), (0,)), ((), ())), preferred_element_type=jnp.float32
    )
    joined = (act_first.astype(jnp.float32) + spread_up(lifted)).astype(jnp.bfloat16)
    padded_joined = fine_rim(joined)
    output = conv_valid(padded_joined, w_fine_out).astype(jnp.bfloat16)
    part_fine_out = tap_grad_direct(padded_joined, cotangent) * scale
    d_joined = conv_valid(fine_rim(cotangent), flipped(w_fine_out))
    d_lift = pool_blocks(d_joined)
    lift_partial = (
        lax.dot_general(
            act_third.astype(jnp.float32),
            d_lift,
            (((1, 2, 3), (1, 2, 3)), ((), ())),
            precision=lax.Precision.HIGHEST,
        )
        * scale
    )
    d_third = lax.dot_general(
        w_lift.astype(jnp.float32),
        d_lift,
        (((1,), (0,)), ((), ())),
        precision=lax.Precision.HIGHEST,
    )
    dz_third = (d_third * silu_slope(z_third)).astype(jnp.bfloat16)
    dz_third_pad = coarse_rim(dz_third)
    part_coarse_mid = None
    grad_coarse_mid = None
    part_coarse_mid = tap_grad_direct(second_pad, dz_third) * scale
    dz_second = (conv_valid(dz_third_pad, flipped(w_coarse_mid)) * silu_slope(z_second)).astype(
        jnp.bfloat16
    )
    dz_second_pad = coarse_rim(dz_second)
    part_coarse_in = tap_grad_direct(pooled_pad, dz_second) * scale
    d_pool = conv_valid(dz_second_pad, flipped(w_coarse_in))
    dz_first = ((d_joined + spread_up(d_pool) / 64.0) * silu_slope(z_first)).astype(jnp.bfloat16)
    part_fine_in = tap_grad_direct(padded_in, dz_first) * scale
    grad_input = conv_valid(fine_rim(dz_first), flipped(w_fine_in)).astype(jnp.bfloat16)
    pending = [part_fine_out, lift_partial[None], part_coarse_in, part_fine_in]
    pending.append(part_coarse_mid)
    reduced = reduce_joint(pending)
    grad_fine_out = reduced[0]
    grad_lift = reduced[1][0]
    grad_coarse_in = reduced[2]
    grad_fine_in = reduced[3]
    grad_coarse_mid = reduced[4]
    return (
        output,
        grad_input,
        grad_fine_in,
        grad_coarse_in,
        grad_coarse_mid,
        grad_lift,
        grad_fine_out,
    )


def solution(mesh):
    split = Mesh(
        mesh.devices.reshape(8, 2, mesh.shape["gy"], mesh.shape["gz"]), ("gx_0", "gx_1", "gy", "gz")
    )
    return jax.shard_map(
        shards,
        mesh=split,
        in_specs=(P(None, GX, "gy", "gz"), P(None, GX, "gy", "gz"), P(), P(), P(), P(), P()),
        out_specs=(
            P(None, GX, "gy", "gz"),
            P(None, GX, "gy", "gz"),
            P(None, GX, ("gy", "gz")),
            P(None, GX, ("gy", "gz")),
            P(None, GX, ("gy", "gz")),
            P(GX, ("gy", "gz")),
            P(None, GX, ("gy", "gz")),
        ),
        check_vma=False,
    )
```

profile of v0, /device:TPU:1, one launch (start us, length us, event | category | flops | bytes accessed | tf_op | source)
XLA Modules:
  0.0 412.0 jit_solution(4777733688109134482)
XLA Ops:
  8.1 4.0 collective-permute-start.24
  14.4 4.6 %collective-permute-start = (bf16[32,1,4,128]{3,0,2,1:T(8,128)(2,1)S(1)}, bf16[32,1,4,128]{3,0,2,1:T(8,128)(2,1)S(1)}, u32[]{:S(2)}, u32[]{:S(2)}) collective-permute-start(bf16[32,1,4,128]{3,0,2,1:T(8,128)(2,1)S(1)} %get-tuple-element.106), channel_id=1, source_target_pairs={{0,32},{32,64},{64,96},{96,128},{128,160},{160,192},{192,224},{224... | collective-permute-start | bytes 98312 | tf_op jit(solution)/shard_map/ppermute | solution.py:20
  25.0 6.1 %collective-permute-start.27 = (bf16[32,6,1,128]{3,2,1,0:T(2,128)(2,1)S(1)}, bf16[32,6,1,128]{3,2,1,0:T(2,128)(2,1)S(1)}, u32[]{:S(2)}, u32[]{:S(2)}) collective-permute-start(bf16[32,6,1,128]{3,2,1,0:T(2,128)(2,1)S(1)} %get-tuple-element.92), channel_id=1, source_target_pairs={{4,0},{8,4},{12,8},{16,12},{20,16},{24,20},{28,24},{5,1},{9,5},{13... | collective-permute-start | bytes 147464 | tf_op jit(solution)/shard_map/ppermute | solution.py:22
  31.1 1.9 collective-permute-start.26
  33.1 2.4 collective-permute-start.3
  35.5 4.1 collective-permute-start.2
  43.1 4.7 %collective-permute-start.28 = (bf16[32,6,6,1]{3,2,1,0:T(8,128)(2,1)}, bf16[32,6,6,1]{3,2,1,0:T(8,128)(2,1)}, u32[]{:S(2)}, u32[]{:S(2)}) collective-permute-start(bf16[32,6,6,1]{3,2,1,0:T(8,128)(2,1)} %get-tuple-element.64), channel_id=1, source_target_pairs={{0,1},{1,2},{2,3},{4,5},{5,6},{6,7},{8,9},{9,10},{10,11},{12,13},{... | collective-permute-start | bytes 6920 | tf_op jit(solution)/shard_map/ppermute | solution.py:20
  49.4 4.0 collective-permute-start.4
  54.3 5.6 %collective-permute-done.5 = bf16[32,6,6,1]{3,0,2,1:T(8,128)(2,1)S(1)} collective-permute-done((bf16[32,6,6,1]{3,0,2,1:T(8,128)(2,1)S(1)}, bf16[32,6,6,1]{3,0,2,1:T(8,128)(2,1)S(1)}, u32[]{:S(2)}, u32[]{:S(2)}) %collective-permute-start.5) | collective-permute-done | bytes 2336 | tf_op jit(solution)/shard_map/ppermute | solution.py:22
  64.6 3.0 copy.977
  68.6 5.0 %add_multiply_fusion = (f32[4,4,8,17,32]{4,2,3,1,0:T(8,128)}, f32[4,4,8,17,32]{4,2,3,1,0:T(8,128)S(1)}, f32[4,4,8,17,32]{4,2,3,1,0:T(8,128)}) fusion(bf16[3,3,3,32,32]{4,3,2,1,0:T(8,128)(2,1)S(1)} %bitcast.1289, bf16[32,6,6,1,7,2]{0,4,5,2,1,3:T(8,128)(2,1)S(1)} %slice.668, bf16[32,6,6,1,8,17]{0,4,5,2,1,3:T(8,128)(2,1)} %copy.977, ...), kind=kOutput, calls=%fused_computation.144 | convolution fusion | flops 122140672 | bytes 1236616 | tf_op jit(solution)/shard_map/conv_general_dilated | solution.py:53
  76.4 5.1 %collective-permute-start.6 = (bf16[32,1,1,32]{0,3,2,1:T(8,128)(2,1)S(1)}, bf16[32,1,1,32]{0,3,2,1:T(8,128)(2,1)S(1)}, u32[]{:S(2)}, u32[]{:S(2)}) collective-permute-start(bf16[32,1,1,32]{0,3,2,1:T(8,128)(2,1)S(1)} %fusion.541), channel_id=1, source_target_pairs={{0,32},{32,64},{64,96},{96,128},{128,160},{160,192},{192,224},{224... | collective-permute-start | bytes 6152 | tf_op jit(solution)/shard_map/ppermute | solution.py:20
  81.5 2.3 maximum_bitcast_fusion
  84.0 2.0 reshape.2414
  86.0 3.9 copy.996
  90.9 3.1 fusion.38
  97.0 1.9 collective-permute-start.9
  98.9 4.5 %collective-permute-start.8 = (bf16[32,3,1,32]{0,3,2,1:T(8,128)(2,1)S(1)}, bf16[32,3,1,32]{0,3,2,1:T(8,128)(2,1)S(1)}, u32[]{:S(2)}, u32[]{:S(2)}) collective-permute-start(bf16[32,3,1,32]{0,3,2,1:T(8,128)(2,1)S(1)} %pad_maximum_fusion.17), channel_id=1, source_target_pairs={{0,4},{4,8},{8,12},{12,16},{16,20},{20,24},{24,28},{1,5},{5,9},{9,... | collective-permute-start | bytes 18440 | tf_op jit(solution)/shard_map/ppermute | solution.py:20
  106.9 4.4 %collective-permute-start.10 = (bf16[32,3,3,1]{0,3,2,1:T(2,128)(2,1)S(1)}, bf16[32,3,3,1]{0,3,2,1:T(2,128)(2,1)S(1)}, u32[]{:S(2)}, u32[]{:S(2)}) collective-permute-start(bf16[32,3,3,1]{0,3,2,1:T(2,128)(2,1)S(1)} %get-tuple-element.149), channel_id=1, source_target_pairs={{0,1},{1,2},{2,3},{4,5},{5,6},{6,7},{8,9},{9,10},{10,11},{12,13},{... | collective-permute-start | bytes 1736 | tf_op jit(solution)/shard_map/ppermute | solution.py:20
  116.4 4.9 %collective-permute-start.12 = (bf16[128,1,1,32]{0,3,2,1:T(8,128)(2,1)S(1)}, bf16[128,1,1,32]{0,3,2,1:T(8,128)(2,1)S(1)}, u32[]{:S(2)}, u32[]{:S(2)}) collective-permute-start(bf16[128,1,1,32]{0,3,2,1:T(8,128)(2,1)S(1)} %multiply_convert_fusion.5), channel_id=1, source_target_pairs={{0,32},{32,64},{64,96},{96,128},{128,160},{160,192},{192,224},{224... | collective-permute-start | bytes 24584 | tf_op jit(solution)/shard_map/ppermute | solution.py:20
  124.0 5.1 %collective-permute-start.14 = (bf16[128,3,1,32]{0,3,2,1:T(8,128)(2,1)S(1)}, bf16[128,3,1,32]{0,3,2,1:T(8,128)(2,1)S(1)}, u32[]{:S(2)}, u32[]{:S(2)}) collective-permute-start(bf16[128,3,1,32]{0,3,2,1:T(8,128)(2,1)S(1)} %pad_maximum_fusion.18), channel_id=1, source_target_pairs={{0,4},{4,8},{8,12},{12,16},{16,20},{20,24},{24,28},{1,5},{5,9},{9,... | collective-permute-start | bytes 73736 | tf_op jit(solution)/shard_map/ppermute | solution.py:20
  131.3 4.3 %collective-permute-start.16 = (bf16[128,3,3,1]{0,3,2,1:T(2,128)(2,1)S(1)}, bf16[128,3,3,1]{0,3,2,1:T(2,128)(2,1)S(1)}, u32[]{:S(2)}, u32[]{:S(2)}) collective-permute-start(bf16[128,3,3,1]{0,3,2,1:T(2,128)(2,1)S(1)} %get-tuple-element.147), channel_id=1, source_target_pairs={{0,1},{1,2},{2,3},{4,5},{5,6},{6,7},{8,9},{9,10},{10,11},{12,13},{... | collective-permute-start | bytes 6920 | tf_op jit(solution)/shard_map/ppermute | solution.py:20
  139.8 5.2 %collective-permute-start.30 = (bf16[128,1,1,32]{0,3,2,1:T(8,128)(2,1)S(1)}, bf16[128,1,1,32]{0,3,2,1:T(8,128)(2,1)S(1)}, u32[]{:S(2)}, u32[]{:S(2)}) collective-permute-start(bf16[128,1,1,32]{0,3,2,1:T(8,128)(2,1)S(1)} %bitcast.1352), channel_id=1, source_target_pairs={{0,32},{32,64},{64,96},{96,128},{128,160},{160,192},{192,224},{224... | collective-permute-start | bytes 24584 | tf_op jit(solution)/shard_map/ppermute | solution.py:20
  161.4 5.7 %collective-permute-start.32 = (bf16[128,3,1,32]{0,3,2,1:T(8,128)(2,1)S(1)}, bf16[128,3,1,32]{0,3,2,1:T(8,128)(2,1)S(1)}, u32[]{:S(2)}, u32[]{:S(2)}) collective-permute-start(bf16[128,3,1,32]{0,3,2,1:T(8,128)(2,1)S(1)} %pad_maximum_fusion.19), channel_id=1, source_target_pairs={{0,4},{4,8},{8,12},{12,16},{16,20},{20,24},{24,28},{1,5},{5,9},{9,... | collective-permute-start | bytes 73736 | tf_op jit(solution)/shard_map/ppermute | solution.py:20
  169.3 4.5 %collective-permute-start.34 = (bf16[128,3,3,1]{0,3,2,1:T(2,128)(2,1)S(1)}, bf16[128,3,3,1]{0,3,2,1:T(2,128)(2,1)S(1)}, u32[]{:S(2)}, u32[]{:S(2)}) collective-permute-start(bf16[128,3,3,1]{0,3,2,1:T(2,128)(2,1)S(1)} %get-tuple-element.145), channel_id=1, source_target_pairs={{0,1},{1,2},{2,3},{4,5},{5,6},{6,7},{8,9},{9,10},{10,11},{12,13},{... | collective-permute-start | bytes 6920 | tf_op jit(solution)/shard_map/ppermute | solution.py:20
  178.2 5.4 %collective-permute-start.36 = (bf16[128,1,1,32]{0,3,2,1:T(8,128)(2,1)S(1)}, bf16[128,1,1,32]{0,3,2,1:T(8,128)(2,1)S(1)}, u32[]{:S(2)}, u32[]{:S(2)}) collective-permute-start(bf16[128,1,1,32]{0,3,2,1:T(8,128)(2,1)S(1)} %fusion.340), channel_id=1, source_target_pairs={{0,32},{32,64},{64,96},{96,128},{128,160},{160,192},{192,224},{224... | collective-permute-start | bytes 24584 | tf_op jit(solution)/shard_map/ppermute | solution.py:20
  196.7 7.5 %broadcast_multiply_fusion = f32[27,16,8,32,4]{3,1,4,2,0:T(8,128)} fusion(f32[27,16,8,32,4]{3,1,4,2,0:T(8,128)} %fusion.50), kind=kLoop, calls=%fused_computation | loop fusion | flops 442368 | bytes 3538944 | tf_op jit(solution)/shard_map/mul | solution.py:178
  210.5 5.7 %collective-permute-start.38 = (bf16[128,3,1,32]{0,3,2,1:T(8,128)(2,1)S(1)}, bf16[128,3,1,32]{0,3,2,1:T(8,128)(2,1)S(1)}, u32[]{:S(2)}, u32[]{:S(2)}) collective-permute-start(bf16[128,3,1,32]{0,3,2,1:T(8,128)(2,1)S(1)} %pad_maximum_fusion.20), channel_id=1, source_target_pairs={{0,4},{4,8},{8,12},{12,16},{16,20},{20,24},{24,28},{1,5},{5,9},{9,... | collective-permute-start | bytes 73736 | tf_op jit(solution)/shard_map/ppermute | solution.py:20
  218.4 4.3 %collective-permute-start.40 = (bf16[128,3,3,1]{0,3,2,1:T(2,128)(2,1)S(1)}, bf16[128,3,3,1]{0,3,2,1:T(2,128)(2,1)S(1)}, u32[]{:S(2)}, u32[]{:S(2)}) collective-permute-start(bf16[128,3,3,1]{0,3,2,1:T(2,128)(2,1)S(1)} %get-tuple-element.143), channel_id=1, source_target_pairs={{0,1},{1,2},{2,3},{4,5},{5,6},{6,7},{8,9},{9,10},{10,11},{12,13},{... | collective-permute-start | bytes 6920 | tf_op jit(solution)/shard_map/ppermute | solution.py:20
  223.7 5.1 %copy.1272 = f32[16,32,864]{2,1,0:T(8,128)S(1)} copy(f32[16,32,864]{1,0,2:T(8,128)} %bitcast.1217) | data formatting | bytes 3538944 | tf_op jit(solution)/shard_map/reshape | solution.py:120
  233.9 5.3 %collective-permute-start.18 = (bf16[32,1,4,128]{3,0,2,1:T(8,128)(2,1)S(1)}, bf16[32,1,4,128]{3,0,2,1:T(8,128)(2,1)S(1)}, u32[]{:S(2)}, u32[]{:S(2)}) collective-permute-start(bf16[32,1,4,128]{3,0,2,1:T(8,128)(2,1)S(1)} %get-tuple-element.103), channel_id=1, source_target_pairs={{0,32},{32,64},{64,96},{96,128},{128,160},{160,192},{192,224},{224... | collective-permute-start | bytes 98312 | tf_op jit(solution)/shard_map/ppermute | solution.py:20
  256.3 2.0 copy.1271
  260.3 5.8 %collective-permute-start.20 = (bf16[32,6,1,128]{3,0,2,1:T(8,128)(2,1)S(1)}, bf16[32,6,1,128]{3,0,2,1:T(8,128)(2,1)S(1)}, u32[]{:S(2)}, u32[]{:S(2)}) collective-permute-start(bf16[32,6,1,128]{3,0,2,1:T(8,128)(2,1)S(1)} %get-tuple-element.93), channel_id=1, source_target_pairs={{0,4},{4,8},{8,12},{12,16},{16,20},{20,24},{24,28},{1,5},{5,9},{9,... | collective-permute-start | bytes 147464 | tf_op jit(solution)/shard_map/ppermute | solution.py:20
  269.7 4.1 %collective-permute-start.22 = (bf16[32,6,6,1]{3,0,2,1:T(8,128)(2,1)S(1)}, bf16[32,6,6,1]{3,0,2,1:T(8,128)(2,1)S(1)}, u32[]{:S(2)}, u32[]{:S(2)}) collective-permute-start(bf16[32,6,6,1]{3,0,2,1:T(8,128)(2,1)S(1)} %get-tuple-element.72), channel_id=1, source_target_pairs={{0,1},{1,2},{2,3},{4,5},{5,6},{6,7},{8,9},{9,10},{10,11},{12,13},{... | collective-permute-start | bytes 6920 | tf_op jit(solution)/shard_map/ppermute | solution.py:20
  274.0 2.0 collective-permute-done.23
  283.1 3.8 concatenate.251
  288.5 5.1 %collective-permute-start.42 = (bf16[32,1,4,128]{3,0,2,1:T(8,128)(2,1)S(1)}, bf16[32,1,4,128]{3,0,2,1:T(8,128)(2,1)S(1)}, u32[]{:S(2)}, u32[]{:S(2)}) collective-permute-start(bf16[32,1,4,128]{3,0,2,1:T(8,128)(2,1)S(1)} %get-tuple-element.99), channel_id=1, source_target_pairs={{0,32},{32,64},{64,96},{96,128},{128,160},{160,192},{192,224},{224... | collective-permute-start | bytes 98312 | tf_op jit(solution)/shard_map/ppermute | solution.py:20
  294.7 1.9 collective-permute-start.45
  296.6 8.2 %collective-permute-start.44 = (bf16[32,6,1,128]{3,0,2,1:T(8,128)(2,1)S(1)}, bf16[32,6,1,128]{3,0,2,1:T(8,128)(2,1)S(1)}, u32[]{:S(2)}, u32[]{:S(2)}) collective-permute-start(bf16[32,6,1,128]{3,0,2,1:T(8,128)(2,1)S(1)} %get-tuple-element.89), channel_id=1, source_target_pairs={{0,4},{4,8},{8,12},{12,16},{16,20},{20,24},{24,28},{1,5},{5,9},{9,... | collective-permute-start | bytes 147464 | tf_op jit(solution)/shard_map/ppermute | solution.py:20
  308.2 5.5 %collective-permute-start.46 = (bf16[32,6,6,1]{3,0,2,1:T(8,128)(2,1)}, bf16[32,6,6,1]{3,0,2,1:T(8,128)(2,1)}, u32[]{:S(2)}, u32[]{:S(2)}) collective-permute-start(bf16[32,6,6,1]{3,0,2,1:T(8,128)(2,1)} %get-tuple-element.70), channel_id=1, source_target_pairs={{0,1},{1,2},{2,3},{4,5},{5,6},{6,7},{8,9},{9,10},{10,11},{12,13},{... | collective-permute-start | bytes 6920 | tf_op jit(solution)/shard_map/ppermute | solution.py:20
  316.0 3.0 copy.992
  320.0 32.5 %reduce-scatter.3.cloned.1.call-done = f32[2,32,1196]{2,1,0:T(8,128)} async-done(((f32[16,32,1196]{2,1,0:T(8,128)}), f32[2,32,1196]{2,1,0:T(8,128)}) %reduce-scatter.3.cloned.1.call-update) | async-done | bytes 306192 | tf_op jit(solution)/shard_map/reduce_scatter | solution.py:31
  352.6 3.4 fusion.44
  359.5 3.0 copy.1009
  363.5 3.0 fusion.47
  366.5 11.4 %reduce-scatter.5.cloned.1.call-done = f32[1,32,1196]{2,1,0:T(8,128)} async-done(((f32[2,32,1196]{2,1,0:T(8,128)}), f32[1,32,1196]{2,1,0:T(8,128)}) %reduce-scatter.5.cloned.1.call-update) | async-done | bytes 153104 | tf_op jit(solution)/shard_map/reduce_scatter | solution.py:31
  379.7 9.1 %all-to-all-start = ((f32[32,1,1,1196]{3,2,1,0:T(1,128)}), f32[32,1,1,1196]{3,2,1,0:T(1,128)S(1)}, u32[]{:S(2)}, u32[]{:S(2)}) async-start(f32[32,1,1,1196]{3,2,1,0:T(1,128)} %copy.1273), calls=%async_computation.2 | async-start | bytes 327680 | tf_op jit(solution)/shard_map/all_to_all | solution.py:42
  391.2 9.3 %all-to-all-done = f32[32,1,1,1196]{3,2,1,0:T(1,128)S(1)} async-done(((f32[32,1,1,1196]{3,2,1,0:T(1,128)}), f32[32,1,1,1196]{3,2,1,0:T(1,128)S(1)}, u32[]{:S(2)}, u32[]{:S(2)}) %all-to-all-start) | async-done | bytes 153120 | tf_op jit(solution)/shard_map/all_to_all | solution.py:42
  (543 shorter events, 146.1 us)
Async XLA Ops:
  7.2 345.3 %reduce-scatter.3.cloned.1.call-start = ((), (), s32[]{:S(2)}) async-start(), calls=%async_computation.3 | async-start | bytes 2949120 | tf_op jit(solution)/shard_map/reduce_scatter | solution.py:31
  8.1 16.6 %collective-permute-start.24 = (bf16[32,1,4,128]{3,2,1,0:T(4,128)(2,1)S(1)}, bf16[32,1,4,128]{3,2,1,0:T(4,128)(2,1)S(1)}, u32[]{:S(2)}, u32[]{:S(2)}) collective-permute-start(bf16[32,1,4,128]{3,2,1,0:T(4,128)(2,1)S(1)} %get-tuple-element.102), channel_id=1, source_target_pairs={{0,32},{32,64},{64,96},{96,128},{128,160},{160,192},{192,224},{224... | collective-permute-start | bytes 98312 | tf_op jit(solution)/shard_map/ppermute | solution.py:20
  12.2 12.6 %collective-permute-start.25 = (bf16[32,1,4,128]{3,2,1,0:T(4,128)(2,1)S(1)}, bf16[32,1,4,128]{3,2,1,0:T(4,128)(2,1)S(1)}, u32[]{:S(2)}, u32[]{:S(2)}) collective-permute-start(bf16[32,1,4,128]{3,2,1,0:T(4,128)(2,1)S(1)} %get-tuple-element.101), channel_id=1, source_target_pairs={{32,0},{64,32},{96,64},{128,96},{160,128},{192,160},{224,192},{256... | collective-permute-start | bytes 98312 | tf_op jit(solution)/shard_map/ppermute | solution.py:22
  14.4 18.6 %collective-permute-start = (bf16[32,1,4,128]{3,0,2,1:T(8,128)(2,1)S(1)}, bf16[32,1,4,128]{3,0,2,1:T(8,128)(2,1)S(1)}, u32[]{:S(2)}, u32[]{:S(2)}) collective-permute-start(bf16[32,1,4,128]{3,0,2,1:T(8,128)(2,1)S(1)} %get-tuple-element.106), channel_id=1, source_target_pairs={{0,32},{32,64},{64,96},{96,128},{128,160},{160,192},{192,224},{224... | collective-permute-start | bytes 98312 | tf_op jit(solution)/shard_map/ppermute | solution.py:20
  19.1 14.0 %collective-permute-start.1 = (bf16[32,1,4,128]{3,0,2,1:T(8,128)(2,1)S(1)}, bf16[32,1,4,128]{3,0,2,1:T(8,128)(2,1)S(1)}, u32[]{:S(2)}, u32[]{:S(2)}) collective-permute-start(bf16[32,1,4,128]{3,0,2,1:T(8,128)(2,1)S(1)} %get-tuple-element.105), channel_id=1, source_target_pairs={{32,0},{64,32},{96,64},{128,96},{160,128},{192,160},{224,192},{256... | collective-permute-start | bytes 98312 | tf_op jit(solution)/shard_map/ppermute | solution.py:22
  25.0 15.4 %collective-permute-start.27 = (bf16[32,6,1,128]{3,2,1,0:T(2,128)(2,1)S(1)}, bf16[32,6,1,128]{3,2,1,0:T(2,128)(2,1)S(1)}, u32[]{:S(2)}, u32[]{:S(2)}) collective-permute-start(bf16[32,6,1,128]{3,2,1,0:T(2,128)(2,1)S(1)} %get-tuple-element.92), channel_id=1, source_target_pairs={{4,0},{8,4},{12,8},{16,12},{20,16},{24,20},{28,24},{5,1},{9,5},{13... | collective-permute-start | bytes 147464 | tf_op jit(solution)/shard_map/ppermute | solution.py:22
  31.1 9.3 %collective-permute-start.26 = (bf16[32,6,1,128]{3,2,1,0:T(2,128)(2,1)S(1)}, bf16[32,6,1,128]{3,2,1,0:T(2,128)(2,1)S(1)}, u32[]{:S(2)}, u32[]{:S(2)}) collective-permute-start(bf16[32,6,1,128]{3,2,1,0:T(2,128)(2,1)S(1)} %get-tuple-element.91), channel_id=1, source_target_pairs={{0,4},{4,8},{8,12},{12,16},{16,20},{20,24},{24,28},{1,5},{5,9},{9,... | collective-permute-start | bytes 147464 | tf_op jit(solution)/shard_map/ppermute | solution.py:20
  33.1 14.7 %collective-permute-start.3 = (bf16[32,6,1,128]{3,0,2,1:T(8,128)(2,1)S(1)}, bf16[32,6,1,128]{3,0,2,1:T(8,128)(2,1)S(1)}, u32[]{:S(2)}, u32[]{:S(2)}) collective-permute-start(bf16[32,6,1,128]{3,0,2,1:T(8,128)(2,1)S(1)} %get-tuple-element.96), channel_id=1, source_target_pairs={{4,0},{8,4},{12,8},{16,12},{20,16},{24,20},{28,24},{5,1},{9,5},{13... | collective-permute-start | bytes 147464 | tf_op jit(solution)/shard_map/ppermute | solution.py:22
  35.5 12.3 %collective-permute-start.2 = (bf16[32,6,1,128]{3,0,2,1:T(8,128)(2,1)S(1)}, bf16[32,6,1,128]{3,0,2,1:T(8,128)(2,1)S(1)}, u32[]{:S(2)}, u32[]{:S(2)}) collective-permute-start(bf16[32,6,1,128]{3,0,2,1:T(8,128)(2,1)S(1)} %get-tuple-element.95), channel_id=1, source_target_pairs={{0,4},{4,8},{8,12},{12,16},{16,20},{20,24},{24,28},{1,5},{5,9},{9,... | collective-permute-start | bytes 147464 | tf_op jit(solution)/shard_map/ppermute | solution.py:20
  41.8 39.7 %collective-permute-start.29 = (bf16[32,6,6,1]{3,2,1,0:T(8,128)(2,1)}, bf16[32,6,6,1]{3,2,1,0:T(8,128)(2,1)}, u32[]{:S(2)}, u32[]{:S(2)}) collective-permute-start(bf16[32,6,6,1]{3,2,1,0:T(8,128)(2,1)} %get-tuple-element.65), channel_id=1, source_target_pairs={{1,0},{2,1},{3,2},{5,4},{6,5},{7,6},{9,8},{10,9},{11,10},{13,12},{... | collective-permute-start | bytes 6920 | tf_op jit(solution)/shard_map/ppermute | solution.py:22
  43.1 38.4 %collective-permute-start.28 = (bf16[32,6,6,1]{3,2,1,0:T(8,128)(2,1)}, bf16[32,6,6,1]{3,2,1,0:T(8,128)(2,1)}, u32[]{:S(2)}, u32[]{:S(2)}) collective-permute-start(bf16[32,6,6,1]{3,2,1,0:T(8,128)(2,1)} %get-tuple-element.64), channel_id=1, source_target_pairs={{0,1},{1,2},{2,3},{4,5},{5,6},{6,7},{8,9},{9,10},{10,11},{12,13},{... | collective-permute-start | bytes 6920 | tf_op jit(solution)/shard_map/ppermute | solution.py:20
  48.1 11.8 %collective-permute-start.5 = (bf16[32,6,6,1]{3,0,2,1:T(8,128)(2,1)S(1)}, bf16[32,6,6,1]{3,0,2,1:T(8,128)(2,1)S(1)}, u32[]{:S(2)}, u32[]{:S(2)}) collective-permute-start(bf16[32,6,6,1]{3,0,2,1:T(8,128)(2,1)S(1)} %get-tuple-element.75), channel_id=1, source_target_pairs={{1,0},{2,1},{3,2},{5,4},{6,5},{7,6},{9,8},{10,9},{11,10},{13,12},{... | collective-permute-start | bytes 6920 | tf_op jit(solution)/shard_map/ppermute | solution.py:22
  49.4 12.3 %collective-permute-start.4 = (bf16[32,6,6,1]{3,0,2,1:T(8,128)(2,1)S(1)}, bf16[32,6,6,1]{3,0,2,1:T(8,128)(2,1)S(1)}, u32[]{:S(2)}, u32[]{:S(2)}) collective-permute-start(bf16[32,6,6,1]{3,0,2,1:T(8,128)(2,1)S(1)} %get-tuple-element.74), channel_id=1, source_target_pairs={{0,1},{1,2},{2,3},{4,5},{5,6},{6,7},{8,9},{9,10},{10,11},{12,13},{... | collective-permute-start | bytes 6920 | tf_op jit(solution)/shard_map/ppermute | solution.py:20
  75.1 21.8 %collective-permute-start.7 = (bf16[32,1,1,32]{0,3,2,1:T(8,128)(2,1)S(1)}, bf16[32,1,1,32]{0,3,2,1:T(8,128)(2,1)S(1)}, u32[]{:S(2)}, u32[]{:S(2)}) collective-permute-start(bf16[32,1,1,32]{0,3,2,1:T(8,128)(2,1)S(1)} %fusion.541), channel_id=1, source_target_pairs={{32,0},{64,32},{96,64},{128,96},{160,128},{192,160},{224,192},{256... | collective-permute-start | bytes 6152 | tf_op jit(solution)/shard_map/ppermute | solution.py:22
  76.4 20.6 %collective-permute-start.6 = (bf16[32,1,1,32]{0,3,2,1:T(8,128)(2,1)S(1)}, bf16[32,1,1,32]{0,3,2,1:T(8,128)(2,1)S(1)}, u32[]{:S(2)}, u32[]{:S(2)}) collective-permute-start(bf16[32,1,1,32]{0,3,2,1:T(8,128)(2,1)S(1)} %fusion.541), channel_id=1, source_target_pairs={{0,32},{32,64},{64,96},{96,128},{128,160},{160,192},{192,224},{224... | collective-permute-start | bytes 6152 | tf_op jit(solution)/shard_map/ppermute | solution.py:20
  97.0 8.5 %collective-permute-start.9 = (bf16[32,3,1,32]{0,3,2,1:T(8,128)(2,1)S(1)}, bf16[32,3,1,32]{0,3,2,1:T(8,128)(2,1)S(1)}, u32[]{:S(2)}, u32[]{:S(2)}) collective-permute-start(bf16[32,3,1,32]{0,3,2,1:T(8,128)(2,1)S(1)} %pad_maximum_fusion.17), channel_id=1, source_target_pairs={{4,0},{8,4},{12,8},{16,12},{20,16},{24,20},{28,24},{5,1},{9,5},{13... | collective-permute-start | bytes 18440 | tf_op jit(solution)/shard_map/ppermute | solution.py:22
  98.9 6.6 %collective-permute-start.8 = (bf16[32,3,1,32]{0,3,2,1:T(8,128)(2,1)S(1)}, bf16[32,3,1,32]{0,3,2,1:T(8,128)(2,1)S(1)}, u32[]{:S(2)}, u32[]{:S(2)}) collective-permute-start(bf16[32,3,1,32]{0,3,2,1:T(8,128)(2,1)S(1)} %pad_maximum_fusion.17), channel_id=1, source_target_pairs={{0,4},{4,8},{8,12},{12,16},{16,20},{20,24},{24,28},{1,5},{5,9},{9,... | collective-permute-start | bytes 18440 | tf_op jit(solution)/shard_map/ppermute | solution.py:20
  105.6 8.7 %collective-permute-start.11 = (bf16[32,3,3,1]{0,3,2,1:T(2,128)(2,1)S(1)}, bf16[32,3,3,1]{0,3,2,1:T(2,128)(2,1)S(1)}, u32[]{:S(2)}, u32[]{:S(2)}) collective-permute-start(bf16[32,3,3,1]{0,3,2,1:T(2,128)(2,1)S(1)} %get-tuple-element.150), channel_id=1, source_target_pairs={{1,0},{2,1},{3,2},{5,4},{6,5},{7,6},{9,8},{10,9},{11,10},{13,12},{... | collective-permute-start | bytes 1736 | tf_op jit(solution)/shard_map/ppermute | solution.py:22
  106.9 7.4 %collective-permute-start.10 = (bf16[32,3,3,1]{0,3,2,1:T(2,128)(2,1)S(1)}, bf16[32,3,3,1]{0,3,2,1:T(2,128)(2,1)S(1)}, u32[]{:S(2)}, u32[]{:S(2)}) collective-permute-start(bf16[32,3,3,1]{0,3,2,1:T(2,128)(2,1)S(1)} %get-tuple-element.149), channel_id=1, source_target_pairs={{0,1},{1,2},{2,3},{4,5},{5,6},{6,7},{8,9},{9,10},{10,11},{12,13},{... | collective-permute-start | bytes 1736 | tf_op jit(solution)/shard_map/ppermute | solution.py:20
  115.1 6.3 %collective-permute-start.13 = (bf16[128,1,1,32]{0,3,2,1:T(8,128)(2,1)S(1)}, bf16[128,1,1,32]{0,3,2,1:T(8,128)(2,1)S(1)}, u32[]{:S(2)}, u32[]{:S(2)}) collective-permute-start(bf16[128,1,1,32]{0,3,2,1:T(8,128)(2,1)S(1)} %multiply_convert_fusion.5), channel_id=1, source_target_pairs={{32,0},{64,32},{96,64},{128,96},{160,128},{192,160},{224,192},{256... | collective-permute-start | bytes 24584 | tf_op jit(solution)/shard_map/ppermute | solution.py:22
  122.1 7.2 %collective-permute-start.15 = (bf16[128,3,1,32]{0,3,2,1:T(8,128)(2,1)S(1)}, bf16[128,3,1,32]{0,3,2,1:T(8,128)(2,1)S(1)}, u32[]{:S(2)}, u32[]{:S(2)}) collective-permute-start(bf16[128,3,1,32]{0,3,2,1:T(8,128)(2,1)S(1)} %pad_maximum_fusion.18), channel_id=1, source_target_pairs={{4,0},{8,4},{12,8},{16,12},{20,16},{24,20},{28,24},{5,1},{9,5},{13... | collective-permute-start | bytes 73736 | tf_op jit(solution)/shard_map/ppermute | solution.py:22
  130.0 7.8 %collective-permute-start.17 = (bf16[128,3,3,1]{0,3,2,1:T(2,128)(2,1)S(1)}, bf16[128,3,3,1]{0,3,2,1:T(2,128)(2,1)S(1)}, u32[]{:S(2)}, u32[]{:S(2)}) collective-permute-start(bf16[128,3,3,1]{0,3,2,1:T(2,128)(2,1)S(1)} %get-tuple-element.148), channel_id=1, source_target_pairs={{1,0},{2,1},{3,2},{5,4},{6,5},{7,6},{9,8},{10,9},{11,10},{13,12},{... | collective-permute-start | bytes 6920 | tf_op jit(solution)/shard_map/ppermute | solution.py:22
  131.3 6.5 %collective-permute-start.16 = (bf16[128,3,3,1]{0,3,2,1:T(2,128)(2,1)S(1)}, bf16[128,3,3,1]{0,3,2,1:T(2,128)(2,1)S(1)}, u32[]{:S(2)}, u32[]{:S(2)}) collective-permute-start(bf16[128,3,3,1]{0,3,2,1:T(2,128)(2,1)S(1)} %get-tuple-element.147), channel_id=1, source_target_pairs={{0,1},{1,2},{2,3},{4,5},{5,6},{6,7},{8,9},{9,10},{10,11},{12,13},{... | collective-permute-start | bytes 6920 | tf_op jit(solution)/shard_map/ppermute | solution.py:20
  138.5 20.9 %collective-permute-start.31 = (bf16[128,1,1,32]{0,3,2,1:T(8,128)(2,1)S(1)}, bf16[128,1,1,32]{0,3,2,1:T(8,128)(2,1)S(1)}, u32[]{:S(2)}, u32[]{:S(2)}) collective-permute-start(bf16[128,1,1,32]{0,3,2,1:T(8,128)(2,1)S(1)} %bitcast.1351), channel_id=1, source_target_pairs={{32,0},{64,32},{96,64},{128,96},{160,128},{192,160},{224,192},{256... | collective-permute-start | bytes 24584 | tf_op jit(solution)/shard_map/ppermute | solution.py:22
  139.8 19.6 %collective-permute-start.30 = (bf16[128,1,1,32]{0,3,2,1:T(8,128)(2,1)S(1)}, bf16[128,1,1,32]{0,3,2,1:T(8,128)(2,1)S(1)}, u32[]{:S(2)}, u32[]{:S(2)}) collective-permute-start(bf16[128,1,1,32]{0,3,2,1:T(8,128)(2,1)S(1)} %bitcast.1352), channel_id=1, source_target_pairs={{0,32},{32,64},{64,96},{96,128},{128,160},{160,192},{192,224},{224... | collective-permute-start | bytes 24584 | tf_op jit(solution)/shard_map/ppermute | solution.py:20
  159.4 7.8 %collective-permute-start.33 = (bf16[128,3,1,32]{0,3,2,1:T(8,128)(2,1)S(1)}, bf16[128,3,1,32]{0,3,2,1:T(8,128)(2,1)S(1)}, u32[]{:S(2)}, u32[]{:S(2)}) collective-permute-start(bf16[128,3,1,32]{0,3,2,1:T(8,128)(2,1)S(1)} %pad_maximum_fusion.19), channel_id=1, source_target_pairs={{4,0},{8,4},{12,8},{16,12},{20,16},{24,20},{28,24},{5,1},{9,5},{13... | collective-permute-start | bytes 73736 | tf_op jit(solution)/shard_map/ppermute | solution.py:22
  161.4 6.6 %collective-permute-start.32 = (bf16[128,3,1,32]{0,3,2,1:T(8,128)(2,1)S(1)}, bf16[128,3,1,32]{0,3,2,1:T(8,128)(2,1)S(1)}, u32[]{:S(2)}, u32[]{:S(2)}) collective-permute-start(bf16[128,3,1,32]{0,3,2,1:T(8,128)(2,1)S(1)} %pad_maximum_fusion.19), channel_id=1, source_target_pairs={{0,4},{4,8},{8,12},{12,16},{16,20},{20,24},{24,28},{1,5},{5,9},{9,... | collective-permute-start | bytes 73736 | tf_op jit(solution)/shard_map/ppermute | solution.py:20
  168.0 8.3 %collective-permute-start.35 = (bf16[128,3,3,1]{0,3,2,1:T(2,128)(2,1)S(1)}, bf16[128,3,3,1]{0,3,2,1:T(2,128)(2,1)S(1)}, u32[]{:S(2)}, u32[]{:S(2)}) collective-permute-start(bf16[128,3,3,1]{0,3,2,1:T(2,128)(2,1)S(1)} %get-tuple-element.146), channel_id=1, source_target_pairs={{1,0},{2,1},{3,2},{5,4},{6,5},{7,6},{9,8},{10,9},{11,10},{13,12},{... | collective-permute-start | bytes 6920 | tf_op jit(solution)/shard_map/ppermute | solution.py:22
  169.3 7.0 %collective-permute-start.34 = (bf16[128,3,3,1]{0,3,2,1:T(2,128)(2,1)S(1)}, bf16[128,3,3,1]{0,3,2,1:T(2,128)(2,1)S(1)}, u32[]{:S(2)}, u32[]{:S(2)}) collective-permute-start(bf16[128,3,3,1]{0,3,2,1:T(2,128)(2,1)S(1)} %get-tuple-element.145), channel_id=1, source_target_pairs={{0,1},{1,2},{2,3},{4,5},{5,6},{6,7},{8,9},{9,10},{10,11},{12,13},{... | collective-permute-start | bytes 6920 | tf_op jit(solution)/shard_map/ppermute | solution.py:20
  176.9 31.6 %collective-permute-start.37 = (bf16[128,1,1,32]{0,3,2,1:T(8,128)(2,1)S(1)}, bf16[128,1,1,32]{0,3,2,1:T(8,128)(2,1)S(1)}, u32[]{:S(2)}, u32[]{:S(2)}) collective-permute-start(bf16[128,1,1,32]{0,3,2,1:T(8,128)(2,1)S(1)} %fusion.340), channel_id=1, source_target_pairs={{32,0},{64,32},{96,64},{128,96},{160,128},{192,160},{224,192},{256... | collective-permute-start | bytes 24584 | tf_op jit(solution)/shard_map/ppermute | solution.py:22
  178.2 30.3 %collective-permute-start.36 = (bf16[128,1,1,32]{0,3,2,1:T(8,128)(2,1)S(1)}, bf16[128,1,1,32]{0,3,2,1:T(8,128)(2,1)S(1)}, u32[]{:S(2)}, u32[]{:S(2)}) collective-permute-start(bf16[128,1,1,32]{0,3,2,1:T(8,128)(2,1)S(1)} %fusion.340), channel_id=1, source_target_pairs={{0,32},{32,64},{64,96},{96,128},{128,160},{160,192},{192,224},{224... | collective-permute-start | bytes 24584 | tf_op jit(solution)/shard_map/ppermute | solution.py:20
  208.6 7.7 %collective-permute-start.39 = (bf16[128,3,1,32]{0,3,2,1:T(8,128)(2,1)S(1)}, bf16[128,3,1,32]{0,3,2,1:T(8,128)(2,1)S(1)}, u32[]{:S(2)}, u32[]{:S(2)}) collective-permute-start(bf16[128,3,1,32]{0,3,2,1:T(8,128)(2,1)S(1)} %pad_maximum_fusion.20), channel_id=1, source_target_pairs={{4,0},{8,4},{12,8},{16,12},{20,16},{24,20},{28,24},{5,1},{9,5},{13... | collective-permute-start | bytes 73736 | tf_op jit(solution)/shard_map/ppermute | solution.py:22
  210.5 6.6 %collective-permute-start.38 = (bf16[128,3,1,32]{0,3,2,1:T(8,128)(2,1)S(1)}, bf16[128,3,1,32]{0,3,2,1:T(8,128)(2,1)S(1)}, u32[]{:S(2)}, u32[]{:S(2)}) collective-permute-start(bf16[128,3,1,32]{0,3,2,1:T(8,128)(2,1)S(1)} %pad_maximum_fusion.20), channel_id=1, source_target_pairs={{0,4},{4,8},{8,12},{12,16},{16,20},{20,24},{24,28},{1,5},{5,9},{9,... | collective-permute-start | bytes 73736 | tf_op jit(solution)/shard_map/ppermute | solution.py:20
  217.1 11.7 %collective-permute-start.41 = (bf16[128,3,3,1]{0,3,2,1:T(2,128)(2,1)S(1)}, bf16[128,3,3,1]{0,3,2,1:T(2,128)(2,1)S(1)}, u32[]{:S(2)}, u32[]{:S(2)}) collective-permute-start(bf16[128,3,3,1]{0,3,2,1:T(2,128)(2,1)S(1)} %get-tuple-element.144), channel_id=1, source_target_pairs={{1,0},{2,1},{3,2},{5,4},{6,5},{7,6},{9,8},{10,9},{11,10},{13,12},{... | collective-permute-start | bytes 6920 | tf_op jit(solution)/shard_map/ppermute | solution.py:22
  218.4 10.4 %collective-permute-start.40 = (bf16[128,3,3,1]{0,3,2,1:T(2,128)(2,1)S(1)}, bf16[128,3,3,1]{0,3,2,1:T(2,128)(2,1)S(1)}, u32[]{:S(2)}, u32[]{:S(2)}) collective-permute-start(bf16[128,3,3,1]{0,3,2,1:T(2,128)(2,1)S(1)} %get-tuple-element.143), channel_id=1, source_target_pairs={{0,1},{1,2},{2,3},{4,5},{5,6},{6,7},{8,9},{9,10},{10,11},{12,13},{... | collective-permute-start | bytes 6920 | tf_op jit(solution)/shard_map/ppermute | solution.py:20
  232.6 25.7 %collective-permute-start.19 = (bf16[32,1,4,128]{3,0,2,1:T(8,128)(2,1)}, bf16[32,1,4,128]{3,0,2,1:T(8,128)(2,1)S(1)}, u32[]{:S(2)}, u32[]{:S(2)}) collective-permute-start(bf16[32,1,4,128]{3,0,2,1:T(8,128)(2,1)} %get-tuple-element.104), channel_id=1, source_target_pairs={{32,0},{64,32},{96,64},{128,96},{160,128},{192,160},{224,192},{256... | collective-permute-start | bytes 98312 | tf_op jit(solution)/shard_map/ppermute | solution.py:22
  233.9 24.4 %collective-permute-start.18 = (bf16[32,1,4,128]{3,0,2,1:T(8,128)(2,1)S(1)}, bf16[32,1,4,128]{3,0,2,1:T(8,128)(2,1)S(1)}, u32[]{:S(2)}, u32[]{:S(2)}) collective-permute-start(bf16[32,1,4,128]{3,0,2,1:T(8,128)(2,1)S(1)} %get-tuple-element.103), channel_id=1, source_target_pairs={{0,32},{32,64},{64,96},{96,128},{128,160},{160,192},{192,224},{224... | collective-permute-start | bytes 98312 | tf_op jit(solution)/shard_map/ppermute | solution.py:20
  258.3 8.1 %collective-permute-start.21 = (bf16[32,6,1,128]{3,0,2,1:T(8,128)(2,1)S(1)}, bf16[32,6,1,128]{3,0,2,1:T(8,128)(2,1)S(1)}, u32[]{:S(2)}, u32[]{:S(2)}) collective-permute-start(bf16[32,6,1,128]{3,0,2,1:T(8,128)(2,1)S(1)} %get-tuple-element.94), channel_id=1, source_target_pairs={{4,0},{8,4},{12,8},{16,12},{20,16},{24,20},{28,24},{5,1},{9,5},{13... | collective-permute-start | bytes 147464 | tf_op jit(solution)/shard_map/ppermute | solution.py:22
  260.3 7.0 %collective-permute-start.20 = (bf16[32,6,1,128]{3,0,2,1:T(8,128)(2,1)S(1)}, bf16[32,6,1,128]{3,0,2,1:T(8,128)(2,1)S(1)}, u32[]{:S(2)}, u32[]{:S(2)}) collective-permute-start(bf16[32,6,1,128]{3,0,2,1:T(8,128)(2,1)S(1)} %get-tuple-element.93), channel_id=1, source_target_pairs={{0,4},{4,8},{8,12},{12,16},{16,20},{20,24},{24,28},{1,5},{5,9},{9,... | collective-permute-start | bytes 147464 | tf_op jit(solution)/shard_map/ppermute | solution.py:20
  268.4 7.6 %collective-permute-start.23 = (bf16[32,6,6,1]{3,0,2,1:T(8,128)(2,1)S(1)}, bf16[32,6,6,1]{3,0,2,1:T(8,128)(2,1)S(1)}, u32[]{:S(2)}, u32[]{:S(2)}) collective-permute-start(bf16[32,6,6,1]{3,0,2,1:T(8,128)(2,1)S(1)} %get-tuple-element.73), channel_id=1, source_target_pairs={{1,0},{2,1},{3,2},{5,4},{6,5},{7,6},{9,8},{10,9},{11,10},{13,12},{... | collective-permute-start | bytes 6920 | tf_op jit(solution)/shard_map/ppermute | solution.py:22
  269.7 7.8 %collective-permute-start.22 = (bf16[32,6,6,1]{3,0,2,1:T(8,128)(2,1)S(1)}, bf16[32,6,6,1]{3,0,2,1:T(8,128)(2,1)S(1)}, u32[]{:S(2)}, u32[]{:S(2)}) collective-permute-start(bf16[32,6,6,1]{3,0,2,1:T(8,128)(2,1)S(1)} %get-tuple-element.72), channel_id=1, source_target_pairs={{0,1},{1,2},{2,3},{4,5},{5,6},{6,7},{8,9},{9,10},{10,11},{12,13},{... | collective-permute-start | bytes 6920 | tf_op jit(solution)/shard_map/ppermute | solution.py:20
  287.0 90.9 %reduce-scatter.5.cloned.1.call-start = ((), (), s32[]{:S(2)}) async-start(), calls=%async_computation.4 | async-start | bytes 491520 | tf_op jit(solution)/shard_map/reduce_scatter | solution.py:31
  287.1 6.5 %collective-permute-start.43 = (bf16[32,1,4,128]{3,0,2,1:T(8,128)(2,1)S(1)}, bf16[32,1,4,128]{3,0,2,1:T(8,128)(2,1)S(1)}, u32[]{:S(2)}, u32[]{:S(2)}) collective-permute-start(bf16[32,1,4,128]{3,0,2,1:T(8,128)(2,1)S(1)} %get-tuple-element.100), channel_id=1, source_target_pairs={{32,0},{64,32},{96,64},{128,96},{160,128},{192,160},{224,192},{256... | collective-permute-start | bytes 98312 | tf_op jit(solution)/shard_map/ppermute | solution.py:22
  294.7 10.9 %collective-permute-start.45 = (bf16[32,6,1,128]{3,0,2,1:T(8,128)(2,1)S(1)}, bf16[32,6,1,128]{3,0,2,1:T(8,128)(2,1)S(1)}, u32[]{:S(2)}, u32[]{:S(2)}) collective-permute-start(bf16[32,6,1,128]{3,0,2,1:T(8,128)(2,1)S(1)} %get-tuple-element.90), channel_id=1, source_target_pairs={{4,0},{8,4},{12,8},{16,12},{20,16},{24,20},{28,24},{5,1},{9,5},{13... | collective-permute-start | bytes 147464 | tf_op jit(solution)/shard_map/ppermute | solution.py:22
  296.6 9.4 %collective-permute-start.44 = (bf16[32,6,1,128]{3,0,2,1:T(8,128)(2,1)S(1)}, bf16[32,6,1,128]{3,0,2,1:T(8,128)(2,1)S(1)}, u32[]{:S(2)}, u32[]{:S(2)}) collective-permute-start(bf16[32,6,1,128]{3,0,2,1:T(8,128)(2,1)S(1)} %get-tuple-element.89), channel_id=1, source_target_pairs={{0,4},{4,8},{8,12},{12,16},{16,20},{20,24},{24,28},{1,5},{5,9},{9,... | collective-permute-start | bytes 147464 | tf_op jit(solution)/shard_map/ppermute | solution.py:20
  307.0 49.3 %collective-permute-start.47 = (bf16[32,6,6,1]{3,0,2,1:T(8,128)(2,1)}, bf16[32,6,6,1]{3,0,2,1:T(8,128)(2,1)}, u32[]{:S(2)}, u32[]{:S(2)}) collective-permute-start(bf16[32,6,6,1]{3,0,2,1:T(8,128)(2,1)} %get-tuple-element.71), channel_id=1, source_target_pairs={{1,0},{2,1},{3,2},{5,4},{6,5},{7,6},{9,8},{10,9},{11,10},{13,12},{... | collective-permute-start | bytes 6920 | tf_op jit(solution)/shard_map/ppermute | solution.py:22
  308.2 48.0 %collective-permute-start.46 = (bf16[32,6,6,1]{3,0,2,1:T(8,128)(2,1)}, bf16[32,6,6,1]{3,0,2,1:T(8,128)(2,1)}, u32[]{:S(2)}, u32[]{:S(2)}) collective-permute-start(bf16[32,6,6,1]{3,0,2,1:T(8,128)(2,1)} %get-tuple-element.70), channel_id=1, source_target_pairs={{0,1},{1,2},{2,3},{4,5},{5,6},{6,7},{8,9},{9,10},{10,11},{12,13},{... | collective-permute-start | bytes 6920 | tf_op jit(solution)/shard_map/ppermute | solution.py:20
  379.7 20.9 %all-to-all-start = ((f32[32,1,1,1196]{3,2,1,0:T(1,128)}), f32[32,1,1,1196]{3,2,1,0:T(1,128)S(1)}, u32[]{:S(2)}, u32[]{:S(2)}) async-start(f32[32,1,1,1196]{3,2,1,0:T(1,128)} %copy.1273), calls=%async_computation.2 | async-start | bytes 327680 | tf_op jit(solution)/shard_map/all_to_all | solution.py:42
  (61 other events, 729.5 us)
Sparse Core Ops, SparseCore 0:
  287.1 65.3 reduce-scatter.2
  355.3 22.5 reduce-scatter.4
where the time goes:
time: 420 us; the launch traced here: 412 us
  starting transfers between devices  166 us (40%)
  local copies, waits for them, and re-layouts  74.3 us (18%)
  waiting for transfers between devices  69.4 us (17%)
  matrix products  65.5 us (16%)
  other arithmetic  19.3 us (5%)
  between operations  17 us (4%)
    ppermute x24, starting transfers between devices, extended(): lax.ppermute(tail, axis, [(i, (i + 1) % count) for i in range(ends)])  116 us
    dot_general x108, matrix products, tap_grad_direct(): lax.dot_general(window, flat_grad, (((1,), (1,)), ((), ())), preferred_el...  48.3 us
    reduce_scatter x2, waiting for transfers between devices, scatter_axes(): shard = lax.psum_scatter(shard, axis, scatter_dimension=dim, tiled=True)  44 us
    ppermute x24, starting transfers between devices, extended(): lax.ppermute(head, axis, [((i + 1) % count, i) for i in range(ends)])  40.8 us
    conv_general_dilated x32, local copies, waits for them, and re-layouts, conv_valid(): lax.conv_general_dilated(padded[None], kernel, (1, 1, 1), 'VALID', dimens...  27.9 us
    conv_general_dilated x8, matrix products, conv_valid(): lax.conv_general_dilated(padded[None], kernel, (1, 1, 1), 'VALID', dimens...  16.8 us
    reshape x5, local copies, waits for them, and re-layouts, reduce_joint(): blocks.transpose(1, 3, 0, 2, 4).reshape(count_x, count_yz, -1)  9.7 us
    all_to_all x1, waiting for transfers between devices, summed_on_arrival(): lax.all_to_all(pieces, axis, split_axis=0, concat_axis=0, tiled=True)  9.32 us
  transfers between devices with their start and end apart: 51, of which 14 were waited for; matrix products, arithmetic and copies ran while one was open for 33% of the time, Pallas kernels for 0%

commit v1 on v0

v1 whole, which is shorter than its diff:
```python
import functools
import math

import jax
import jax.numpy as jnp
import numpy as np
from jax import lax
from jax.experimental import pallas as pl
from jax.experimental.pallas import tpu as pltpu
from jax.sharding import Mesh
from jax.sharding import PartitionSpec as P

GX = ("gx_0", "gx_1")
INTERPRET = False
VMEM_BYTES = 44 * 1024 * 1024
BF = jnp.bfloat16
F32 = jnp.float32
PAD = 5
OWN = 32
PITCH = 48
NT = (((1,), (1,)), ((), ()))
TN = (((0,), (0,)), ((), ()))
COARSE_OF = (0, 1, 1, 1, 1, 2)


def mm(lhs, rhs):
    return jnp.dot(lhs, rhs, preferred_element_type=F32)


def mm_nt(lhs, rhs):
    return lax.dot_general(lhs, rhs, NT, preferred_element_type=F32)


def mm_tn(lhs, rhs):
    return lax.dot_general(lhs, rhs, TN, preferred_element_type=F32)


def lane_roll(value, shift):
    return pltpu.roll(value, shift % value.shape[1], 1)


def row_roll(value, shift):
    return pltpu.roll(value, shift % value.shape[0], 0)


def call(body, out_shape, scratch, n_in, smem_first):
    spec = [pl.BlockSpec(memory_space=pltpu.VMEM)] * n_in
    if smem_first:
        spec[0] = pl.BlockSpec(memory_space=pltpu.SMEM)
    return pl.pallas_call(
        body,
        out_shape=out_shape,
        in_specs=spec,
        out_specs=jax.tree.map(lambda _: pl.BlockSpec(memory_space=pltpu.VMEM), out_shape),
        scratch_shapes=scratch,
        compiler_params=pltpu.CompilerParams(vmem_limit_bytes=VMEM_BYTES),
        interpret=INTERPRET,
    )


def rows_of(own, xlo, xhi, ylo, yhi):
    def row(arr, xi, yi):
        if yi < 2:
            return ylo[arr, xi, yi]
        if yi >= 6:
            return yhi[arr, xi, yi - 6]
        if xi < 2:
            return xlo[arr, xi, yi - 2]
        if xi >= 6:
            return xhi[arr, xi - 6, yi - 2]
        return own[arr, xi - 2, yi - 2]

    return row


def z_faces(own, xlo, xhi, ylo, yhi, perm, out):
    row = rows_of(own, xlo, xhi, ylo, yhi)
    lane = lax.broadcasted_iota(jnp.int32, (32, 128), 1)
    for arr in range(2):
        halves = []
        for half in range(2):
            gathered = jnp.zeros((32, 128), F32)
            for at in range(32):
                cell = half * 32 + at
                value = row(arr, cell // 8, cell % 8).astype(F32)
                moved = lane_roll(value, 4 * at + 2)
                here = (lane >= 4 * at) & (lane < 4 * at + 4)
                gathered = jnp.where(here, moved, gathered)
            halves.append(gathered.astype(BF))
        tiles = mm(jnp.concatenate(halves, axis=1), perm[...]).astype(BF)
        out[arr, 0] = tiles[:, :128]
        out[arr, 1] = tiles[:, 128:]


def face_perm():
    perm = np.zeros((256, 256), np.float32)
    for cell in range(64):
        perm[4 * cell + 0, cell] = 1
        perm[4 * cell + 3, 64 + cell] = 1
        perm[4 * cell + 1, 128 + cell] = 1
        perm[4 * cell + 2, 192 + cell] = 1
    return jnp.asarray(perm, BF)


def stacked_row(value, edge, cell, lane):
    before = jnp.where(lane == 0, lane_roll(edge, -cell), lane_roll(value, 1))
    after = jnp.where(lane == 127, lane_roll(edge, 63 - cell), lane_roll(value, -1))
    return jnp.concatenate([before, value, after], axis=0).astype(BF)


def edge_sum(weight, tile):
    product = mm(weight, tile)
    total = None
    for ab in range(9):
        part = lane_roll(product[ab * 32 : ab * 32 + 32], -(ab // 3 * 8 + ab % 3))
        total = part if total is None else total + part
    return total


def slope_of(value):
    sigma = jax.nn.sigmoid(value)
    return sigma, sigma * (1.0 + value * (1.0 - sigma))


def fine_first(
    sizes, place, own, xlo, xhi, ylo, yhi, face, face_l, face_r, w_z, w_d, pool,
    act, slope, d_join, act_e, slope_e, d_join_e, msg, acc, vbuf,
):
    count_x, count_y, count_z = sizes
    gx, gy, gz = place[0], place[1], place[2]
    row = rows_of(own, xlo, xhi, ylo, yhi)
    lane = lax.broadcasted_iota(jnp.int32, (32, 128), 1)
    lower = lane < 64
    x_in = [gx > 0, None, None, None, None, gx < count_x - 1]
    y_in = [gy > 0, None, None, None, None, gy < count_y - 1]

    def factor(flag):
        return 1.0 if flag is None else jnp.where(flag, 1.0, 0.0)

    pooled = {}
    for arr, weight in ((0, w_z), (1, w_d)):
        tile_a, tile_b = face[arr, 0].astype(F32), face[arr, 1].astype(F32)
        left_a, left_b = face_l[arr, 0].astype(F32), face_l[arr, 1].astype(F32)
        right_a, right_b = face_r[arr, 0].astype(F32), face_r[arr, 1].astype(F32)
        swapped = lane_roll(tile_b, 64)
        edge_0 = jnp.where(lower, left_a, swapped)
        edge_1 = jnp.where(lower, left_b, right_b)
        edge_2 = jnp.where(lower, swapped, right_a)
        edges = edge_sum(weight[...], jnp.concatenate([edge_0, edge_1, edge_2], axis=0).astype(BF))
        for m in range(6):
            acc[m] = jnp.zeros((32, 768), F32)
        for xi in range(8):
            for yi in range(8):
                value = row(arr, xi, yi).astype(F32)
                vbuf[:, yi * 128 : yi * 128 + 128] = stacked_row(value, edge_1, xi * 8 + yi, lane)
            product = mm(weight[...], vbuf[...])
            for a in range(3):
                m = xi - a
                if 0 <= m < 6:
                    part = None
                    for b in range(3):
                        at = (3 * a + b) * 32
                        piece = product[at : at + 32, b * 128 : b * 128 + 768]
                        part = piece if part is None else part + piece
                    acc[m] = acc[m] + part
        total = jnp.zeros((32, 128), F32)
        if arr == 0:
            x_at = lax.broadcasted_iota(jnp.int32, (32, 128), 1) % 64 // 8
            y_at = lax.broadcasted_iota(jnp.int32, (32, 128), 1) % 8
            inside = jnp.where(lower, factor(gz > 0), factor(gz < count_z - 1))
            inside = inside * jnp.where(x_at == 0, factor(x_in[0]), 1.0)
            inside = inside * jnp.where(x_at == 5, factor(x_in[5]), 1.0)
            inside = inside * jnp.where(y_at == 0, factor(y_in[0]), 1.0)
            inside = inside * jnp.where(y_at == 5, factor(y_in[5]), 1.0)
            sigma, steep = slope_of(edges)
            act_e[...] = (edges * sigma * inside).astype(BF).astype(F32)
            slope_e[...] = steep * inside
            for m in range(6):
                for k in range(6):
                    at = slice(k * 128, k * 128 + 128)
                    mask = factor(x_in[m]) * factor(y_in[k])
                    value = acc[m, :, at]
                    sigma, steep = slope_of(value)
                    first = (value * sigma * mask).astype(BF)
                    act[m, :, at] = first
                    slope[m, :, at] = steep * mask
                    if 1 <= m < 5 and 1 <= k < 5:
                        total = total + first.astype(F32)
            total = total * (1.0 / 64.0)
        else:
            d_join_e[...] = edges
            for m in range(6):
                d_join[m] = acc[m]
                if 1 <= m < 5:
                    for k in range(1, 5):
                        total = total + acc[m, :, k * 128 : k * 128 + 128]
        pooled[arr] = lax.dot_general(
            pool[...], total, NT, preferred_element_type=F32, precision=lax.Precision.HIGHEST
        )
    msg[...] = jnp.concatenate([pooled[0], pooled[1]], axis=1).astype(BF)


def coarse(
    sizes, scale, place, recv, w_in, w_mid, w_lift, w_lift_64,
    g_mid, g_in, g_lift, out_ld,
    raw, p3, c3, d3, e3, s2, c2, ws_mid, ws_in, lds,
):
    count_x, count_y, count_z = sizes
    gx, gy, gz = place[0], place[1], place[2]
    rows = count_y * PITCH
    body_rows = slice(PITCH, PITCH + rows)

    z_at = lax.broadcasted_iota(jnp.int32, (PITCH, 128), 0)
    z_all = z_at + (gz * OWN - PAD)
    z_mask = jnp.where((z_all >= 0) & (z_all < count_z * OWN), 1.0, 0.0)
    z_mask = jnp.concatenate([z_mask] * count_y, axis=0)
    own_mask = jnp.where((z_at >= PAD) & (z_at < PAD + OWN), 1.0, 0.0)
    own_mask = jnp.concatenate([own_mask] * count_y, axis=0)

    for store in (p3, c3, d3, e3):
        for plane in range(store.shape[0]):
            blank = jnp.zeros((PITCH, store.shape[2]), BF)
            store[plane, 0:PITCH] = blank
            store[plane, PITCH + rows : 2 * PITCH + rows] = blank
    lds[...] = jnp.zeros(lds.shape, F32)
    for tap in range(27):
        at = tap % 3 * 128
        ws_mid[tap // 3, :, at : at + 128] = w_mid[26 - tap]
        ws_in[tap // 3, :, at : at + 128] = w_in[26 - tap]

    def inside(plane):
        at = gx + plane - PAD
        return (at >= 0) & (at < count_x), jnp.clip(at, 0, count_x - 1)

    def stacked(value):
        return jnp.concatenate([row_roll(value, 1), value, row_roll(value, -1)], axis=1).astype(BF)

    def unpack(plane, carry):
        ok, at = inside(plane)
        keep = jnp.where(ok, 1.0, 0.0)
        parts = []
        for y in range(count_y):
            block = recv[at, y].astype(F32) * keep
            parts.append(block[:, :64])
            parts.append(block[:, 64:])
        whole = jnp.concatenate(parts, axis=0)
        raw[plane] = whole.astype(BF)
        p3[plane, body_rows, :] = stacked(whole[:, :32])
        return carry

    lax.fori_loop(0, 11, unpack, 0)

    def taps(store, first, weight, product):
        total = None
        for ab in range(9):
            a, b = ab // 3, ab % 3
            part = product(store[first + a, b * PITCH : b * PITCH + rows, :], weight(ab))
            total = part if total is None else total + part
        return total

    def level_2(plane, carry):
        ok, _ = inside(plane)
        mask = z_mask * jnp.where(ok, 1.0, 0.0)
        z_2 = taps(p3, plane - 1, lambda ab: w_in_ref(ab), mm)
        sigma, steep = slope_of(z_2)
        s2[plane - 1] = steep * mask
        c3[plane - 1, body_rows, :] = stacked(z_2 * sigma * mask)
        return carry

    def w_in_ref(ab):
        return jnp.concatenate([w_in[3 * ab], w_in[3 * ab + 1], w_in[3 * ab + 2]], axis=0)

    def w_mid_ref(ab):
        return jnp.concatenate([w_mid[3 * ab], w_mid[3 * ab + 1], w_mid[3 * ab + 2]], axis=0)

    lax.fori_loop(1, 10, level_2, 0)

    def level_3(plane, carry):
        ok, _ = inside(plane)
        mask = z_mask * jnp.where(ok, 1.0, 0.0)
        z_3 = taps(c3, plane - 2, lambda ab: w_mid_ref(ab), mm)
        sigma, steep = slope_of(z_3)
        c2[plane - 2] = (z_3 * sigma * mask).astype(BF)
        d_third = mm_nt(raw[plane], w_lift_64[...])
        d3[plane - 2, body_rows, :] = stacked(d_third * steep)
        return carry

    lax.fori_loop(2, 9, level_3, 0)

    def level_2_back(plane, carry):
        total = taps(d3, plane - 3, lambda ab: ws_mid[ab], mm_nt)
        e3[plane - 3, body_rows, :] = stacked(total * s2[plane - 1])
        return carry

    lax.fori_loop(3, 8, level_2_back, 0)

    def level_1_back(plane, carry):
        d_pool = taps(e3, plane - 4, lambda ab: ws_in[ab], mm_nt)
        lifted = mm(c2[plane - 2], w_lift[...])
        both = jnp.concatenate([lifted, d_pool], axis=1)
        for y in range(count_y):
            lds[plane - 4, 1 + y] = both[y * PITCH : y * PITCH + PITCH]
        return carry

    lax.fori_loop(4, 7, level_1_back, 0)
    for i in range(3):
        for j in range(3):
            out_ld[i, j] = lds[i, gy + j]

    span = 128 // count_y
    pick = lax.broadcasted_iota(jnp.int32, (span, 128), 1)
    pick = pick == lax.broadcasted_iota(jnp.int32, (span, 128), 0) + gy * span
    pick = jnp.where(pick, 1.0, 0.0).astype(BF)
    dz3 = (d3[3, body_rows, 128:256].astype(F32) * own_mask).astype(BF)
    dz3 = mm_nt(pick, dz3).astype(BF)
    dz2 = (e3[2, body_rows, 128:256].astype(F32) * own_mask).astype(BF)
    dz2 = mm_nt(pick, dz2).astype(BF)
    for ab in range(9):
        a, b = ab // 3, ab % 3
        at = slice(b * PITCH, b * PITCH + rows)
        g_mid[ab] = mm(dz3, c3[3 + a, at, :]) * scale
        g_in[ab] = mm(dz2, p3[4 + a, at, :]) * scale
    lift_rows = g_lift.shape[0]
    pick = lax.broadcasted_iota(jnp.int32, (lift_rows, 64), 1)
    pick = pick == lax.broadcasted_iota(jnp.int32, (lift_rows, 64), 0) + (32 + gy * (32 // count_y))
    pick = jnp.where(pick, 1.0, 0.0).astype(BF)
    d_lift = mm_nt(pick, raw[5]).astype(BF)
    third = (c2[3].astype(F32) * own_mask).astype(BF)
    g_lift[...] = mm(d_lift, third) * scale


def up_matrix():
    up = np.zeros((PITCH, 128), np.float32)
    for lane in range(128):
        up[PAD + lane // 4, lane] = 1
    return jnp.asarray(np.concatenate([up, up], axis=0), BF)


def edge_matrix():
    edge = np.zeros((24, 128), np.float32)
    for side in range(2):
        for x in range(6):
            for y in range(6):
                source = side * 9 + COARSE_OF[x] * 3 + COARSE_OF[y]
                edge[source, side * 64 + x * 8 + y] = 1
    return jnp.asarray(np.concatenate([edge, edge], axis=0), BF)


def split_two(value):
    high = value.astype(BF)
    low = (value - high.astype(F32)).astype(BF)
    return jnp.concatenate([high, low], axis=0)


def fine_second(
    scale, own, act, slope, d_join, act_e, slope_e, d_join_e, ld, up, edge_up, w_o, w_g,
    out, g_in, g_out_w, g_in_w, v_join, v_dz, acc, edge_rows,
):
    lane = lax.broadcasted_iota(jnp.int32, (32, 128), 1)
    spread = {}
    for x in range(3):
        for y in range(3):
            spread[x, y] = mm_tn(split_two(ld[x, y]), up[...])
    edge_rows[...] = jnp.zeros(edge_rows.shape, F32)
    for side in range(2):
        for x in range(3):
            for y in range(3):
                at = side * 9 + x * 3 + y
                z = PAD - 1 if side == 0 else PAD + OWN
                edge_rows[at : at + 1, :] = ld[x, y, z : z + 1, :]
    spread_e = mm_tn(split_two(edge_rows[...]), edge_up[...])
    join_e = (act_e[...] + spread_e[:32]).astype(BF).astype(F32)
    dz_e = ((d_join_e[...] + spread_e[32:] * (1.0 / 64.0)) * slope_e[...]).astype(BF).astype(F32)
    for m in range(6):
        for k in range(6):
            at = slice(k * 128, k * 128 + 128)
            over = spread[COARSE_OF[m], COARSE_OF[k]]
            join = (act[m, :, at].astype(F32) + over[:32]).astype(BF).astype(F32)
            v_join[m, :, at] = stacked_row(join, join_e, m * 8 + k, lane)
            dz = (d_join[m, :, at] + over[32:] * (1.0 / 64.0)) * slope[m, :, at]
            v_dz[m, :, at] = stacked_row(dz.astype(BF).astype(F32), dz_e, m * 8 + k, lane)
    for store, weight, result in ((v_join, w_o, out), (v_dz, w_g, g_in)):
        for x in range(4):
            acc[x] = jnp.zeros((32, 512), F32)
        for m in range(6):
            product = mm(weight[...], store[m])
            for a in range(3):
                x = m - a
                if 0 <= x < 4:
                    part = None
                    for b in range(3):
                        at = (3 * a + b) * 32
                        piece = product[at : at + 32, b * 128 : b * 128 + 512]
                        part = piece if part is None else part + piece
                    acc[x] = acc[x] + part
        for x in range(4):
            for y in range(4):
                result[x, y] = acc[x, :, y * 128 : y * 128 + 128].astype(BF)
    flat = [
        [jnp.concatenate([own[arr, x, y] for y in range(4)], axis=1) for x in range(4)]
        for arr in range(2)
    ]
    for ab in range(9):
        a, b = ab // 3, ab % 3
        at = slice(b * 128, b * 128 + 512)
        total_o = None
        total_i = None
        for x in range(4):
            part_o = mm_nt(flat[1][x], v_join[x + a, :, at])
            part_i = mm_nt(v_dz[x + a, :, at], flat[0][x])
            total_o = part_o if total_o is None else total_o + part_o
            total_i = part_i if total_i is None else total_i + part_i
        g_out_w[ab] = total_o * scale
        by_tap = [total_i[c * 32 : c * 32 + 32] for c in range(3)]
        g_in_w[ab] = jnp.concatenate(by_tap, axis=1) * scale


def from_below(value, axis):
    count = lax.axis_size(axis)
    return lax.ppermute(value, axis, [(i, i + 1) for i in range(count - 1)])


def from_above(value, axis):
    count = lax.axis_size(axis)
    return lax.ppermute(value, axis, [(i + 1, i) for i in range(count - 1)])


def forward_taps(weight):
    return weight.reshape(9, 3, 32, 32).transpose(0, 3, 1, 2).reshape(288, 96)


def backward_taps(weight):
    return jnp.flip(weight, 0).reshape(9, 3, 32, 32).transpose(0, 2, 1, 3).reshape(288, 96)


def shape_of(shape, dtype):
    return jax.ShapeDtypeStruct(shape, dtype)


def shards(features, cotangent, w_fine_in, w_coarse_in, w_coarse_mid, w_lift, w_fine_out):
    sizes = (lax.axis_size(GX), lax.axis_size("gy"), lax.axis_size("gz"))
    count_x, count_y, count_z = sizes
    cells = count_x * count_y * count_z * 4 * 4 * 128
    scale = 1.0 / math.sqrt(cells)
    place = jnp.stack([lax.axis_index(GX), lax.axis_index("gy"), lax.axis_index("gz")])
    place = place.astype(jnp.int32)

    own = jnp.stack([features, cotangent]).transpose(0, 2, 3, 1, 4)
    xlo = from_below(own[:, 2:4], GX)
    xhi = from_above(own[:, 0:2], GX)
    y_tail = jnp.concatenate([xlo[:, :, 2:4], own[:, :, 2:4], xhi[:, :, 2:4]], axis=1)
    y_head = jnp.concatenate([xlo[:, :, 0:2], own[:, :, 0:2], xhi[:, :, 0:2]], axis=1)
    ylo = from_below(y_tail, "gy")
    yhi = from_above(y_head, "gy")
    face = call(z_faces, shape_of((2, 2, 32, 128), BF), [], 6, False)(
        own, xlo, xhi, ylo, yhi, face_perm()
    )
    face_l = from_below(face, "gz")
    face_r = from_above(face, "gz")

    pool = np.zeros((32, 128), np.float32)
    for at in range(128):
        pool[at // 4, at] = 1
    act, slope, d_join, act_e, slope_e, d_join_e, msg = call(
        functools.partial(fine_first, sizes),
        (
            shape_of((6, 32, 768), BF),
            shape_of((6, 32, 768), F32),
            shape_of((6, 32, 768), F32),
            shape_of((32, 128), F32),
            shape_of((32, 128), F32),
            shape_of((32, 128), F32),
            shape_of((32, 64), BF),
        ),
        [pltpu.VMEM((6, 32, 768), F32), pltpu.VMEM((96, 1024), BF)],
        12,
        True,
    )(
        place, own, xlo, xhi, ylo, yhi, face, face_l, face_r,
        forward_taps(w_fine_in), backward_taps(w_fine_out), jnp.asarray(pool),
    )

    z_lo = from_below(msg[24:32], "gz")
    z_hi = from_above(msg[0:8], "gz")
    window = jnp.concatenate(
        [z_lo[8 - PAD :], msg, z_hi[:PAD], jnp.zeros((PITCH - OWN - 2 * PAD, 64), BF)], axis=0
    )
    packed = jnp.concatenate([window[:24], window[24:]], axis=1)
    plane_axes = GX + ("gy",)
    recv = lax.all_to_all(
        jnp.broadcast_to(packed[None], (count_x * count_y, 24, 128)),
        plane_axes,
        split_axis=0,
        concat_axis=0,
        tiled=True,
    ).reshape(count_x, count_y, 24, 128)

    rows = count_y * PITCH
    span = 128 // count_y
    lift_span = 32 // count_y
    g_mid, g_in, g_lift, ld = call(
        functools.partial(coarse, sizes, scale),
        (
            shape_of((9, span, 384), F32),
            shape_of((9, span, 96), F32),
            shape_of((max(8, lift_span), 128), F32),
            shape_of((3, 3, PITCH, 64), F32),
        ),
        [
            pltpu.VMEM((11, rows, 64), BF),
            pltpu.VMEM((11, rows + 2 * PITCH, 96), BF),
            pltpu.VMEM((9, rows + 2 * PITCH, 384), BF),
            pltpu.VMEM((7, rows + 2 * PITCH, 384), BF),
            pltpu.VMEM((5, rows + 2 * PITCH, 384), BF),
            pltpu.VMEM((9, rows, 128), F32),
            pltpu.VMEM((7, rows, 128), BF),
            pltpu.VMEM((9, 128, 384), BF),
            pltpu.VMEM((9, 32, 384), BF),
            pltpu.VMEM((3, count_y + 2, PITCH, 64), F32),
        ],
        6,
        True,
    )(
        place, recv, w_coarse_in, w_coarse_mid, w_lift,
        jnp.concatenate([jnp.zeros((128, 32), BF), w_lift], axis=1),
    )

    out, grad_input, g_fo, g_fi = call(
        functools.partial(fine_second, scale),
        (
            shape_of((4, 4, 32, 128), BF),
            shape_of((4, 4, 32, 128), BF),
            shape_of((9, 32, 96), F32),
            shape_of((9, 32, 96), F32),
        ),
        [
            pltpu.VMEM((6, 96, 768), BF),
            pltpu.VMEM((6, 96, 768), BF),
            pltpu.VMEM((4, 32, 512), F32),
            pltpu.VMEM((24, 64), F32),
        ],
        12,
        False,
    )(
        own, act, slope, d_join, act_e, slope_e, d_join_e, ld, up_matrix(), edge_matrix(),
        forward_taps(w_fine_out), backward_taps(w_fine_in),
    )
    out = out.transpose(2, 0, 1, 3)
    grad_input = grad_input.transpose(2, 0, 1, 3)

    fine = jnp.stack([g_fo, g_fi]).reshape(2, 9, count_y, 32 // count_y, 96)
    fine = fine.transpose(2, 0, 1, 3, 4)
    fine = lax.all_to_all(fine, "gy", split_axis=0, concat_axis=0, tiled=True).sum(axis=0)

    def blocks(value, o_each, i_each):
        value = value.reshape(9, count_z, o_each, 3, count_x, i_each)
        value = value.transpose(4, 1, 0, 3, 5, 2)
        return value.reshape(count_x, count_z, -1)

    i_fine = 32 // count_x
    o_fine = 32 // (count_y * count_z)
    i_mid = 128 // count_x
    o_mid = 128 // (count_y * count_z)
    lift = g_lift[:lift_span].reshape(count_z, o_fine, count_x, i_mid).transpose(2, 0, 3, 1)
    pieces = [
        blocks(g_mid, o_mid, i_mid),
        blocks(g_in, o_mid, i_fine),
        blocks(fine[0], o_fine, i_fine),
        blocks(fine[1], o_fine, i_fine),
        lift.reshape(count_x, count_z, -1),
    ]
    widths = [piece.shape[2] for piece in pieces]
    joint = jnp.concatenate(pieces, axis=2).reshape(count_x * count_z, -1)
    joint = lax.all_to_all(joint, GX + ("gz",), split_axis=0, concat_axis=0, tiled=True)
    joint = joint.sum(axis=0)
    ends = np.cumsum([0] + widths)
    flat = [joint[ends[at] : ends[at + 1]] for at in range(5)]
    grad_coarse_mid = flat[0].reshape(27, i_mid, o_mid)
    grad_coarse_in = flat[1].reshape(27, i_fine, o_mid)
    grad_fine_out = flat[2].reshape(27, i_fine, o_fine)
    grad_fine_in = jnp.flip(flat[3].reshape(27, i_fine, o_fine), 0)
    grad_lift = flat[4].reshape(i_mid, o_fine)
    return (
        out,
        grad_input,
        grad_fine_in,
        grad_coarse_in,
        grad_coarse_mid,
        grad_lift,
        grad_fine_out,
    )


def solution(mesh):
    split = Mesh(
        mesh.devices.reshape(mesh.shape["gx"] // 2, 2, mesh.shape["gy"], mesh.shape["gz"]),
        ("gx_0", "gx_1", "gy", "gz"),
    )
    return jax.shard_map(
        shards,
        mesh=split,
        in_specs=(P(None, GX, "gy", "gz"), P(None, GX, "gy", "gz"), P(), P(), P(), P(), P()),
        out_specs=(
            P(None, GX, "gy", "gz"),
            P(None, GX, "gy", "gz"),
            P(None, GX, ("gy", "gz")),
            P(None, GX, ("gy", "gz")),
            P(None, GX, ("gy", "gz")),
            P(GX, ("gy", "gz")),
            P(None, GX, ("gy", "gz")),
        ),
        check_vma=False,
    )
```

time: 420 us -> 187 us (0.45); the launches traced: 412 us -> 185 us
  starting transfers between devices: 166 us -> 58.5 us
  matrix products: 65.5 us -> 0 us
  waiting for transfers between devices: 69.4 us -> 37.5 us
  Pallas kernels: 0 us -> 29.4 us
  other arithmetic: 19.3 us -> 1.42 us
  local copies, waits for them, and re-layouts: 74.3 us -> 56.8 us
  between operations: 17 us -> 1.09 us
    ppermute x48 -> x8, starting transfers between devices: 157 us -> 27.3 us  [the longest x4 18.7 us: from_below(): return lax.ppermute(value, axis, [(i, i + 1) for i in range(count - 1)])]
    dot_general x111 -> x0, matrix products: 48.7 us -> none  [the longest x108 48.3 us: tap_grad_direct(): lax.dot_general(window, flat_grad, (((1,), (1,)), ((), ())), preferred_el...]
    reduce_scatter x2 -> x0, waiting for transfers between devices: 44 us -> none  [scatter_axes(): shard = lax.psum_scatter(shard, axis, scatter_dimension=dim, tiled=True)]
    pallas_call x0 -> x4, Pallas kernels: none -> 29.4 us  [the longest x1 21.6 us: shards(): call(functools.partial(coarse, sizes, scale), (shape_of((9, span, 384), F...]
    conv_general_dilated x32 -> x0, local copies, waits for them, and re-layouts: 27.9 us -> none  [conv_valid(): lax.conv_general_dilated(padded[None], kernel, (1, 1, 1), 'VALID', dimens...]
    all_to_all x1 -> x3, starting transfers between devices: 9.08 us -> 31.2 us  [the longest x1 19.2 us: shards(): lax.all_to_all(jnp.broadcast_to(packed[None], (count_x * count_y, 24, 128...]
    all_to_all x1 -> x3, waiting for transfers between devices: 9.32 us -> 28.5 us  [the longest x1 16.7 us: shards(): lax.all_to_all(jnp.broadcast_to(packed[None], (count_x * count_y, 24, 128...]
    conv_general_dilated x8 -> x0, matrix products: 16.8 us -> none  [conv_valid(): lax.conv_general_dilated(padded[None], kernel, (1, 1, 1), 'VALID', dimens...]
  transfers between devices with their start and end apart: 51 -> 11, of which waited for: 14 -> 6; matrix products, arithmetic and copies ran while one was open for 33% -> 21% of each run, Pallas kernels for 0% -> 0%
where the time goes in v1:
time: 187 us; the launch traced here: 185 us
  starting transfers between devices  58.5 us (31%)
  local copies, waits for them, and re-layouts  56.8 us (30%)
  waiting for transfers between devices  37.5 us (20%)
  Pallas kernels  29.4 us (16%)
    pallas_call x1, Pallas kernels, shards(): call(functools.partial(coarse, sizes, scale), (shape_of((9, span, 384), F...  21.6 us
    all_to_all x1, starting transfers between devices, shards(): lax.all_to_all(jnp.broadcast_to(packed[None], (count_x * count_y, 24, 128...  19.2 us
    ppermute x4, starting transfers between devices, from_below(): return lax.ppermute(value, axis, [(i, i + 1) for i in range(count - 1)])  18.7 us
    all_to_all x1, waiting for transfers between devices, shards(): lax.all_to_all(jnp.broadcast_to(packed[None], (count_x * count_y, 24, 128...  16.7 us
    unnamed x49, local copies, waits for them, and re-layouts  14.1 us
    transpose x3, local copies, waits for them, and re-layouts, blocks(): value = value.transpose(4, 1, 0, 3, 5, 2)  14.1 us
    all_to_all x1, waiting for transfers between devices, shards(): lax.all_to_all(joint, GX + ('gz',), split_axis=0, concat_axis=0, tiled=True)  11.8 us
    concatenate x8, local copies, waits for them, and re-layouts, shards(): joint = jnp.concatenate(pieces, axis=2).reshape(count_x * count_z, -1)  9.21 us
  transfers between devices with their start and end apart: 11, of which 6 were waited for; matrix products, arithmetic and copies ran while one was open for 21% of the time, Pallas kernels for 0%

profile of v1, /device:TPU:1, one launch (start us, length us, event | category | flops | bytes accessed | tf_op | source)
XLA Modules:
  0.0 184.7 jit_solution(9987396776369310407)
XLA Ops:
  0.7 1.1 copy_bitcast_fusion.3
  1.8 1.3 collective-permute-start.1
  3.1 4.7 %collective-permute-start = (bf16[2,2,4,32,128]{4,3,2,1,0:T(8,128)(2,1)S(1)}, bf16[2,2,4,32,128]{4,3,2,1,0:T(8,128)(2,1)S(1)}, u32[]{:S(2)}, u32[]{:S(2)}) collective-permute-start(bf16[2,2,4,32,128]{4,3,2,1,0:T(8,128)(2,1)S(1)} %get-tuple-element.61), channel_id=1, source_target_pairs={{0,32},{32,64},{64,96},{96,128},{128,160},{160,192},{192,224},{224... | collective-permute-start | bytes 393224 | tf_op jit(solution)/shard_map/ppermute | solution.py:420
  8.2 1.5 collective-permute-done.xlo
  9.8 6.1 %collective-permute-start.2 = (bf16[2,8,2,32,128]{4,3,2,1,0:T(8,128)(2,1)S(1)}, bf16[2,8,2,32,128]{4,3,2,1,0:T(8,128)(2,1)S(1)}, u32[]{:S(2)}, u32[]{:S(2)}) collective-permute-start(bf16[2,8,2,32,128]{4,3,2,1,0:T(8,128)(2,1)S(1)} %pad_maximum_fusion.1), channel_id=1, source_target_pairs={{0,4},{4,8},{8,12},{12,16},{16,20},{20,24},{24,28},{1,5},{5,9},{9,... | collective-permute-start | bytes 786440 | tf_op jit(solution)/shard_map/ppermute | solution.py:420
  15.9 4.7 %collective-permute-start.3 = (bf16[2,8,2,32,128]{4,3,2,1,0:T(8,128)(2,1)S(1)}, bf16[2,8,2,32,128]{4,3,2,1,0:T(8,128)(2,1)S(1)}, u32[]{:S(2)}, u32[]{:S(2)}) collective-permute-start(bf16[2,8,2,32,128]{4,3,2,1,0:T(8,128)(2,1)S(1)} %pad_maximum_fusion.2), channel_id=1, source_target_pairs={{4,0},{8,4},{12,8},{16,12},{20,16},{24,20},{28,24},{5,1},{9,5},{13... | collective-permute-start | bytes 786440 | tf_op jit(solution)/shard_map/ppermute | solution.py:425
  20.7 6.4 %collective-permute-done.3.yhi = bf16[2,8,2,32,128]{4,3,2,1,0:T(8,128)(2,1)S(1)} collective-permute-done((bf16[2,8,2,32,128]{4,3,2,1,0:T(8,128)(2,1)S(1)}, bf16[2,8,2,32,128]{4,3,2,1,0:T(8,128)(2,1)S(1)}, u32[]{:S(2)}, u32[]{:S(2)}) %collective-permute-start.3) | collective-permute-done | bytes 262176 | tf_op jit(solution)/shard_map/ppermute | solution.py:425
  27.5 1.3 collective-permute-start.5
  28.8 4.0 %collective-permute-start.4 = (bf16[2,2,32,128]{3,2,1,0:T(8,128)(2,1)S(1)}, bf16[2,2,32,128]{3,2,1,0:T(8,128)(2,1)S(1)}, u32[]{:S(2)}, u32[]{:S(2)}) collective-permute-start(bf16[2,2,32,128]{3,2,1,0:T(8,128)(2,1)S(1)} %shard_map.162.face), channel_id=1, source_target_pairs={{0,1},{1,2},{2,3},{4,5},{5,6},{6,7},{8,9},{9,10},{10,11},{12,13},{... | collective-permute-start | bytes 98312 | tf_op jit(solution)/shard_map/ppermute | solution.py:420
  33.5 0.8 reshape.106.w_z
  34.9 0.9 copy-done.2
  35.8 0.8 copy-done.9
  36.6 0.7 copy-done.11
  37.3 3.5 %shard_map.163 = (bf16[6,32,768]{2,1,0:T(8,128)(2,1)S(1)}, f32[6,32,768]{2,1,0:T(8,128)S(1)}, f32[6,32,768]{2,1,0:T(8,128)S(1)}, f32[32,128]{1,0:T(8,128)S(1)}, ...) custom-call(s32[3]{0:T(128)S(1)} %pad_add_fusion.place, ...), custom_call_target="tpu_custom_call" | custom-call | tf_op jit(solution)/shard_map/pallas_call | solution.py:464
  40.9 1.3 collective-permute-start.7
  42.3 4.0 %collective-permute-start.6 = (bf16[8,64]{1,0:T(8,128)(2,1)S(1)}, bf16[8,64]{1,0:T(8,128)(2,1)S(1)}, u32[]{:S(2)}, u32[]{:S(2)}) collective-permute-start(bf16[8,64]{1,0:T(8,128)(2,1)S(1)} %get-tuple-element.71), channel_id=1, source_target_pairs={{0,1},{1,2},{2,3},{4,5},{5,6},{6,7},{8,9},{9,10},{10,11},{12,13},{... | collective-permute-start | bytes 3080 | tf_op jit(solution)/shard_map/ppermute | solution.py:420
  47.0 1.0 broadcast_in_dim.5
  48.0 19.2 %all-to-all-start = ((bf16[128,24,128]{2,1,0:T(8,128)(2,1)}), bf16[128,24,128]{2,1,0:T(8,128)(2,1)S(1)}, u32[]{:S(2)}, u32[]{:S(2)}) async-start(bf16[128,24,128]{2,1,0:T(8,128)(2,1)} %broadcast_in_dim.5), calls=%async_computation | async-start | bytes 1572864 | tf_op jit(solution)/shard_map/all_to_all | solution.py:490
  67.2 1.6 rev.12
  68.8 0.8 copy.58.w_lift
  69.7 1.8 copy.93
  71.5 1.1 reshape.113.w_g
  72.7 1.8 copy.59
  74.5 1.8 reshape.111.w_o
  76.3 16.7 %all-to-all-done = bf16[128,24,128]{2,1,0:T(8,128)(2,1)S(1)} async-done(((bf16[128,24,128]{2,1,0:T(8,128)(2,1)}), bf16[128,24,128]{2,1,0:T(8,128)(2,1)S(1)}, u32[]{:S(2)}, u32[]{:S(2)}) %all-to-all-start) | async-done | bytes 786464 | tf_op jit(solution)/shard_map/all_to_all | solution.py:490
  93.0 0.9 copy-done.3
  93.9 21.6 %shard_map.164 = (f32[9,16,384]{2,1,0:T(8,128)S(1)}, f32[9,16,96]{2,1,0:T(8,128)S(1)}, f32[8,128]{1,0:T(8,128)S(1)}, f32[3,3,48,64]{3,2,1,0:T(8,128)S(1)}) custom-call(s32[3]{0:T(128)S(1)} %pad_add_fusion.place, bf16[16,8,24,128]{3,2,1,0:T(8,128)(2,1)S(1)} %bitcast.54, bf16[27,32,128]{2,1,0:T(8,128)(2,1)S(1)} %copy-done.3, ...), custom_call_target="tpu_custom_call" | custom-call | tf_op jit(solution)/shard_map/pallas_call | solution.py:501
  116.3 0.9 copy-done.1
  117.2 0.7 copy-done.10
  117.9 0.7 copy-done.13
  118.7 0.7 copy-done.15
  119.4 0.7 copy-done.17
  120.1 0.7 copy-done.18
  120.8 3.8 %shard_map.165 = (bf16[4,4,32,128]{3,2,1,0:T(8,128)(2,1)S(1)}, bf16[4,4,32,128]{3,2,1,0:T(8,128)(2,1)S(1)}, f32[9,32,96]{2,1,0:T(8,128)S(1)}, f32[9,32,96]{2,1,0:T(8,128)S(1)}) custom-call(bf16[2,4,4,32,128]{4,3,2,1,0:T(8,128)(2,1)S(1)} %maximum_bitcast_fusion.own, bf16[6,32,768]{2,1,0:T(8,128)(2,1)S(1)} %get-tuple-element.22.act, ...), custom_call_target="tpu_custom_call" | custom-call | tf_op jit(solution)/shard_map/pallas_call | solution.py:528
  124.6 0.8 copy_bitcast_fusion
  125.4 3.9 %all-to-all-start.1 = ((f32[8,2,9,4,96]{4,3,2,1,0:T(4,128)}), f32[8,2,9,4,96]{4,3,2,1,0:T(4,128)S(1)}, u32[]{:S(2)}, u32[]{:S(2)}) async-start(f32[8,2,9,4,96]{4,3,2,1,0:T(4,128)} %copy_bitcast_fusion), calls=%async_computation.1 | async-start | bytes 589824 | tf_op jit(solution)/shard_map/all_to_all | solution.py:553
  129.4 1.2 copy.62
  130.6 2.9 %copy.82 = f32[16,4,9,3,2,4]{5,4,3,2,1,0:T(2,128)S(1)} copy(f32[16,4,9,3,2,4]{2,4,0,3,5,1:T(2,128)S(1)} %bitcast.60) | data formatting | bytes 110592 | tf_op jit(solution)/shard_map/concatenate | solution.py:573
  133.5 1.0 reshape.122
  134.6 3.8 %reshape.114 = f32[9,4,4,3,16,8]{5,4,3,2,1,0:T(8,128)} reshape(f32[9,16,384]{2,1,0:T(8,128)S(1)} %copy-done.5) | data formatting | bytes 442368 | tf_op jit(solution)/shard_map/reshape | solution.py:556
  138.4 12.7 %copy.61 = f32[16,4,9,3,8,4]{5,4,3,2,1,0:T(8,128)} copy(f32[16,4,9,3,8,4]{4,0,3,5,1,2:T(8,128)} %bitcast.59) | data formatting | bytes 442368 | tf_op jit(solution)/shard_map/transpose | solution.py:557
  151.1 4.5 %concatenate.40 = f32[64,864]{1,0:T(8,128)S(1)} reshape(f32[16,4,9,3,8,4]{5,4,3,2,1,0:T(8,128)} %copy.61) | data formatting | bytes 442368 | tf_op jit(solution)/shard_map/concatenate | solution.py:573
  158.1 1.1 copy.75
  159.2 8.1 %all-to-all-start.2 = ((f32[64,1,1196]{2,1,0:T(1,128)}), f32[64,1,1196]{2,1,0:T(1,128)S(1)}, u32[]{:S(2)}, u32[]{:S(2)}) async-start(f32[64,1,1196]{2,1,0:T(1,128)} %copy.75), calls=%async_computation.2 | async-start | bytes 655360 | tf_op jit(solution)/shard_map/all_to_all | solution.py:574
  167.3 0.7 copy.76
  168.0 0.7 copy.77
  168.7 11.8 %all-to-all-done.2 = f32[64,1,1196]{2,1,0:T(1,128)S(1)} async-done(((f32[64,1,1196]{2,1,0:T(1,128)}), f32[64,1,1196]{2,1,0:T(1,128)S(1)}, u32[]{:S(2)}, u32[]{:S(2)}) %all-to-all-start.2) | async-done | bytes 306208 | tf_op jit(solution)/shard_map/all_to_all | solution.py:574
  184.0 0.7 copy.80
  (86 shorter events, 9.9 us)
Async XLA Ops:
  0.6 26.4 %copy-start.6 = (bf16[256,256]{1,0:T(8,128)(2,1)S(1)}, bf16[256,256]{1,0:T(8,128)(2,1)}, u32[]{:S(2)}) copy-start(bf16[256,256]{1,0:T(8,128)(2,1)} %constant.34.clone.perm) | copy-start | bytes 393220
  0.6 32.3 %copy-start.20 = (bf16[27,32,32]{2,1,0:T(8,128)(2,1)S(1)}, bf16[27,32,32]{2,1,0:T(8,128)(2,1)}, u32[]{:S(2)}) copy-start(bf16[27,32,32]{2,1,0:T(8,128)(2,1)} %param.17) | copy-start | bytes 165892
  0.7 32.6 %copy-start.19 = (bf16[27,32,32]{2,1,0:T(8,128)(2,1)S(1)}, bf16[27,32,32]{2,1,0:T(8,128)(2,1)}, u32[]{:S(2)}) copy-start(bf16[27,32,32]{2,1,0:T(8,128)(2,1)} %param.13) | copy-start | bytes 165892
  1.8 6.4 %collective-permute-start.1 = (bf16[2,2,4,32,128]{4,3,2,1,0:T(8,128)(2,1)S(1)}, bf16[2,2,4,32,128]{4,3,2,1,0:T(8,128)(2,1)S(1)}, u32[]{:S(2)}, u32[]{:S(2)}) collective-permute-start(bf16[2,2,4,32,128]{4,3,2,1,0:T(8,128)(2,1)S(1)} %get-tuple-element.60), channel_id=1, source_target_pairs={{32,0},{64,32},{96,64},{128,96},{160,128},{192,160},{224,192},{256... | collective-permute-start | bytes 393224 | tf_op jit(solution)/shard_map/ppermute | solution.py:425
  3.1 6.6 %collective-permute-start = (bf16[2,2,4,32,128]{4,3,2,1,0:T(8,128)(2,1)S(1)}, bf16[2,2,4,32,128]{4,3,2,1,0:T(8,128)(2,1)S(1)}, u32[]{:S(2)}, u32[]{:S(2)}) collective-permute-start(bf16[2,2,4,32,128]{4,3,2,1,0:T(8,128)(2,1)S(1)} %get-tuple-element.61), channel_id=1, source_target_pairs={{0,32},{32,64},{64,96},{96,128},{128,160},{160,192},{192,224},{224... | collective-permute-start | bytes 393224 | tf_op jit(solution)/shard_map/ppermute | solution.py:420
  9.8 10.9 %collective-permute-start.2 = (bf16[2,8,2,32,128]{4,3,2,1,0:T(8,128)(2,1)S(1)}, bf16[2,8,2,32,128]{4,3,2,1,0:T(8,128)(2,1)S(1)}, u32[]{:S(2)}, u32[]{:S(2)}) collective-permute-start(bf16[2,8,2,32,128]{4,3,2,1,0:T(8,128)(2,1)S(1)} %pad_maximum_fusion.1), channel_id=1, source_target_pairs={{0,4},{4,8},{8,12},{12,16},{16,20},{20,24},{24,28},{1,5},{5,9},{9,... | collective-permute-start | bytes 786440 | tf_op jit(solution)/shard_map/ppermute | solution.py:420
  15.9 11.2 %collective-permute-start.3 = (bf16[2,8,2,32,128]{4,3,2,1,0:T(8,128)(2,1)S(1)}, bf16[2,8,2,32,128]{4,3,2,1,0:T(8,128)(2,1)S(1)}, u32[]{:S(2)}, u32[]{:S(2)}) collective-permute-start(bf16[2,8,2,32,128]{4,3,2,1,0:T(8,128)(2,1)S(1)} %pad_maximum_fusion.2), channel_id=1, source_target_pairs={{4,0},{8,4},{12,8},{16,12},{20,16},{24,20},{28,24},{5,1},{9,5},{13... | collective-permute-start | bytes 786440 | tf_op jit(solution)/shard_map/ppermute | solution.py:425
  27.5 6.8 %collective-permute-start.5 = (bf16[2,2,32,128]{3,2,1,0:T(8,128)(2,1)S(1)}, bf16[2,2,32,128]{3,2,1,0:T(8,128)(2,1)S(1)}, u32[]{:S(2)}, u32[]{:S(2)}) collective-permute-start(bf16[2,2,32,128]{3,2,1,0:T(8,128)(2,1)S(1)} %shard_map.162.face), channel_id=1, source_target_pairs={{1,0},{2,1},{3,2},{5,4},{6,5},{7,6},{9,8},{10,9},{11,10},{13,12},{... | collective-permute-start | bytes 98312 | tf_op jit(solution)/shard_map/ppermute | solution.py:425
  28.8 5.5 %collective-permute-start.4 = (bf16[2,2,32,128]{3,2,1,0:T(8,128)(2,1)S(1)}, bf16[2,2,32,128]{3,2,1,0:T(8,128)(2,1)S(1)}, u32[]{:S(2)}, u32[]{:S(2)}) collective-permute-start(bf16[2,2,32,128]{3,2,1,0:T(8,128)(2,1)S(1)} %shard_map.162.face), channel_id=1, source_target_pairs={{0,1},{1,2},{2,3},{4,5},{5,6},{6,7},{8,9},{9,10},{10,11},{12,13},{... | collective-permute-start | bytes 98312 | tf_op jit(solution)/shard_map/ppermute | solution.py:420
  33.3 59.7 %copy-start = (bf16[27,128,128]{2,1,0:T(8,128)(2,1)S(1)}, bf16[27,128,128]{2,1,0:T(8,128)(2,1)}, u32[]{:S(2)}) copy-start(bf16[27,128,128]{2,1,0:T(8,128)(2,1)} %w_mid.1) | copy-start | bytes 2654212
  34.3 0.6 copy-start.8
  34.9 0.9 copy-start.2
  35.8 0.8 copy-start.9
  36.6 0.7 copy-start.11
  40.8 6.2 %copy-start.12 = (f32[32,128]{1,0:T(8,128)}, f32[32,128]{1,0:T(8,128)S(1)}, u32[]{:S(2)}) copy-start(f32[32,128]{1,0:T(8,128)S(1)} %get-tuple-element.25.act_e) | copy-start | bytes 49156
  40.8 6.2 %copy-start.14 = (f32[32,128]{1,0:T(8,128)}, f32[32,128]{1,0:T(8,128)S(1)}, u32[]{:S(2)}) copy-start(f32[32,128]{1,0:T(8,128)S(1)} %get-tuple-element.26.slope_e) | copy-start | bytes 49156
  40.8 6.2 %copy-start.16 = (f32[32,128]{1,0:T(8,128)}, f32[32,128]{1,0:T(8,128)S(1)}, u32[]{:S(2)}) copy-start(f32[32,128]{1,0:T(8,128)S(1)} %get-tuple-element.27.d_join_e) | copy-start | bytes 49156
  40.9 5.4 %collective-permute-start.7 = (bf16[8,64]{1,0:T(8,128)(2,1)S(1)}, bf16[8,64]{1,0:T(8,128)(2,1)S(1)}, u32[]{:S(2)}, u32[]{:S(2)}) collective-permute-start(bf16[8,64]{1,0:T(8,128)(2,1)S(1)} %get-tuple-element.70), channel_id=1, source_target_pairs={{1,0},{2,1},{3,2},{5,4},{6,5},{7,6},{9,8},{10,9},{11,10},{13,12},{... | collective-permute-start | bytes 3080 | tf_op jit(solution)/shard_map/ppermute | solution.py:425
  42.3 4.7 %collective-permute-start.6 = (bf16[8,64]{1,0:T(8,128)(2,1)S(1)}, bf16[8,64]{1,0:T(8,128)(2,1)S(1)}, u32[]{:S(2)}, u32[]{:S(2)}) collective-permute-start(bf16[8,64]{1,0:T(8,128)(2,1)S(1)} %get-tuple-element.71), channel_id=1, source_target_pairs={{0,1},{1,2},{2,3},{4,5},{5,6},{6,7},{8,9},{9,10},{10,11},{12,13},{... | collective-permute-start | bytes 3080 | tf_op jit(solution)/shard_map/ppermute | solution.py:420
  48.0 45.0 %all-to-all-start = ((bf16[128,24,128]{2,1,0:T(8,128)(2,1)}), bf16[128,24,128]{2,1,0:T(8,128)(2,1)S(1)}, u32[]{:S(2)}, u32[]{:S(2)}) async-start(bf16[128,24,128]{2,1,0:T(8,128)(2,1)} %broadcast_in_dim.5), calls=%async_computation | async-start | bytes 1572864 | tf_op jit(solution)/shard_map/all_to_all | solution.py:490
  93.0 0.9 copy-start.3
  115.6 0.7 copy-start.4
  116.3 8.3 %copy-start.7 = (f32[9,16,96]{2,1,0:T(8,128)}, f32[9,16,96]{2,1,0:T(8,128)S(1)}, u32[]{:S(2)}) copy-start(f32[9,16,96]{2,1,0:T(8,128)S(1)} %get-tuple-element.33) | copy-start | bytes 165892
  116.3 0.9 copy-start.1
  117.2 0.7 copy-start.10
  117.9 0.7 copy-start.13
  118.7 0.7 copy-start.15
  119.4 0.7 copy-start.17
  120.1 0.7 copy-start.18
  124.6 10.0 %copy-start.5 = (f32[9,16,384]{2,1,0:T(8,128)S(1)}, f32[9,16,384]{2,1,0:T(8,128)}, u32[]{:S(2)}) copy-start(f32[9,16,384]{2,1,0:T(8,128)} %copy-done.4) | copy-start | bytes 663556
  125.4 30.2 %all-to-all-start.1 = ((f32[8,2,9,4,96]{4,3,2,1,0:T(4,128)}), f32[8,2,9,4,96]{4,3,2,1,0:T(4,128)S(1)}, u32[]{:S(2)}, u32[]{:S(2)}) async-start(f32[8,2,9,4,96]{4,3,2,1,0:T(4,128)} %copy_bitcast_fusion), calls=%async_computation.1 | async-start | bytes 589824 | tf_op jit(solution)/shard_map/all_to_all | solution.py:553
  159.2 21.4 %all-to-all-start.2 = ((f32[64,1,1196]{2,1,0:T(1,128)}), f32[64,1,1196]{2,1,0:T(1,128)S(1)}, u32[]{:S(2)}, u32[]{:S(2)}) async-start(f32[64,1,1196]{2,1,0:T(1,128)} %copy.75), calls=%async_computation.2 | async-start | bytes 655360 | tf_op jit(solution)/shard_map/all_to_all | solution.py:574

commit v2 on v1

v2 whole, which is shorter than its diff:
```python
import functools
import math

import jax
import jax.numpy as jnp
import numpy as np
from jax import lax
from jax.experimental import pallas as pl
from jax.experimental.pallas import tpu as pltpu
from jax.sharding import Mesh
from jax.sharding import PartitionSpec as P

GX = ("gx_0", "gx_1")
INTERPRET = False
BF = jnp.bfloat16
F32 = jnp.float32
PAD = 5
OWN = 32
PITCH = 48
NT = (((1,), (1,)), ((), ()))
TN = (((0,), (0,)), ((), ()))
COARSE_OF = (0, 1, 1, 1, 1, 2)


def mm(lhs, rhs):
    return jnp.dot(lhs, rhs, preferred_element_type=F32)


def mm_nt(lhs, rhs):
    return lax.dot_general(lhs, rhs, NT, preferred_element_type=F32)


def mm_tn(lhs, rhs):
    return lax.dot_general(lhs, rhs, TN, preferred_element_type=F32)


def lane_roll(value, shift):
    return pltpu.roll(value, shift % value.shape[1], 1)


def row_roll(value, shift):
    return pltpu.roll(value, shift % value.shape[0], 0)


def call(body, out_shape, scratch, n_in, smem_first, megabytes, keep_out=True):
    spec = [pl.BlockSpec(memory_space=pltpu.VMEM)] * n_in
    if smem_first:
        spec[0] = pl.BlockSpec(memory_space=pltpu.SMEM)
    out_spec = pl.BlockSpec(memory_space=pltpu.VMEM) if keep_out else pl.BlockSpec()
    return pl.pallas_call(
        body,
        out_shape=out_shape,
        in_specs=spec,
        out_specs=jax.tree.map(lambda _: out_spec, out_shape),
        scratch_shapes=scratch,
        compiler_params=pltpu.CompilerParams(vmem_limit_bytes=megabytes * 1024 * 1024),
        interpret=INTERPRET,
    )


def rows_of(own, xlo, xhi, ylo, yhi):
    def row(arr, xi, yi):
        if yi < 2:
            return ylo[arr, xi, yi]
        if yi >= 6:
            return yhi[arr, xi, yi - 6]
        if xi < 2:
            return xlo[arr, xi, yi - 2]
        if xi >= 6:
            return xhi[arr, xi - 6, yi - 2]
        return own[arr, xi - 2, yi - 2]

    return row


def iota(shape, dim):
    return lax.broadcasted_iota(jnp.int32, shape, dim)


def ones_where(flag):
    return jnp.where(flag, 1.0, 0.0)


def z_faces(own, xlo, xhi, ylo, yhi, out):
    row = rows_of(own, xlo, xhi, ylo, yhi)
    lane = iota((32, 128), 1)
    column = iota((256, 256), 1)
    source = jnp.where(column < 128, 0, 1)
    source = jnp.where(column % 128 < 64, source, 3 - source)
    perm = ones_where(iota((256, 256), 0) == column % 64 * 4 + source).astype(BF)
    for arr in range(2):
        halves = []
        for half in range(2):
            gathered = jnp.zeros((32, 128), F32)
            for at in range(32):
                cell = half * 32 + at
                value = row(arr, cell // 8, cell % 8).astype(F32)
                moved = lane_roll(value, 4 * at + 2)
                here = (lane >= 4 * at) & (lane < 4 * at + 4)
                gathered = jnp.where(here, moved, gathered)
            halves.append(gathered.astype(BF))
        tiles = mm(jnp.concatenate(halves, axis=1), perm).astype(BF)
        out[arr, 0] = tiles[:, :128]
        out[arr, 1] = tiles[:, 128:]


def stacked_row(value, edge, cell, lane):
    before = jnp.where(lane == 0, lane_roll(edge, -cell), lane_roll(value, 1))
    after = jnp.where(lane == 127, lane_roll(edge, 63 - cell), lane_roll(value, -1))
    return jnp.concatenate([before, value, after], axis=0).astype(BF)


def edge_sum(weight, tile):
    product = mm(weight, tile)
    total = None
    for ab in range(9):
        part = lane_roll(product[ab * 32 : ab * 32 + 32], -(ab // 3 * 8 + ab % 3))
        total = part if total is None else total + part
    return total


def slope_of(value):
    sigma = jax.nn.sigmoid(value)
    return sigma, sigma * (1.0 + value * (1.0 - sigma))


def forward_taps(weight, store):
    same = ones_where(iota((32, 32), 0) == iota((32, 32), 1)).astype(BF)
    for ab in range(9):
        stack = jnp.concatenate([weight[3 * ab + c] for c in range(3)], axis=0)
        store[ab * 32 : ab * 32 + 32, :] = mm_nt(same, stack).astype(BF)


def backward_taps(weight, store):
    for ab in range(9):
        stack = [weight[26 - 3 * ab - c].astype(F32) for c in range(3)]
        store[ab * 32 : ab * 32 + 32, :] = jnp.concatenate(stack, axis=1).astype(BF)


def fine_first(
    sizes, place, own, xlo, xhi, ylo, yhi, face, face_l, face_r, w_fine_in, w_fine_out,
    act, slope, d_join, edge, msg, acc, vbuf, w_z, w_d,
):
    count_x, count_y, count_z = sizes
    gx, gy, gz = place[0], place[1], place[2]
    row = rows_of(own, xlo, xhi, ylo, yhi)
    lane = iota((32, 128), 1)
    lower = lane < 64
    x_in = [gx > 0, None, None, None, None, gx < count_x - 1]
    y_in = [gy > 0, None, None, None, None, gy < count_y - 1]
    forward_taps(w_fine_in, w_z)
    backward_taps(w_fine_out, w_d)

    def factor(flag):
        return 1.0 if flag is None else jnp.where(flag, 1.0, 0.0)

    pooled = {}
    pool = ones_where(iota((32, 128), 1) // 4 == iota((32, 128), 0))
    for arr, weight in ((0, w_z), (1, w_d)):
        tile_a, tile_b = face[arr, 0].astype(F32), face[arr, 1].astype(F32)
        left_a, left_b = face_l[arr, 0].astype(F32), face_l[arr, 1].astype(F32)
        right_a, right_b = face_r[arr, 0].astype(F32), face_r[arr, 1].astype(F32)
        swapped = lane_roll(tile_b, 64)
        edge_0 = jnp.where(lower, left_a, swapped)
        edge_1 = jnp.where(lower, left_b, right_b)
        edge_2 = jnp.where(lower, swapped, right_a)
        edges = edge_sum(weight[...], jnp.concatenate([edge_0, edge_1, edge_2], axis=0).astype(BF))
        for m in range(6):
            acc[m] = jnp.zeros((32, 768), F32)
        for xi in range(8):
            for yi in range(8):
                value = row(arr, xi, yi).astype(F32)
                vbuf[:, yi * 128 : yi * 128 + 128] = stacked_row(value, edge_1, xi * 8 + yi, lane)
            product = mm(weight[...], vbuf[...])
            for a in range(3):
                m = xi - a
                if 0 <= m < 6:
                    part = None
                    for b in range(3):
                        at = (3 * a + b) * 32
                        piece = product[at : at + 32, b * 128 : b * 128 + 768]
                        part = piece if part is None else part + piece
                    acc[m] = acc[m] + part
        total = jnp.zeros((32, 128), F32)
        if arr == 0:
            x_at = lane % 64 // 8
            y_at = lane % 8
            inside = jnp.where(lower, factor(gz > 0), factor(gz < count_z - 1))
            inside = inside * jnp.where(x_at == 0, factor(x_in[0]), 1.0)
            inside = inside * jnp.where(x_at == 5, factor(x_in[5]), 1.0)
            inside = inside * jnp.where(y_at == 0, factor(y_in[0]), 1.0)
            inside = inside * jnp.where(y_at == 5, factor(y_in[5]), 1.0)
            sigma, steep = slope_of(edges)
            edge[0] = (edges * sigma * inside).astype(BF).astype(F32)
            edge[1] = steep * inside
            for m in range(6):
                for k in range(6):
                    at = slice(k * 128, k * 128 + 128)
                    mask = factor(x_in[m]) * factor(y_in[k])
                    value = acc[m, :, at]
                    sigma, steep = slope_of(value)
                    first = (value * sigma * mask).astype(BF)
                    act[m, :, at] = first
                    slope[m, :, at] = steep * mask
                    if 1 <= m < 5 and 1 <= k < 5:
                        total = total + first.astype(F32)
            total = total * (1.0 / 64.0)
        else:
            edge[2] = edges
            for m in range(6):
                d_join[m] = acc[m]
                if 1 <= m < 5:
                    for k in range(1, 5):
                        total = total + acc[m, :, k * 128 : k * 128 + 128]
        pooled[arr] = lax.dot_general(
            pool, total, NT, preferred_element_type=F32, precision=lax.Precision.HIGHEST
        )
    msg[...] = jnp.concatenate([pooled[0], pooled[1]], axis=1).astype(BF)


def split_two(value):
    high = value.astype(BF)
    low = (value - high.astype(F32)).astype(BF)
    return jnp.concatenate([high, low], axis=0)


def lane_tiles(sizes):
    count_x, count_y, count_z = sizes
    span, lift = 128 // count_y, 32 // count_y
    first = -(-(27 * span + lift) // 128)
    second = -(-(27 * span // count_z + lift // count_z) // 128)
    return first, second


def message_rows(sizes):
    i_mid, i_fine = 128 // sizes[0], 32 // sizes[0]
    tiles, _ = lane_tiles(sizes)
    used = tiles * i_mid + tiles * i_fine + 18 * i_fine
    return -(-used // 16) * 16


def final_rows(sizes):
    i_mid, i_fine = 128 // sizes[0], 32 // sizes[0]
    _, tiles = lane_tiles(sizes)
    used = tiles * i_mid + tiles * i_fine + 3 * (32 // (sizes[1] * sizes[2]))
    return -(-used // 8) * 8


def second(
    sizes, scale, place, recv, w_in, w_mid, w_lift, own, act, slope, d_join, edge,
    w_fine_in, w_fine_out,
    out, g_in, msg,
    raw, p3, c3, d3, e3, s2, c2, wp_in, wp_mid, bp_mid, b_in, lds, edge_rows,
    v_join, v_dz, acc, w_o, w_g, mbuf,
):
    count_x, count_y, count_z = sizes
    gx, gy, gz = place[0], place[1], place[2]
    rows = count_y * PITCH
    body_rows = slice(PITCH, PITCH + rows)
    deep_rows = slice(2 * PITCH, 2 * PITCH + rows)

    z_at = iota((PITCH, 128), 0)
    z_all = z_at + (gz * OWN - PAD)
    z_mask = ones_where((z_all >= 0) & (z_all < count_z * OWN))
    z_mask = jnp.concatenate([z_mask] * count_y, axis=0)
    own_mask = ones_where((z_at >= PAD) & (z_at < PAD + OWN))
    own_mask = jnp.concatenate([own_mask] * count_y, axis=0)

    for store, pads in ((p3, 1), (c3, 1), (d3, 1), (e3, 2), (c2, 1)):
        for plane in range(store.shape[0]):
            blank = jnp.zeros((pads * PITCH, store.shape[2]), BF)
            store[plane, 0 : pads * PITCH] = blank
            store[plane, pads * PITCH + rows : 2 * pads * PITCH + rows] = blank
    for a in range(3):
        for b in range(3):
            for c in range(3):
                tap = 9 * a + 3 * b + c
                side = slice(b * 128, b * 128 + 128)
                deep = slice(c * 128, c * 128 + 128)
                wp_in[a, c * 32 : c * 32 + 32, side] = w_in[tap]
                wp_mid[a, deep, side] = w_mid[tap]
                bp_mid[a, side, deep] = w_mid[26 - tap]
                b_in[3 * a + b, :, deep] = w_in[26 - tap]

    def inside(plane):
        at = gx + plane - PAD
        return (at >= 0) & (at < count_x), jnp.clip(at, 0, count_x - 1)

    def stacked(value):
        return jnp.concatenate([row_roll(value, 1), value, row_roll(value, -1)], axis=1).astype(BF)

    def unpack(plane, carry):
        ok, at = inside(plane)
        keep = ones_where(ok)
        parts = []
        for y in range(count_y):
            block = recv[at, y].astype(F32) * keep
            parts.append(block[:, :64])
            parts.append(block[:, 64:])
        whole = jnp.concatenate(parts, axis=0)
        raw[plane] = whole.astype(BF)
        p3[plane, body_rows, :] = stacked(whole[:, :32])
        return carry

    lax.fori_loop(0, 11, unpack, 0)

    def taps(store, first, pair, alone, product):
        total = None
        for a in range(3):
            both = product(store[first + a, 0 : rows + PITCH, :], pair(a))
            last = product(store[first + a, 2 * PITCH : 2 * PITCH + rows, :], alone(a))
            part = both[:rows, :128] + both[PITCH:, 128:] + last
            total = part if total is None else total + part
        return total

    def level_2(plane, carry):
        ok, _ = inside(plane)
        mask = z_mask * ones_where(ok)
        z_2 = taps(p3, plane - 1, lambda a: wp_in[a, :, :256], lambda a: wp_in[a, :, 256:], mm)
        sigma, steep = slope_of(z_2)
        s2[plane - 1] = steep * mask
        c3[plane - 1, body_rows, :] = stacked(z_2 * sigma * mask)
        return carry

    lax.fori_loop(1, 10, level_2, 0)
    lift_64 = jnp.concatenate([jnp.zeros((128, 32), F32), w_lift[...].astype(F32)], axis=1)
    lift_64 = lift_64.astype(BF)

    def level_3(plane, carry):
        ok, _ = inside(plane)
        mask = z_mask * ones_where(ok)
        z_3 = taps(c3, plane - 2, lambda a: wp_mid[a, :, :256], lambda a: wp_mid[a, :, 256:], mm)
        sigma, steep = slope_of(z_3)
        c2[plane - 2, body_rows, :] = (z_3 * sigma * mask).astype(BF)
        d_third = mm_nt(raw[plane], lift_64)
        d3[plane - 2, body_rows, :] = stacked(d_third * steep)
        return carry

    lax.fori_loop(2, 9, level_3, 0)

    def level_2_back(plane, carry):
        total = taps(d3, plane - 3, lambda a: bp_mid[a, :256], lambda a: bp_mid[a, 256:], mm_nt)
        e3[plane - 3, deep_rows, :] = stacked(total * s2[plane - 1])
        return carry

    lax.fori_loop(3, 8, level_2_back, 0)

    near = 3 * PITCH
    for x in range(3):
        d_pool = None
        for ab in range(9):
            start = pl.multiple_of((gy + ab % 3) * PITCH, PITCH)
            part = mm_nt(e3[x + ab // 3, pl.ds(start, near), :], b_in[ab])
            d_pool = part if d_pool is None else d_pool + part
        lifted = mm(c2[2 + x, pl.ds(pl.multiple_of(gy * PITCH, PITCH), near), :], w_lift[...])
        lds[x] = jnp.concatenate([lifted, d_pool], axis=1)

    span, lift_span = 128 // count_y, 32 // count_y
    tiles, _ = lane_tiles(sizes)
    lanes = tiles * 128
    col = iota((384, 3 * span), 1)
    share = iota((384, 3 * span), 0) == col // span * 128 + col % span + gy * span
    share = ones_where(share).astype(BF)

    def shifted(store, first, pads):
        parts = []
        for a in range(3):
            picked = mm(store[first + a], share)
            for b in range(3):
                start = (pads - 1 + b) * PITCH
                parts.append(picked[start : start + rows])
        parts.append(jnp.zeros((rows, lanes - 27 * span), F32))
        return jnp.concatenate(parts, axis=1).astype(BF)

    c1_own = (c3[4, body_rows, 128:256].astype(F32) * own_mask).astype(BF)
    c2_own = (c2[3, body_rows, :].astype(F32) * own_mask).astype(BF)
    raw_own = (raw[5].astype(F32) * own_mask[:, :64]).astype(BF)
    col = iota((64, lanes), 1) - 27 * span
    pick = (iota((64, lanes), 0) == col + 32 + gy * lift_span) & (col >= 0) & (col < lift_span)
    d_lift = mm(raw[5], ones_where(pick).astype(BF)).astype(BF)
    g_mid = (mm_tn(c1_own, shifted(d3, 2, 1)) + mm_tn(c2_own, d_lift)) * scale
    g_coarse = mm_tn(raw_own, shifted(e3, 1, 2)) * scale
    i_mid, i_fine = 128 // count_x, 32 // count_x
    for x in range(count_x):
        for tile in range(tiles):
            at = slice(tile * 128, tile * 128 + 128)
            to = tile * i_mid
            mbuf[x, to : to + i_mid, :] = g_mid[x * i_mid : (x + 1) * i_mid, at]
            to = tiles * i_mid + tile * i_fine
            mbuf[x, to : to + i_fine, :] = g_coarse[x * i_fine : (x + 1) * i_fine, at]

    forward_taps(w_fine_out, w_o)
    backward_taps(w_fine_in, w_g)
    lane = iota((32, 128), 1)
    up = ones_where(iota((PITCH, 128), 0) == iota((PITCH, 128), 1) // 4 + PAD).astype(BF)
    up = jnp.concatenate([up, up], axis=0)
    spread = {}
    for x in range(3):
        for y in range(3):
            spread[x, y] = mm_tn(split_two(lds[x, y * PITCH : y * PITCH + PITCH]), up)
    edge_rows[...] = jnp.zeros(edge_rows.shape, F32)
    for side in range(2):
        for x in range(3):
            for y in range(3):
                at = side * 9 + x * 3 + y
                z = y * PITCH + (PAD - 1 if side == 0 else PAD + OWN)
                edge_rows[at : at + 1, :] = lds[x, z : z + 1, :]
    cell = iota((24, 128), 1)
    x_at, y_at = cell % 64 // 8, cell % 8
    x_of = jnp.where(x_at == 0, 0, jnp.where(x_at == 5, 2, 1))
    y_of = jnp.where(y_at == 0, 0, jnp.where(y_at == 5, 2, 1))
    edge_up = iota((24, 128), 0) == cell // 64 * 9 + x_of * 3 + y_of
    edge_up = ones_where(edge_up & (x_at < 6) & (y_at < 6))
    edge_up = jnp.concatenate([edge_up, edge_up], axis=0).astype(BF)
    spread_e = mm_tn(split_two(edge_rows[...]), edge_up)
    join_e = (edge[0] + spread_e[:32]).astype(BF).astype(F32)
    dz_e = ((edge[2] + spread_e[32:] * (1.0 / 64.0)) * edge[1]).astype(BF).astype(F32)
    for m in range(6):
        for k in range(6):
            at = slice(k * 128, k * 128 + 128)
            over = spread[COARSE_OF[m], COARSE_OF[k]]
            join = (act[m, :, at].astype(F32) + over[:32]).astype(BF).astype(F32)
            v_join[m, :, at] = stacked_row(join, join_e, m * 8 + k, lane)
            dz = (d_join[m, :, at] + over[32:] * (1.0 / 64.0)) * slope[m, :, at]
            v_dz[m, :, at] = stacked_row(dz.astype(BF).astype(F32), dz_e, m * 8 + k, lane)
    for store, weight, result in ((v_join, w_o, out), (v_dz, w_g, g_in)):
        for x in range(4):
            acc[x] = jnp.zeros((32, 512), F32)
        for m in range(6):
            product = mm(weight[...], store[m])
            for a in range(3):
                x = m - a
                if 0 <= x < 4:
                    part = None
                    for b in range(3):
                        at = (3 * a + b) * 32
                        piece = product[at : at + 32, b * 128 : b * 128 + 512]
                        part = piece if part is None else part + piece
                    acc[x] = acc[x] + part
        for x in range(4):
            for y in range(4):
                result[x, y] = acc[x, :, y * 128 : y * 128 + 128].astype(BF)
    flat = [
        [jnp.concatenate([own[arr, x, y] for y in range(4)], axis=1) for x in range(4)]
        for arr in range(2)
    ]
    base = tiles * (i_mid + i_fine)
    for ab in range(9):
        a, b = ab // 3, ab % 3
        at = slice(b * 128, b * 128 + 512)
        total_o = None
        total_i = None
        for x in range(4):
            part_o = mm_nt(v_join[x + a, :, at], flat[1][x])
            part_i = mm_nt(flat[0][x], v_dz[x + a, :, at])
            total_o = part_o if total_o is None else total_o + part_o
            total_i = part_i if total_i is None else total_i + part_i
        by_tap = [total_o[c * 32 : c * 32 + 32] for c in range(3)]
        both = (jnp.concatenate(by_tap, axis=1) * scale, total_i * scale)
        for kind in range(2):
            to = base + (kind * 9 + ab) * i_fine
            for x in range(count_x):
                mbuf[x, to : to + i_fine, 0:96] = both[kind][x * i_fine : (x + 1) * i_fine]
                mbuf[x, to : to + i_fine, 96:128] = jnp.zeros((i_fine, 32), F32)
    used = base + 18 * i_fine
    for x in range(count_x):
        if used < mbuf.shape[1]:
            mbuf[x, used:, :] = jnp.zeros((mbuf.shape[1] - used, 128), F32)
        msg[x] = mbuf[x].astype(BF)


def gz_perm(sizes):
    count_x, count_y, count_z = sizes
    tiles, parts = lane_tiles(sizes)
    span, lift = 128 // count_y, 32 // count_y
    each, lift_each = span // count_z, lift // count_z
    perm = np.zeros((tiles * 128, count_z * parts * 128), np.float32)
    for z in range(count_z):
        base = z * parts * 128
        for tap in range(27):
            for o in range(each):
                perm[tap * span + z * each + o, base + tap * each + o] = 1
        for o in range(lift_each):
            perm[27 * span + z * lift_each + o, base + 27 * each + o] = 1
    return jnp.asarray(perm, BF)


def split_three(value):
    high = value.astype(BF)
    rest = value - high.astype(F32)
    mid = rest.astype(BF)
    low = (rest - mid.astype(F32)).astype(BF)
    return high, mid, low


def regroup(sizes, place, recv, perm, out, buf):
    count_x, count_y, count_z = sizes
    gy = place[1]
    i_mid, i_fine = 128 // count_x, 32 // count_x
    tiles, parts = lane_tiles(sizes)
    total = recv[0].astype(F32)
    for x in range(1, count_x):
        total = total + recv[x].astype(F32)
    base = tiles * i_mid
    mid = jnp.concatenate([total[t * i_mid : (t + 1) * i_mid] for t in range(tiles)], axis=1)
    low = [total[base + t * i_fine : base + (t + 1) * i_fine] for t in range(tiles)]
    low = jnp.concatenate(low, axis=1)
    count = i_mid + i_fine
    padded = -(-count // 16) * 16
    blank = jnp.zeros((padded - count, tiles * 128), F32)
    coarse = jnp.concatenate([mid, low, blank], axis=0)
    moved = None
    for part in split_three(coarse):
        term = mm(part, perm[...])
        moved = term if moved is None else moved + term
    base = tiles * (i_mid + i_fine)
    fine = total[base : base + 18 * i_fine]
    fine = jnp.concatenate([fine, jnp.zeros((128 - 18 * i_fine, 128), F32)], axis=0)
    buf[...] = jnp.transpose(fine)
    each = 32 // (count_y * count_z)
    fine_at = parts * count
    for y in range(count_y):
        keep = ones_where(gy == y)
        for z in range(count_z):
            at = y * count_z + z
            for t in range(parts):
                piece = moved[:count, (z * parts + t) * 128 : (z * parts + t + 1) * 128] * keep
                out[at, t * count : (t + 1) * count, :] = piece
            for c in range(3):
                to = fine_at + c * each
                source = c * 32 + at * each
                out[at, to : to + each, :] = buf[source : source + each, :]
            used = fine_at + 3 * each
            if used < out.shape[1]:
                out[at, used:, :] = jnp.zeros((out.shape[1] - used, 128), F32)


def finish(sizes, recv, fine_in, coarse_in, coarse_mid, lift, fine_out):
    count_x, count_y, count_z = sizes
    i_mid, i_fine = 128 // count_x, 32 // count_x
    _, parts = lane_tiles(sizes)
    total = recv[0]
    for at in range(1, count_y * count_z):
        total = total + recv[at]
    count = i_mid + i_fine
    wide = jnp.concatenate([total[t * count : (t + 1) * count] for t in range(parts)], axis=1)
    each = 128 // (count_y * count_z)
    for tap in range(27):
        piece = wide[:, tap * each : (tap + 1) * each]
        coarse_mid[26 - tap] = piece[:i_mid]
        coarse_in[26 - tap] = piece[i_mid:]
    lift_each = 32 // (count_y * count_z)
    lift[...] = wide[:i_mid, 27 * each : 27 * each + lift_each]
    base = parts * count
    rest = total[base : base + 3 * lift_each]
    rest = jnp.concatenate([rest, jnp.zeros((128 - 3 * lift_each, 128), F32)], axis=0)
    rest = jnp.transpose(rest)
    for ab in range(9):
        for c in range(3):
            side = slice(c * lift_each, (c + 1) * lift_each)
            tap = 3 * ab + c
            fine_out[tap] = rest[ab * i_fine : (ab + 1) * i_fine, side]
            fine_in[26 - tap] = rest[(9 + ab) * i_fine : (10 + ab) * i_fine, side]


def from_below(value, axis):
    count = lax.axis_size(axis)
    return lax.ppermute(value, axis, [(i, i + 1) for i in range(count - 1)])


def from_above(value, axis):
    count = lax.axis_size(axis)
    return lax.ppermute(value, axis, [(i + 1, i) for i in range(count - 1)])


def shape_of(shape, dtype):
    return jax.ShapeDtypeStruct(shape, dtype)


def shards(features, cotangent, w_fine_in, w_coarse_in, w_coarse_mid, w_lift, w_fine_out):
    sizes = (lax.axis_size(GX), lax.axis_size("gy"), lax.axis_size("gz"))
    count_x, count_y, count_z = sizes
    cells = count_x * count_y * count_z * 4 * 4 * 128
    scale = 1.0 / math.sqrt(cells)
    place = jnp.stack([lax.axis_index(GX), lax.axis_index("gy"), lax.axis_index("gz")])
    place = place.astype(jnp.int32)

    own = jnp.stack([features, cotangent]).transpose(0, 2, 3, 1, 4)
    xlo = from_below(own[:, 2:4], GX)
    xhi = from_above(own[:, 0:2], GX)
    y_tail = jnp.concatenate([xlo[:, :, 2:4], own[:, :, 2:4], xhi[:, :, 2:4]], axis=1)
    y_head = jnp.concatenate([xlo[:, :, 0:2], own[:, :, 0:2], xhi[:, :, 0:2]], axis=1)
    ylo = from_below(y_tail, "gy")
    yhi = from_above(y_head, "gy")
    face = call(z_faces, shape_of((2, 2, 32, 128), BF), [], 5, False, 4)(own, xlo, xhi, ylo, yhi)
    face_l = from_below(face, "gz")
    face_r = from_above(face, "gz")
    taps = pltpu.VMEM((288, 96), BF)
    act, slope, d_join, edge, msg = call(
        functools.partial(fine_first, sizes),
        (
            shape_of((6, 32, 768), BF),
            shape_of((6, 32, 768), F32),
            shape_of((6, 32, 768), F32),
            shape_of((3, 32, 128), F32),
            shape_of((32, 64), BF),
        ),
        [pltpu.VMEM((6, 32, 768), F32), pltpu.VMEM((96, 1024), BF), taps, taps],
        11,
        True,
        10,
    )(place, own, xlo, xhi, ylo, yhi, face, face_l, face_r, w_fine_in, w_fine_out)

    z_lo = from_below(msg[24:32], "gz")
    z_hi = from_above(msg[0:8], "gz")
    window = jnp.concatenate(
        [z_lo[8 - PAD :], msg, z_hi[:PAD], jnp.zeros((PITCH - OWN - 2 * PAD, 64), BF)], axis=0
    )
    packed = jnp.concatenate([window[:24], window[24:]], axis=1)
    recv = lax.all_to_all(
        jnp.broadcast_to(packed[None], (count_x * count_y, 24, 128)),
        GX + ("gy",),
        split_axis=0,
        concat_axis=0,
        tiled=True,
    ).reshape(count_x, count_y, 24, 128)

    rows = count_y * PITCH
    wide = rows + 2 * PITCH
    out, grad_input, msg = call(
        functools.partial(second, sizes, scale),
        (
            shape_of((4, 4, 32, 128), BF),
            shape_of((4, 4, 32, 128), BF),
            shape_of((count_x, message_rows(sizes), 128), BF),
        ),
        [
            pltpu.VMEM((11, rows, 64), BF),
            pltpu.VMEM((11, wide, 96), BF),
            pltpu.VMEM((9, wide, 384), BF),
            pltpu.VMEM((7, wide, 384), BF),
            pltpu.VMEM((5, wide + 2 * PITCH, 384), BF),
            pltpu.VMEM((9, rows, 128), F32),
            pltpu.VMEM((7, wide, 128), BF),
            pltpu.VMEM((3, 96, 384), BF),
            pltpu.VMEM((3, 384, 384), BF),
            pltpu.VMEM((3, 384, 384), BF),
            pltpu.VMEM((9, 32, 384), BF),
            pltpu.VMEM((3, 3 * PITCH, 64), F32),
            pltpu.VMEM((24, 64), F32),
            pltpu.VMEM((6, 96, 768), BF),
            pltpu.VMEM((6, 96, 768), BF),
            pltpu.VMEM((4, 32, 512), F32),
            taps,
            taps,
            pltpu.VMEM((count_x, message_rows(sizes), 128), F32),
        ],
        12,
        True,
        34,
    )(
        place, recv, w_coarse_in, w_coarse_mid, w_lift, own, act, slope, d_join, edge,
        w_fine_in, w_fine_out,
    )
    out = out.transpose(2, 0, 1, 3)
    grad_input = grad_input.transpose(2, 0, 1, 3)

    msg = lax.all_to_all(msg, GX, split_axis=0, concat_axis=0, tiled=True)
    msg = call(
        functools.partial(regroup, sizes),
        shape_of((count_y * count_z, final_rows(sizes), 128), F32),
        [pltpu.VMEM((128, 128), F32)],
        3,
        True,
        6,
    )(place, msg, gz_perm(sizes))
    msg = lax.all_to_all(msg, ("gy", "gz"), split_axis=0, concat_axis=0, tiled=True)
    i_mid, i_fine = 128 // count_x, 32 // count_x
    o_mid, o_fine = 128 // (count_y * count_z), 32 // (count_y * count_z)
    grads = call(
        functools.partial(finish, sizes),
        (
            shape_of((27, i_fine, o_fine), F32),
            shape_of((27, i_fine, o_mid), F32),
            shape_of((27, i_mid, o_mid), F32),
            shape_of((i_mid, o_fine), F32),
            shape_of((27, i_fine, o_fine), F32),
        ),
        [],
        1,
        False,
        6,
        False,
    )(msg)
    return (out, grad_input, *grads)


def solution(mesh):
    split = Mesh(
        mesh.devices.reshape(mesh.shape["gx"] // 2, 2, mesh.shape["gy"], mesh.shape["gz"]),
        ("gx_0", "gx_1", "gy", "gz"),
    )
    return jax.shard_map(
        shards,
        mesh=split,
        in_specs=(P(None, GX, "gy", "gz"), P(None, GX, "gy", "gz"), P(), P(), P(), P(), P()),
        out_specs=(
            P(None, GX, "gy", "gz"),
            P(None, GX, "gy", "gz"),
            P(None, GX, ("gy", "gz")),
            P(None, GX, ("gy", "gz")),
            P(None, GX, ("gy", "gz")),
            P(GX, ("gy", "gz")),
            P(None, GX, ("gy", "gz")),
        ),
        check_vma=False,
    )
```

time: 187 us -> 164 us (0.88); the launches traced: 185 us -> 164 us
  local copies, waits for them, and re-layouts: 56.8 us -> 14 us
  blocking collectives: 0 us -> 14.5 us
  waiting for transfers between devices: 37.5 us -> 49.9 us
  starting transfers between devices: 58.5 us -> 55.3 us
    all_to_all x0 -> x1, blocking collectives: none -> 14.5 us  [shards(): msg = lax.all_to_all(msg, GX, split_axis=0, concat_axis=0, tiled=True)]
    transpose x4 -> x0, local copies, waits for them, and re-layouts: 14.1 us -> none  [the longest x3 14.1 us: blocks(): value = value.transpose(4, 1, 0, 3, 5, 2)]
    reshape x15 -> x0, local copies, waits for them, and re-layouts: 12.7 us -> none  [the longest x4 4.62 us: forward_taps(): return weight.reshape(9, 3, 32, 32).transpose(0, 3, 1, 2).reshape(288, 96)]
    concatenate x9 -> x0, local copies, waits for them, and re-layouts: 9.29 us -> none  [the longest x8 9.21 us: shards(): joint = jnp.concatenate(pieces, axis=2).reshape(count_x * count_z, -1)]
    all_to_all x1, waiting for transfers between devices: 16.7 us -> 24.4 us  [shards(): lax.all_to_all(jnp.broadcast_to(packed[None], (count_x * count_y, 24, 128...]
    ppermute x4, waiting for transfers between devices: 6.81 us -> 12.6 us  [from_above(): return lax.ppermute(value, axis, [(i + 1, i) for i in range(count - 1)])]
    ppermute x4, starting transfers between devices: 18.7 us -> 13.4 us  [from_below(): return lax.ppermute(value, axis, [(i, i + 1) for i in range(count - 1)])]
    all_to_all x1, starting transfers between devices: 19.2 us -> 23 us  [shards(): lax.all_to_all(jnp.broadcast_to(packed[None], (count_x * count_y, 24, 128...]
  transfers between devices with their start and end apart: 11 -> 10, of which waited for: 6 -> 7; matrix products, arithmetic and copies ran while one was open for 21% -> 2% of each run, Pallas kernels for 0% -> 0%
where the time goes in v2:
time: 164 us
  starting transfers between devices  55.3 us (34%)
  waiting for transfers between devices  49.9 us (30%)
  Pallas kernels  28.8 us (18%)
  blocking collectives  14.5 us (9%)
  local copies, waits for them, and re-layouts  14 us (9%)
    all_to_all x1, waiting for transfers between devices, shards(): lax.all_to_all(jnp.broadcast_to(packed[None], (count_x * count_y, 24, 128...  24.4 us
    all_to_all x1, starting transfers between devices, shards(): lax.all_to_all(jnp.broadcast_to(packed[None], (count_x * count_y, 24, 128...  23 us
    pallas_call x1, Pallas kernels, shards(): call(functools.partial(second, sizes, scale), (shape_of((4, 4, 32, 128),...  22.9 us
    all_to_all x1, blocking collectives, shards(): msg = lax.all_to_all(msg, GX, split_axis=0, concat_axis=0, tiled=True)  14.5 us
    ppermute x4, starting transfers between devices, from_below(): return lax.ppermute(value, axis, [(i, i + 1) for i in range(count - 1)])  13.4 us
    ppermute x4, waiting for transfers between devices, from_above(): return lax.ppermute(value, axis, [(i + 1, i) for i in range(count - 1)])  12.6 us
    unnamed x40, local copies, waits for them, and re-layouts  11.8 us
    all_to_all x1, waiting for transfers between devices, shards(): lax.all_to_all(msg, ('gy', 'gz'), split_axis=0, concat_axis=0, tiled=True)  11.7 us
  transfers between devices with their start and end apart: 10, of which 7 were waited for; matrix products, arithmetic and copies ran while one was open for 2% of the time, Pallas kernels for 0%

profile of v2, /device:TPU:1, one launch (start us, length us, event | category | flops | bytes accessed | tf_op | source)
XLA Modules:
  0.0 163.7 jit_solution(6198784715014952756)
XLA Ops:
  0.6 1.0 copy_bitcast_fusion
  1.7 4.0 %collective-permute-start = (bf16[2,2,4,32,128]{4,3,2,1,0:T(8,128)(2,1)S(1)}, bf16[2,2,4,32,128]{4,3,2,1,0:T(8,128)(2,1)S(1)}, u32[]{:S(2)}, u32[]{:S(2)}) collective-permute-start(bf16[2,2,4,32,128]{4,3,2,1,0:T(8,128)(2,1)S(1)} %get-tuple-element.43), channel_id=1, source_target_pairs={{0,32},{32,64},{64,96},{96,128},{128,160},{160,192},{192,224},{224... | collective-permute-start | bytes 393224 | tf_op jit(solution)/shard_map/ppermute | solution.py:568
  5.8 1.3 collective-permute-start.1
  7.1 0.6 collective-permute-done.xlo
  7.7 5.2 %collective-permute-done.1.xhi = bf16[2,2,4,32,128]{4,3,2,1,0:T(8,128)(2,1)S(1)} collective-permute-done((bf16[2,2,4,32,128]{4,3,2,1,0:T(8,128)(2,1)S(1)}, bf16[2,2,4,32,128]{4,3,2,1,0:T(8,128)(2,1)S(1)}, u32[]{:S(2)}, u32[]{:S(2)}) %collective-permute-start.1) | collective-permute-done | bytes 131104 | tf_op jit(solution)/shard_map/ppermute | solution.py:573
  12.9 5.8 %collective-permute-start.3 = (bf16[2,8,2,32,128]{4,3,2,1,0:T(8,128)(2,1)S(1)}, bf16[2,8,2,32,128]{4,3,2,1,0:T(8,128)(2,1)S(1)}, u32[]{:S(2)}, u32[]{:S(2)}) collective-permute-start(bf16[2,8,2,32,128]{4,3,2,1,0:T(8,128)(2,1)S(1)} %pad_maximum_fusion.1), channel_id=1, source_target_pairs={{4,0},{8,4},{12,8},{16,12},{20,16},{24,20},{28,24},{5,1},{9,5},{13... | collective-permute-start | bytes 786440 | tf_op jit(solution)/shard_map/ppermute | solution.py:573
  18.8 2.3 %collective-permute-start.2 = (bf16[2,8,2,32,128]{4,3,2,1,0:T(8,128)(2,1)S(1)}, bf16[2,8,2,32,128]{4,3,2,1,0:T(8,128)(2,1)S(1)}, u32[]{:S(2)}, u32[]{:S(2)}) collective-permute-start(bf16[2,8,2,32,128]{4,3,2,1,0:T(8,128)(2,1)S(1)} %pad_maximum_fusion), channel_id=1, source_target_pairs={{0,4},{4,8},{8,12},{12,16},{16,20},{20,24},{24,28},{1,5},{5,9},{9,... | collective-permute-start | bytes 786440 | tf_op jit(solution)/shard_map/ppermute | solution.py:568
  21.1 0.0 copy-start.1
  21.2 4.1 %collective-permute-done.3.yhi = bf16[2,8,2,32,128]{4,3,2,1,0:T(8,128)(2,1)S(1)} collective-permute-done((bf16[2,8,2,32,128]{4,3,2,1,0:T(8,128)(2,1)S(1)}, bf16[2,8,2,32,128]{4,3,2,1,0:T(8,128)(2,1)S(1)}, u32[]{:S(2)}, u32[]{:S(2)}) %collective-permute-start.3) | collective-permute-done | bytes 262176 | tf_op jit(solution)/shard_map/ppermute | solution.py:573
  25.3 0.5 shard_map.135.face
  25.8 3.1 %collective-permute-start.4 = (bf16[2,2,32,128]{3,2,1,0:T(8,128)(2,1)S(1)}, bf16[2,2,32,128]{3,2,1,0:T(8,128)(2,1)S(1)}, u32[]{:S(2)}, u32[]{:S(2)}) collective-permute-start(bf16[2,2,32,128]{3,2,1,0:T(8,128)(2,1)S(1)} %shard_map.135.face), channel_id=1, source_target_pairs={{0,1},{1,2},{2,3},{4,5},{5,6},{6,7},{8,9},{9,10},{10,11},{12,13},{... | collective-permute-start | bytes 98312 | tf_op jit(solution)/shard_map/ppermute | solution.py:568
  28.9 1.3 collective-permute-start.5
  30.2 0.1 pad_add_fusion.place
  30.3 3.3 %collective-permute-done.5.face_r = bf16[2,2,32,128]{3,2,1,0:T(8,128)(2,1)S(1)} collective-permute-done((bf16[2,2,32,128]{3,2,1,0:T(8,128)(2,1)S(1)}, bf16[2,2,32,128]{3,2,1,0:T(8,128)(2,1)S(1)}, u32[]{:S(2)}, u32[]{:S(2)}) %collective-permute-start.5) | collective-permute-done | bytes 32800 | tf_op jit(solution)/shard_map/ppermute | solution.py:573
  33.5 3.6 %shard_map.136 = (bf16[6,32,768]{2,1,0:T(8,128)(2,1)S(1)}, f32[6,32,768]{2,1,0:T(8,128)S(1)}, f32[6,32,768]{2,1,0:T(8,128)S(1)}, f32[3,32,128]{2,1,0:T(8,128)S(1)}, bf16[32,64]{1,0:T(8,128)(2,1)S(1)}) custom-call(s32[3]{0:T(128)S(1)} %pad_add_fusion.place, bf16[2,4,4,32,128]{4,3,2,1,0:T(8,128)(2,1)S(1)} %maximum_bitcast_fusion.own, ...), custom_call_target="tpu_custom_call" | custom-call | tf_op jit(solution)/shard_map/pallas_call | solution.py:599
  37.1 0.0 copy-start.4
  37.2 0.7 copy-done.4
  37.9 0.6 copy-done.12
  38.5 1.3 collective-permute-start.7
  39.8 0.1 pad_slice_fusion
  39.9 4.0 %collective-permute-start.6 = (bf16[8,64]{1,0:T(8,128)(2,1)S(1)}, bf16[8,64]{1,0:T(8,128)(2,1)S(1)}, u32[]{:S(2)}, u32[]{:S(2)}) collective-permute-start(bf16[8,64]{1,0:T(8,128)(2,1)S(1)} %get-tuple-element.49), channel_id=1, source_target_pairs={{0,1},{1,2},{2,3},{4,5},{5,6},{6,7},{8,9},{9,10},{10,11},{12,13},{... | collective-permute-start | bytes 3080 | tf_op jit(solution)/shard_map/ppermute | solution.py:568
  43.9 0.1 fusion
  43.9 0.6 collective-permute-done.6
  44.6 0.1 fusion.1
  44.7 1.0 broadcast_in_dim.10
  45.7 23.0 %all-to-all-start = ((bf16[128,24,128]{2,1,0:T(8,128)(2,1)}), bf16[128,24,128]{2,1,0:T(8,128)(2,1)S(1)}, u32[]{:S(2)}, u32[]{:S(2)}) async-start(bf16[128,24,128]{2,1,0:T(8,128)(2,1)} %broadcast_in_dim.10), calls=%async_computation | async-start | bytes 1572864 | tf_op jit(solution)/shard_map/all_to_all | solution.py:620
  68.7 1.4 copy.17.w_lift
  70.1 24.4 %all-to-all-done = bf16[128,24,128]{2,1,0:T(8,128)(2,1)S(1)} async-done(((bf16[128,24,128]{2,1,0:T(8,128)(2,1)}), bf16[128,24,128]{2,1,0:T(8,128)(2,1)S(1)}, u32[]{:S(2)}, u32[]{:S(2)}) %all-to-all-start) | async-done | bytes 786464 | tf_op jit(solution)/shard_map/all_to_all | solution.py:620
  94.5 0.7 copy-done.15
  95.2 1.0 copy-done.5
  96.1 0.9 copy-done.6
  97.1 0.8 copy-done.7
  97.8 0.8 copy-done.13
  98.6 22.9 %shard_map.137 = (bf16[4,4,32,128]{3,2,1,0:T(8,128)(2,1)S(1)}, bf16[4,4,32,128]{3,2,1,0:T(8,128)(2,1)S(1)}, bf16[16,80,128]{2,1,0:T(8,128)(2,1)S(1)}) custom-call(s32[3]{0:T(128)S(1)} %copy-done.15, bf16[16,8,24,128]{3,2,1,0:T(8,128)(2,1)S(1)} %bitcast.13, bf16[27,32,128]{2,1,0:T(8,128)(2,1)S(1)} %copy-done.6, bf16[27,128,128]{2,1,0:T(8,128)(2,1)S(1)} %copy-done, ...), custom_call_target="tpu_custom_call" | custom-call | tf_op jit(solution)/shard_map/pallas_call | solution.py:630
  121.6 0.0 copy-start.3
  121.6 14.5 %all_to_all.15.recv = bf16[16,80,128]{2,1,0:T(8,128)(2,1)S(1)} all-to-all(bf16[16,80,128]{2,1,0:T(8,128)(2,1)S(1)} %get-tuple-element.27), channel_id=1, replica_groups=mesh['gx_0'=8,'gx_1'=2,'gy'=8,'gz'=4] {'gx_0','gx_1'}, dimensions={0} | all-to-all | bytes 655360 | tf_op jit(solution)/shard_map/all_to_all | solution.py:668
  136.1 1.6 shard_map.138
  137.7 9.1 %all-to-all-start.2 = ((f32[32,16,128]{2,1,0:T(8,128)}), f32[32,16,128]{2,1,0:T(8,128)S(1)}, u32[]{:S(2)}, u32[]{:S(2)}) async-start(f32[32,16,128]{2,1,0:T(8,128)} %shard_map.138), calls=%async_computation.2 | async-start | bytes 524288 | tf_op jit(solution)/shard_map/all_to_all | solution.py:677
  146.9 0.7 copy.18
  147.6 0.2 copy-done.9
  147.8 0.7 copy.19
  148.5 11.7 %all-to-all-done.2.recv = f32[32,16,128]{2,1,0:T(8,128)S(1)} async-done(((f32[32,16,128]{2,1,0:T(8,128)}), f32[32,16,128]{2,1,0:T(8,128)S(1)}, u32[]{:S(2)}, u32[]{:S(2)}) %all-to-all-start.2) | async-done | bytes 262176 | tf_op jit(solution)/shard_map/all_to_all | solution.py:677
  160.2 0.2 shard_map.139
  160.4 0.7 copy.22
  161.1 0.7 copy.21
  161.8 0.6 copy.20
  162.4 0.6 copy.24
  163.1 0.6 copy.23
  (34 shorter events, 0.2 us)
Async XLA Ops:
  1.7 6.0 %collective-permute-start = (bf16[2,2,4,32,128]{4,3,2,1,0:T(8,128)(2,1)S(1)}, bf16[2,2,4,32,128]{4,3,2,1,0:T(8,128)(2,1)S(1)}, u32[]{:S(2)}, u32[]{:S(2)}) collective-permute-start(bf16[2,2,4,32,128]{4,3,2,1,0:T(8,128)(2,1)S(1)} %get-tuple-element.43), channel_id=1, source_target_pairs={{0,32},{32,64},{64,96},{96,128},{128,160},{160,192},{192,224},{224... | collective-permute-start | bytes 393224 | tf_op jit(solution)/shard_map/ppermute | solution.py:568
  5.8 7.1 %collective-permute-start.1 = (bf16[2,2,4,32,128]{4,3,2,1,0:T(8,128)(2,1)S(1)}, bf16[2,2,4,32,128]{4,3,2,1,0:T(8,128)(2,1)S(1)}, u32[]{:S(2)}, u32[]{:S(2)}) collective-permute-start(bf16[2,2,4,32,128]{4,3,2,1,0:T(8,128)(2,1)S(1)} %get-tuple-element.42), channel_id=1, source_target_pairs={{32,0},{64,32},{96,64},{128,96},{160,128},{192,160},{224,192},{256... | collective-permute-start | bytes 393224 | tf_op jit(solution)/shard_map/ppermute | solution.py:573
  12.9 12.3 %collective-permute-start.3 = (bf16[2,8,2,32,128]{4,3,2,1,0:T(8,128)(2,1)S(1)}, bf16[2,8,2,32,128]{4,3,2,1,0:T(8,128)(2,1)S(1)}, u32[]{:S(2)}, u32[]{:S(2)}) collective-permute-start(bf16[2,8,2,32,128]{4,3,2,1,0:T(8,128)(2,1)S(1)} %pad_maximum_fusion.1), channel_id=1, source_target_pairs={{4,0},{8,4},{12,8},{16,12},{20,16},{24,20},{28,24},{5,1},{9,5},{13... | collective-permute-start | bytes 786440 | tf_op jit(solution)/shard_map/ppermute | solution.py:573
  18.8 6.5 %collective-permute-start.2 = (bf16[2,8,2,32,128]{4,3,2,1,0:T(8,128)(2,1)S(1)}, bf16[2,8,2,32,128]{4,3,2,1,0:T(8,128)(2,1)S(1)}, u32[]{:S(2)}, u32[]{:S(2)}) collective-permute-start(bf16[2,8,2,32,128]{4,3,2,1,0:T(8,128)(2,1)S(1)} %pad_maximum_fusion), channel_id=1, source_target_pairs={{0,4},{4,8},{8,12},{12,16},{16,20},{20,24},{24,28},{1,5},{5,9},{9,... | collective-permute-start | bytes 786440 | tf_op jit(solution)/shard_map/ppermute | solution.py:568
  21.1 12.4 %copy-start.1 = (bf16[27,32,32]{2,1,0:T(8,128)(2,1)S(1)}, bf16[27,32,32]{2,1,0:T(8,128)(2,1)}, u32[]{:S(2)}) copy-start(bf16[27,32,32]{2,1,0:T(8,128)(2,1)} %w_fine_in.3) | copy-start | bytes 165892
  21.1 12.4 %copy-start.2 = (bf16[27,32,32]{2,1,0:T(8,128)(2,1)S(1)}, bf16[27,32,32]{2,1,0:T(8,128)(2,1)}, u32[]{:S(2)}) copy-start(bf16[27,32,32]{2,1,0:T(8,128)(2,1)} %w_fine_out.3) | copy-start | bytes 165892
  25.8 4.5 %collective-permute-start.4 = (bf16[2,2,32,128]{3,2,1,0:T(8,128)(2,1)S(1)}, bf16[2,2,32,128]{3,2,1,0:T(8,128)(2,1)S(1)}, u32[]{:S(2)}, u32[]{:S(2)}) collective-permute-start(bf16[2,2,32,128]{3,2,1,0:T(8,128)(2,1)S(1)} %shard_map.135.face), channel_id=1, source_target_pairs={{0,1},{1,2},{2,3},{4,5},{5,6},{6,7},{8,9},{9,10},{10,11},{12,13},{... | collective-permute-start | bytes 98312 | tf_op jit(solution)/shard_map/ppermute | solution.py:568
  28.9 4.7 %collective-permute-start.5 = (bf16[2,2,32,128]{3,2,1,0:T(8,128)(2,1)S(1)}, bf16[2,2,32,128]{3,2,1,0:T(8,128)(2,1)S(1)}, u32[]{:S(2)}, u32[]{:S(2)}) collective-permute-start(bf16[2,2,32,128]{3,2,1,0:T(8,128)(2,1)S(1)} %shard_map.135.face), channel_id=1, source_target_pairs={{1,0},{2,1},{3,2},{5,4},{6,5},{7,6},{9,8},{10,9},{11,10},{13,12},{... | collective-permute-start | bytes 98312 | tf_op jit(solution)/shard_map/ppermute | solution.py:573
  30.3 6.9 %copy-start.14 = (s32[3]{0:T(128)}, s32[3]{0:T(128)S(1)}, u32[]{:S(2)}) copy-start(s32[3]{0:T(128)S(1)} %pad_add_fusion.place) | copy-start | bytes 40
  37.1 0.7 copy-start.4
  37.9 0.6 copy-start.12
  38.5 5.4 %collective-permute-start.7 = (bf16[8,64]{1,0:T(8,128)(2,1)S(1)}, bf16[8,64]{1,0:T(8,128)(2,1)S(1)}, u32[]{:S(2)}, u32[]{:S(2)}) collective-permute-start(bf16[8,64]{1,0:T(8,128)(2,1)S(1)} %get-tuple-element.48), channel_id=1, source_target_pairs={{1,0},{2,1},{3,2},{5,4},{6,5},{7,6},{9,8},{10,9},{11,10},{13,12},{... | collective-permute-start | bytes 3080 | tf_op jit(solution)/shard_map/ppermute | solution.py:573
  39.9 4.7 %collective-permute-start.6 = (bf16[8,64]{1,0:T(8,128)(2,1)S(1)}, bf16[8,64]{1,0:T(8,128)(2,1)S(1)}, u32[]{:S(2)}, u32[]{:S(2)}) collective-permute-start(bf16[8,64]{1,0:T(8,128)(2,1)S(1)} %get-tuple-element.49), channel_id=1, source_target_pairs={{0,1},{1,2},{2,3},{4,5},{5,6},{6,7},{8,9},{9,10},{10,11},{12,13},{... | collective-permute-start | bytes 3080 | tf_op jit(solution)/shard_map/ppermute | solution.py:568
  45.6 48.9 %copy-start = (bf16[27,128,128]{2,1,0:T(8,128)(2,1)S(1)}, bf16[27,128,128]{2,1,0:T(8,128)(2,1)}, u32[]{:S(2)}) copy-start(bf16[27,128,128]{2,1,0:T(8,128)(2,1)} %w_mid.1) | copy-start | bytes 2654212
  45.7 48.8 %all-to-all-start = ((bf16[128,24,128]{2,1,0:T(8,128)(2,1)}), bf16[128,24,128]{2,1,0:T(8,128)(2,1)S(1)}, u32[]{:S(2)}, u32[]{:S(2)}) async-start(bf16[128,24,128]{2,1,0:T(8,128)(2,1)} %broadcast_in_dim.10), calls=%async_computation | async-start | bytes 1572864 | tf_op jit(solution)/shard_map/all_to_all | solution.py:620
  94.5 0.7 copy-start.15
  95.2 1.0 copy-start.5
  96.1 0.9 copy-start.6
  97.1 0.8 copy-start.7
  97.8 0.8 copy-start.13
  121.5 14.6 %copy-start.8 = (bf16[4,4,32,128]{3,2,1,0:T(8,128)(2,1)}, bf16[4,4,32,128]{3,2,1,0:T(8,128)(2,1)S(1)}, u32[]{:S(2)}) copy-start(bf16[4,4,32,128]{3,2,1,0:T(8,128)(2,1)S(1)} %get-tuple-element.26) | copy-start | bytes 393220
  121.6 14.6 %copy-start.10 = (bf16[4,4,32,128]{3,2,1,0:T(8,128)(2,1)}, bf16[4,4,32,128]{3,2,1,0:T(8,128)(2,1)S(1)}, u32[]{:S(2)}) copy-start(bf16[4,4,32,128]{3,2,1,0:T(8,128)(2,1)S(1)} %get-tuple-element.25) | copy-start | bytes 393220
  121.6 14.6 %copy-start.3 = (bf16[512,512]{1,0:T(8,128)(2,1)S(1)}, bf16[512,512]{1,0:T(8,128)(2,1)}, u32[]{:S(2)}) copy-start(bf16[512,512]{1,0:T(8,128)(2,1)} %constant.25.clone.perm) | copy-start | bytes 1572868
  137.7 9.1 %copy-start.11 = (bf16[4,4,32,128]{3,2,1,0:T(8,128)(2,1)S(1)}, bf16[4,4,32,128]{3,2,1,0:T(8,128)(2,1)}, u32[]{:S(2)}) copy-start(bf16[4,4,32,128]{3,2,1,0:T(8,128)(2,1)} %copy-done.10) | copy-start | bytes 393220
  137.7 22.4 %all-to-all-start.2 = ((f32[32,16,128]{2,1,0:T(8,128)}), f32[32,16,128]{2,1,0:T(8,128)S(1)}, u32[]{:S(2)}, u32[]{:S(2)}) async-start(f32[32,16,128]{2,1,0:T(8,128)} %shard_map.138), calls=%async_computation.2 | async-start | bytes 524288 | tf_op jit(solution)/shard_map/all_to_all | solution.py:677
  146.9 0.9 copy-start.9

commit v3 on v2

--- a/solution.py
+++ b/solution.py
@@ -11,6 +11,7 @@
 from jax.sharding import PartitionSpec as P
 
 GX = ("gx_0", "gx_1")
+GY = ("gy_0", "gy_1")
 INTERPRET = False
 BF = jnp.bfloat16
 F32 = jnp.float32
@@ -42,10 +43,11 @@
     return pltpu.roll(value, shift % value.shape[0], 0)
 
 
-def call(body, out_shape, scratch, n_in, smem_first, megabytes, keep_out=True):
+def call(body, out_shape, scratch, n_in, smem_first, megabytes, keep_out=True, in_hbm=0):
     spec = [pl.BlockSpec(memory_space=pltpu.VMEM)] * n_in
     if smem_first:
         spec[0] = pl.BlockSpec(memory_space=pltpu.SMEM)
+    spec = spec + [pl.BlockSpec(memory_space=pl.ANY)] * in_hbm
     out_spec = pl.BlockSpec(memory_space=pltpu.VMEM) if keep_out else pl.BlockSpec()
     return pl.pallas_call(
         body,
@@ -139,7 +141,7 @@
 
 def fine_first(
     sizes, place, own, xlo, xhi, ylo, yhi, face, face_l, face_r, w_fine_in, w_fine_out,
-    act, slope, d_join, edge, msg, acc, vbuf, w_z, w_d,
+    keep, msg, acc, vbuf, w_z, w_d,
 ):
     count_x, count_y, count_z = sizes
     gx, gy, gz = place[0], place[1], place[2]
@@ -191,8 +193,8 @@
             inside = inside * jnp.where(y_at == 0, factor(y_in[0]), 1.0)
             inside = inside * jnp.where(y_at == 5, factor(y_in[5]), 1.0)
             sigma, steep = slope_of(edges)
-            edge[0] = (edges * sigma * inside).astype(BF).astype(F32)
-            edge[1] = steep * inside
+            keep[18, :, 0:128] = (edges * sigma * inside).astype(BF).astype(F32)
+            keep[18, :, 128:256] = steep * inside
             for m in range(6):
                 for k in range(6):
                     at = slice(k * 128, k * 128 + 128)
@@ -200,15 +202,15 @@
                     value = acc[m, :, at]
                     sigma, steep = slope_of(value)
                     first = (value * sigma * mask).astype(BF)
-                    act[m, :, at] = first
-                    slope[m, :, at] = steep * mask
+                    keep[m, :, at] = first.astype(F32)
+                    keep[6 + m, :, at] = steep * mask
                     if 1 <= m < 5 and 1 <= k < 5:
                         total = total + first.astype(F32)
             total = total * (1.0 / 64.0)
         else:
-            edge[2] = edges
+            keep[18, :, 256:384] = edges
             for m in range(6):
-                d_join[m] = acc[m]
+                keep[12 + m] = acc[m]
                 if 1 <= m < 5:
                     for k in range(1, 5):
                         total = total + acc[m, :, k * 128 : k * 128 + 128]
@@ -228,7 +230,7 @@
     count_x, count_y, count_z = sizes
     span, lift = 128 // count_y, 32 // count_y
     first = -(-(27 * span + lift) // 128)
-    second = -(-(27 * span // count_z + lift // count_z) // 128)
+    second = -(-(span // count_z * 32) // 128)
     return first, second
 
 
@@ -243,17 +245,31 @@
     i_mid, i_fine = 128 // sizes[0], 32 // sizes[0]
     _, tiles = lane_tiles(sizes)
     used = tiles * i_mid + tiles * i_fine + 3 * (32 // (sizes[1] * sizes[2]))
-    return -(-used // 8) * 8
+    return -(-used // 16) * 16
 
 
 def second(
-    sizes, scale, place, recv, w_in, w_mid, w_lift, own, act, slope, d_join, edge,
-    w_fine_in, w_fine_out,
+    sizes, scale, place, recv, recv_far, own, keep,
+    w_in_hbm, w_mid_hbm, w_lift_hbm, w_fine_in_hbm, w_fine_out_hbm,
     out, g_in, msg,
     raw, p3, c3, d3, e3, s2, c2, wp_in, wp_mid, bp_mid, b_in, lds, edge_rows,
-    v_join, v_dz, acc, w_o, w_g, mbuf,
+    v_join, v_dz, acc, w_o, w_g, mbuf, w_in, w_mid, w_lift, w_fine_in, w_fine_out, arrived,
 ):
     count_x, count_y, count_z = sizes
+    loads = [
+        pltpu.make_async_copy(source, target, arrived.at[at])
+        for at, (source, target) in enumerate(
+            (
+                (w_in_hbm, w_in),
+                (w_mid_hbm, w_mid),
+                (w_lift_hbm, w_lift),
+                (w_fine_in_hbm, w_fine_in),
+                (w_fine_out_hbm, w_fine_out),
+            )
+        )
+    ]
+    for load in loads:
+        load.start()
     gx, gy, gz = place[0], place[1], place[2]
     rows = count_y * PITCH
     body_rows = slice(PITCH, PITCH + rows)
@@ -271,75 +287,78 @@
             blank = jnp.zeros((pads * PITCH, store.shape[2]), BF)
             store[plane, 0 : pads * PITCH] = blank
             store[plane, pads * PITCH + rows : 2 * pads * PITCH + rows] = blank
+    def inside(plane):
+        at = gx + plane - PAD
+        return (at >= 0) & (at < count_x), jnp.clip(at, 0, count_x - 1)
+
+    def stacked(value):
+        return jnp.concatenate([row_roll(value, 1), value, row_roll(value, -1)], axis=1).astype(BF)
+
+    def unpack(plane, carry):
+        ok, at = inside(plane)
+        valid = ones_where(ok)
+        parts = []
+        for y in range(count_y):
+            near_by = lax.rem(gy, 2) == y % 2
+            block = jnp.where(near_by, recv[at, y // 2], recv_far[at, y // 2]).astype(F32) * valid
+            parts.append(block[:, :64])
+            parts.append(block[:, 64:])
+        whole = jnp.concatenate(parts, axis=0)
+        raw[plane] = whole.astype(BF)
+        first = whole[:, :32]
+        around = [row_roll(first, 1), first, row_roll(first, -1), jnp.zeros((rows, 32), F32)]
+        p3[plane, body_rows, :] = jnp.concatenate(around, axis=1).astype(BF)
+        return carry
+
+    lax.fori_loop(0, 11, unpack, 0)
+
+    for load in loads:
+        load.wait()
+    wp_in[...] = jnp.zeros(wp_in.shape, BF)
     for a in range(3):
         for b in range(3):
             for c in range(3):
                 tap = 9 * a + 3 * b + c
                 side = slice(b * 128, b * 128 + 128)
-                deep = slice(c * 128, c * 128 + 128)
-                wp_in[a, c * 32 : c * 32 + 32, side] = w_in[tap]
-                wp_mid[a, deep, side] = w_mid[tap]
-                bp_mid[a, side, deep] = w_mid[26 - tap]
-                b_in[3 * a + b, :, deep] = w_in[26 - tap]
-
-    def inside(plane):
-        at = gx + plane - PAD
-        return (at >= 0) & (at < count_x), jnp.clip(at, 0, count_x - 1)
-
-    def stacked(value):
-        return jnp.concatenate([row_roll(value, 1), value, row_roll(value, -1)], axis=1).astype(BF)
-
-    def unpack(plane, carry):
-        ok, at = inside(plane)
-        keep = ones_where(ok)
-        parts = []
-        for y in range(count_y):
-            block = recv[at, y].astype(F32) * keep
-            parts.append(block[:, :64])
-            parts.append(block[:, 64:])
-        whole = jnp.concatenate(parts, axis=0)
-        raw[plane] = whole.astype(BF)
-        p3[plane, body_rows, :] = stacked(whole[:, :32])
-        return carry
-
-    lax.fori_loop(0, 11, unpack, 0)
+                deep = slice(a * 384 + c * 128, a * 384 + c * 128 + 128)
+                wp_in[a * 128 + c * 32 : a * 128 + c * 32 + 32, side] = w_in[tap]
+                wp_mid[deep, side] = w_mid[tap]
+                bp_mid[side, deep] = w_mid[26 - tap]
+                b_in[3 * a + b, :, c * 128 : c * 128 + 128] = w_in[26 - tap]
 
     def taps(store, first, pair, alone, product):
-        total = None
-        for a in range(3):
-            both = product(store[first + a, 0 : rows + PITCH, :], pair(a))
-            last = product(store[first + a, 2 * PITCH : 2 * PITCH + rows, :], alone(a))
-            part = both[:rows, :128] + both[PITCH:, 128:] + last
-            total = part if total is None else total + part
-        return total
+        top = [store[first + a, 0 : rows + PITCH, :] for a in range(3)]
+        end = [store[first + a, 2 * PITCH : 2 * PITCH + rows, :] for a in range(3)]
+        both = product(jnp.concatenate(top, axis=1), pair)
+        last = product(jnp.concatenate(end, axis=1), alone)
+        return both[:rows, :128] + both[PITCH:, 128:] + last
 
     def level_2(plane, carry):
         ok, _ = inside(plane)
         mask = z_mask * ones_where(ok)
-        z_2 = taps(p3, plane - 1, lambda a: wp_in[a, :, :256], lambda a: wp_in[a, :, 256:], mm)
+        z_2 = taps(p3, plane - 1, wp_in[:, :256], wp_in[:, 256:], mm)
         sigma, steep = slope_of(z_2)
         s2[plane - 1] = steep * mask
         c3[plane - 1, body_rows, :] = stacked(z_2 * sigma * mask)
         return carry
 
     lax.fori_loop(1, 10, level_2, 0)
-    lift_64 = jnp.concatenate([jnp.zeros((128, 32), F32), w_lift[...].astype(F32)], axis=1)
-    lift_64 = lift_64.astype(BF)
+    lift_64 = jnp.concatenate([jnp.zeros((32, 128), BF), w_lift[...]], axis=0)
 
     def level_3(plane, carry):
         ok, _ = inside(plane)
         mask = z_mask * ones_where(ok)
-        z_3 = taps(c3, plane - 2, lambda a: wp_mid[a, :, :256], lambda a: wp_mid[a, :, 256:], mm)
+        z_3 = taps(c3, plane - 2, wp_mid[:, :256], wp_mid[:, 256:], mm)
         sigma, steep = slope_of(z_3)
         c2[plane - 2, body_rows, :] = (z_3 * sigma * mask).astype(BF)
-        d_third = mm_nt(raw[plane], lift_64)
+        d_third = mm(raw[plane], lift_64)
         d3[plane - 2, body_rows, :] = stacked(d_third * steep)
         return carry
 
     lax.fori_loop(2, 9, level_3, 0)
 
     def level_2_back(plane, carry):
-        total = taps(d3, plane - 3, lambda a: bp_mid[a, :256], lambda a: bp_mid[a, 256:], mm_nt)
+        total = taps(d3, plane - 3, bp_mid[:256, :], bp_mid[256:, :], mm_nt)
         e3[plane - 3, deep_rows, :] = stacked(total * s2[plane - 1])
         return carry
 
@@ -352,7 +371,7 @@
             start = pl.multiple_of((gy + ab % 3) * PITCH, PITCH)
             part = mm_nt(e3[x + ab // 3, pl.ds(start, near), :], b_in[ab])
             d_pool = part if d_pool is None else d_pool + part
-        lifted = mm(c2[2 + x, pl.ds(pl.multiple_of(gy * PITCH, PITCH), near), :], w_lift[...])
+        lifted = mm_nt(c2[2 + x, pl.ds(pl.multiple_of(gy * PITCH, PITCH), near), :], w_lift[...])
         lds[x] = jnp.concatenate([lifted, d_pool], axis=1)
 
     span, lift_span = 128 // count_y, 32 // count_y
@@ -413,15 +432,16 @@
     edge_up = ones_where(edge_up & (x_at < 6) & (y_at < 6))
     edge_up = jnp.concatenate([edge_up, edge_up], axis=0).astype(BF)
     spread_e = mm_tn(split_two(edge_rows[...]), edge_up)
-    join_e = (edge[0] + spread_e[:32]).astype(BF).astype(F32)
-    dz_e = ((edge[2] + spread_e[32:] * (1.0 / 64.0)) * edge[1]).astype(BF).astype(F32)
+    join_e = (keep[18, :, 0:128] + spread_e[:32]).astype(BF).astype(F32)
+    dz_e = (keep[18, :, 256:384] + spread_e[32:] * (1.0 / 64.0)) * keep[18, :, 128:256]
+    dz_e = dz_e.astype(BF).astype(F32)
     for m in range(6):
         for k in range(6):
             at = slice(k * 128, k * 128 + 128)
             over = spread[COARSE_OF[m], COARSE_OF[k]]
-            join = (act[m, :, at].astype(F32) + over[:32]).astype(BF).astype(F32)
+            join = (keep[m, :, at] + over[:32]).astype(BF).astype(F32)
             v_join[m, :, at] = stacked_row(join, join_e, m * 8 + k, lane)
-            dz = (d_join[m, :, at] + over[32:] * (1.0 / 64.0)) * slope[m, :, at]
+            dz = (keep[12 + m, :, at] + over[32:] * (1.0 / 64.0)) * keep[6 + m, :, at]
             v_dz[m, :, at] = stacked_row(dz.astype(BF).astype(F32), dz_e, m * 8 + k, lane)
     for store, weight, result in ((v_join, w_o, out), (v_dz, w_g, g_in)):
         for x in range(4):
@@ -479,9 +499,9 @@
         base = z * parts * 128
         for tap in range(27):
             for o in range(each):
-                perm[tap * span + z * each + o, base + tap * each + o] = 1
+                perm[tap * span + z * each + o, base + o * 32 + 26 - tap] = 1
         for o in range(lift_each):
-            perm[27 * span + z * lift_each + o, base + 27 * each + o] = 1
+            perm[27 * span + z * lift_each + o, base + o * 32 + 27] = 1
     return jnp.asarray(perm, BF)
 
 
@@ -493,7 +513,7 @@
     return high, mid, low
 
 
-def regroup(sizes, place, recv, perm, out, buf):
+def regroup(sizes, place, recv, perm, out, buf, line):
     count_x, count_y, count_z = sizes
     gy = place[1]
     i_mid, i_fine = 128 // count_x, 32 // count_x
@@ -519,48 +539,62 @@
     buf[...] = jnp.transpose(fine)
     each = 32 // (count_y * count_z)
     fine_at = parts * count
+    line[...] = jnp.zeros(line.shape, F32)
     for y in range(count_y):
-        keep = ones_where(gy == y)
+        own_y = ones_where(gy == y)
         for z in range(count_z):
             at = y * count_z + z
             for t in range(parts):
-                piece = moved[:count, (z * parts + t) * 128 : (z * parts + t + 1) * 128] * keep
-                out[at, t * count : (t + 1) * count, :] = piece
+                piece = moved[:count, (z * parts + t) * 128 : (z * parts + t + 1) * 128] * own_y
+                line[t * count : (t + 1) * count, :] = piece
             for c in range(3):
                 to = fine_at + c * each
                 source = c * 32 + at * each
-                out[at, to : to + each, :] = buf[source : source + each, :]
-            used = fine_at + 3 * each
-            if used < out.shape[1]:
-                out[at, used:, :] = jnp.zeros((out.shape[1] - used, 128), F32)
+                line[to : to + each, :] = buf[source : source + each, :]
+            out[at] = line[...].astype(BF)
 
 
 def finish(sizes, recv, fine_in, coarse_in, coarse_mid, lift, fine_out):
     count_x, count_y, count_z = sizes
     i_mid, i_fine = 128 // count_x, 32 // count_x
     _, parts = lane_tiles(sizes)
-    total = recv[0]
+    total = recv[0].astype(F32)
     for at in range(1, count_y * count_z):
-        total = total + recv[at]
+        total = total + recv[at].astype(F32)
     count = i_mid + i_fine
     wide = jnp.concatenate([total[t * count : (t + 1) * count] for t in range(parts)], axis=1)
-    each = 128 // (count_y * count_z)
-    for tap in range(27):
-        piece = wide[:, tap * each : (tap + 1) * each]
-        coarse_mid[26 - tap] = piece[:i_mid]
-        coarse_in[26 - tap] = piece[i_mid:]
+    for o in range(128 // (count_y * count_z)):
+        piece = wide[:, o * 32 : o * 32 + 27]
+        for i in range(i_mid):
+            coarse_mid[i, o : o + 1, :] = piece[i : i + 1]
+        for i in range(i_fine):
+            coarse_in[i, o : o + 1, :] = piece[i_mid + i : i_mid + i + 1]
     lift_each = 32 // (count_y * count_z)
-    lift[...] = wide[:i_mid, 27 * each : 27 * each + lift_each]
+    shape = (8, parts * 128)
+    pick = ones_where(iota(shape, 1) == iota(shape, 0) * 32 + 27)
+    exact = lax.Precision.HIGHEST
+    moved = lax.dot_general(
+        pick, wide[:i_mid], NT, preferred_element_type=F32, precision=exact
+    )
+    lift[...] = moved[:lift_each]
     base = parts * count
-    rest = total[base : base + 3 * lift_each]
-    rest = jnp.concatenate([rest, jnp.zeros((128 - 3 * lift_each, 128), F32)], axis=0)
-    rest = jnp.transpose(rest)
-    for ab in range(9):
+    cell = iota((8, 128), 1)
+    keep = ones_where(iota((8, 128), 0) == cell // (9 * i_fine) * i_fine + cell % i_fine)
+    cell = iota((384, 128), 0) % 128
+    tap = cell // i_fine % 9 * 3 + iota((384, 128), 0) // 128
+    tap = jnp.where(cell // (9 * i_fine) == 0, tap, 26 - tap)
+    perm = ones_where((iota((384, 128), 1) == tap) & (cell < 18 * i_fine))
+    for o in range(lift_each):
+        rows = []
         for c in range(3):
-            side = slice(c * lift_each, (c + 1) * lift_each)
-            tap = 3 * ab + c
-            fine_out[tap] = rest[ab * i_fine : (ab + 1) * i_fine, side]
-            fine_in[26 - tap] = rest[(9 + ab) * i_fine : (10 + ab) * i_fine, side]
+            at = base + c * lift_each + o
+            rows.append(jnp.broadcast_to(total[at : at + 1], (8, 128)) * keep)
+        moved = jnp.dot(
+            jnp.concatenate(rows, axis=1), perm, preferred_element_type=F32, precision=exact
+        )
+        for i in range(i_fine):
+            fine_out[i, o : o + 1, :] = moved[i : i + 1, :27]
+            fine_in[i, o : o + 1, :] = moved[i_fine + i : i_fine + i + 1, :27]
 
 
 def from_below(value, axis):
@@ -578,11 +612,11 @@
 
 
 def shards(features, cotangent, w_fine_in, w_coarse_in, w_coarse_mid, w_lift, w_fine_out):
-    sizes = (lax.axis_size(GX), lax.axis_size("gy"), lax.axis_size("gz"))
+    sizes = (lax.axis_size(GX), lax.axis_size(GY), lax.axis_size("gz"))
     count_x, count_y, count_z = sizes
     cells = count_x * count_y * count_z * 4 * 4 * 128
     scale = 1.0 / math.sqrt(cells)
-    place = jnp.stack([lax.axis_index(GX), lax.axis_index("gy"), lax.axis_index("gz")])
+    place = jnp.stack([lax.axis_index(GX), lax.axis_index(GY), lax.axis_index("gz")])
     place = place.astype(jnp.int32)
 
     own = jnp.stack([features, cotangent]).transpose(0, 2, 3, 1, 4)
@@ -590,19 +624,16 @@
     xhi = from_above(own[:, 0:2], GX)
     y_tail = jnp.concatenate([xlo[:, :, 2:4], own[:, :, 2:4], xhi[:, :, 2:4]], axis=1)
     y_head = jnp.concatenate([xlo[:, :, 0:2], own[:, :, 0:2], xhi[:, :, 0:2]], axis=1)
-    ylo = from_below(y_tail, "gy")
-    yhi = from_above(y_head, "gy")
+    ylo = from_below(y_tail, GY)
+    yhi = from_above(y_head, GY)
     face = call(z_faces, shape_of((2, 2, 32, 128), BF), [], 5, False, 4)(own, xlo, xhi, ylo, yhi)
     face_l = from_below(face, "gz")
     face_r = from_above(face, "gz")
     taps = pltpu.VMEM((288, 96), BF)
-    act, slope, d_join, edge, msg = call(
+    keep, msg = call(
         functools.partial(fine_first, sizes),
         (
-            shape_of((6, 32, 768), BF),
-            shape_of((6, 32, 768), F32),
-            shape_of((6, 32, 768), F32),
-            shape_of((3, 32, 128), F32),
+            shape_of((19, 32, 768), F32),
             shape_of((32, 64), BF),
         ),
         [pltpu.VMEM((6, 32, 768), F32), pltpu.VMEM((96, 1024), BF), taps, taps],
@@ -617,13 +648,15 @@
         [z_lo[8 - PAD :], msg, z_hi[:PAD], jnp.zeros((PITCH - OWN - 2 * PAD, 64), BF)], axis=0
     )
     packed = jnp.concatenate([window[:24], window[24:]], axis=1)
+    half_y = count_y // 2
     recv = lax.all_to_all(
-        jnp.broadcast_to(packed[None], (count_x * count_y, 24, 128)),
-        GX + ("gy",),
+        jnp.broadcast_to(packed[None], (count_x * half_y, 24, 128)),
+        GX + ("gy_0",),
         split_axis=0,
         concat_axis=0,
         tiled=True,
-    ).reshape(count_x, count_y, 24, 128)
+    ).reshape(count_x, half_y, 24, 128)
+    recv_far = lax.ppermute(recv, "gy_1", [(0, 1), (1, 0)])
 
     rows = count_y * PITCH
     wide = rows + 2 * PITCH
@@ -636,15 +669,15 @@
         ),
         [
             pltpu.VMEM((11, rows, 64), BF),
-            pltpu.VMEM((11, wide, 96), BF),
+            pltpu.VMEM((11, wide, 128), BF),
             pltpu.VMEM((9, wide, 384), BF),
             pltpu.VMEM((7, wide, 384), BF),
             pltpu.VMEM((5, wide + 2 * PITCH, 384), BF),
             pltpu.VMEM((9, rows, 128), F32),
             pltpu.VMEM((7, wide, 128), BF),
-            pltpu.VMEM((3, 96, 384), BF),
-            pltpu.VMEM((3, 384, 384), BF),
-            pltpu.VMEM((3, 384, 384), BF),
+            pltpu.VMEM((384, 384), BF),
+            pltpu.VMEM((1152, 384), BF),
+            pltpu.VMEM((384, 1152), BF),
             pltpu.VMEM((9, 32, 384), BF),
             pltpu.VMEM((3, 3 * PITCH, 64), F32),
             pltpu.VMEM((24, 64), F32),
@@ -654,13 +687,20 @@
             taps,
             taps,
             pltpu.VMEM((count_x, message_rows(sizes), 128), F32),
+            pltpu.VMEM((27, 32, 128), BF),
+            pltpu.VMEM((27, 128, 128), BF),
+            pltpu.VMEM((32, 128), BF),
+            pltpu.VMEM((27, 32, 32), BF),
+            pltpu.VMEM((27, 32, 32), BF),
+            pltpu.SemaphoreType.DMA((5,)),
         ],
-        12,
+        5,
         True,
-        34,
+        30,
+        in_hbm=5,
     )(
-        place, recv, w_coarse_in, w_coarse_mid, w_lift, own, act, slope, d_join, edge,
-        w_fine_in, w_fine_out,
+        place, recv, recv_far, own, keep,
+        w_coarse_in, w_coarse_mid, w_lift.T, w_fine_in, w_fine_out,
     )
     out = out.transpose(2, 0, 1, 3)
     grad_input = grad_input.transpose(2, 0, 1, 3)
@@ -668,23 +708,23 @@
     msg = lax.all_to_all(msg, GX, split_axis=0, concat_axis=0, tiled=True)
     msg = call(
         functools.partial(regroup, sizes),
-        shape_of((count_y * count_z, final_rows(sizes), 128), F32),
-        [pltpu.VMEM((128, 128), F32)],
+        shape_of((count_y * count_z, final_rows(sizes), 128), BF),
+        [pltpu.VMEM((128, 128), F32), pltpu.VMEM((final_rows(sizes), 128), F32)],
         3,
         True,
         6,
     )(place, msg, gz_perm(sizes))
-    msg = lax.all_to_all(msg, ("gy", "gz"), split_axis=0, concat_axis=0, tiled=True)
+    msg = lax.all_to_all(msg, GY + ("gz",), split_axis=0, concat_axis=0, tiled=True)
     i_mid, i_fine = 128 // count_x, 32 // count_x
     o_mid, o_fine = 128 // (count_y * count_z), 32 // (count_y * count_z)
     grads = call(
         functools.partial(finish, sizes),
         (
-            shape_of((27, i_fine, o_fine), F32),
-            shape_of((27, i_fine, o_mid), F32),
-            shape_of((27, i_mid, o_mid), F32),
-            shape_of((i_mid, o_fine), F32),
-            shape_of((27, i_fine, o_fine), F32),
+            shape_of((i_fine, o_fine, 27), F32),
+            shape_of((i_fine, o_mid, 27), F32),
+            shape_of((i_mid, o_mid, 27), F32),
+            shape_of((o_fine, i_mid), F32),
+            shape_of((i_fine, o_fine, 27), F32),
         ),
         [],
         1,
@@ -692,26 +732,30 @@
         6,
         False,
     )(msg)
-    return (out, grad_input, *grads)
+    fine_in, coarse_in, coarse_mid, lift, fine_out = grads
+    return (
+        out,
+        grad_input,
+        fine_in.transpose(2, 0, 1),
+        coarse_in.transpose(2, 0, 1),
+        coarse_mid.transpose(2, 0, 1),
+        lift.T,
+        fine_out.transpose(2, 0, 1),
+    )
 
 
 def solution(mesh):
+    shape = mesh.shape
     split = Mesh(
-        mesh.devices.reshape(mesh.shape["gx"] // 2, 2, mesh.shape["gy"], mesh.shape["gz"]),
-        ("gx_0", "gx_1", "gy", "gz"),
+        mesh.devices.reshape(shape["gx"] // 2, 2, shape["gy"] // 2, 2, shape["gz"]),
+        GX + GY + ("gz",),
     )
+    field = P(None, GX, GY, "gz")
+    grad = P(None, GX, GY + ("gz",))
     return jax.shard_map(
         shards,
         mesh=split,
-        in_specs=(P(None, GX, "gy", "gz"), P(None, GX, "gy", "gz"), P(), P(), P(), P(), P()),
-        out_specs=(
-            P(None, GX, "gy", "gz"),
-            P(None, GX, "gy", "gz"),
-            P(None, GX, ("gy", "gz")),
-            P(None, GX, ("gy", "gz")),
-            P(None, GX, ("gy", "gz")),
-            P(GX, ("gy", "gz")),
-            P(None, GX, ("gy", "gz")),
-        ),
+        in_specs=(field, field, P(), P(), P(), P(), P()),
+        out_specs=(field, field, grad, grad, grad, P(GX, GY + ("gz",)), grad),
         check_vma=False,
     )

time: 164 us -> 143 us (0.87)
  blocking collectives: 14.5 us -> 47.5 us
  waiting for transfers between devices: 49.9 us -> 20.7 us
  starting transfers between devices: 55.3 us -> 41.3 us
  local copies, waits for them, and re-layouts: 14 us -> 2.72 us
    all_to_all x0 -> x1, blocking collectives: none -> 33.3 us  [shards(): lax.all_to_all(jnp.broadcast_to(packed[None], (count_x * half_y, 24, 128)...]
    all_to_all x2 -> x1, waiting for transfers between devices: 36 us -> 9.71 us  [shards(): lax.all_to_all(msg, GY + ('gz',), split_axis=0, concat_axis=0, tiled=True)]
    all_to_all x2 -> x1, starting transfers between devices: 32.2 us -> 8.25 us  [shards(): lax.all_to_all(msg, GY + ('gz',), split_axis=0, concat_axis=0, tiled=True)]
    unnamed x40 -> x14, local copies, waits for them, and re-layouts: 11.8 us -> 1.48 us
    ppermute x4, waiting for transfers between devices: 12.6 us -> 6.77 us  [from_above(): return lax.ppermute(value, axis, [(i + 1, i) for i in range(count - 1)])]
    ppermute x4, starting transfers between devices: 13.4 us -> 19 us  [from_below(): return lax.ppermute(value, axis, [(i, i + 1) for i in range(count - 1)])]
    ppermute x0 -> x1, starting transfers between devices: none -> 5.32 us  [shards(): recv_far = lax.ppermute(recv, 'gy_1', [(0, 1), (1, 0)])]
    ppermute x4, waiting for transfers between devices: 1.23 us -> 3.05 us  [from_below(): return lax.ppermute(value, axis, [(i, i + 1) for i in range(count - 1)])]
  transfers between devices with their start and end apart: 10 -> 10, of which waited for: 7 -> 7; matrix products, arithmetic and copies ran while one was open for 2% -> 1% of each run, Pallas kernels for 0% -> 0%
where the time goes in v3:
time: 143 us
  blocking collectives  47.5 us (33%)
  starting transfers between devices  41.3 us (29%)
  Pallas kernels  29.4 us (21%)
  waiting for transfers between devices  20.7 us (14%)
  local copies, waits for them, and re-layouts  2.72 us (2%)
    all_to_all x1, blocking collectives, shards(): lax.all_to_all(jnp.broadcast_to(packed[None], (count_x * half_y, 24, 128)...  33.3 us
    pallas_call x1, Pallas kernels, shards(): call(functools.partial(second, sizes, scale), (shape_of((4, 4, 32, 128),...  22.8 us
    ppermute x4, starting transfers between devices, from_below(): return lax.ppermute(value, axis, [(i, i + 1) for i in range(count - 1)])  19 us
    all_to_all x1, blocking collectives, shards(): msg = lax.all_to_all(msg, GX, split_axis=0, concat_axis=0, tiled=True)  14.2 us
    all_to_all x1, waiting for transfers between devices, shards(): lax.all_to_all(msg, GY + ('gz',), split_axis=0, concat_axis=0, tiled=True)  9.71 us
    ppermute x4, starting transfers between devices, from_above(): return lax.ppermute(value, axis, [(i + 1, i) for i in range(count - 1)])  8.73 us
    all_to_all x1, starting transfers between devices, shards(): lax.all_to_all(msg, GY + ('gz',), split_axis=0, concat_axis=0, tiled=True)  8.25 us
    ppermute x4, waiting for transfers between devices, from_above(): return lax.ppermute(value, axis, [(i + 1, i) for i in range(count - 1)])  6.77 us
  transfers between devices with their start and end apart: 10, of which 7 were waited for; matrix products, arithmetic and copies ran while one was open for 1% of the time, Pallas kernels for 0%

profile of v3, /device:TPU:1, one launch (start us, length us, event | category | flops | bytes accessed | tf_op | source)
XLA Modules:
  0.0 142.8 jit_solution(3569240753638101219)
XLA Ops:
  0.6 1.0 copy_bitcast_fusion
  1.7 0.0 copy-start.1
  1.7 0.0 copy-start.2
  1.8 1.4 collective-permute-start.1
  3.2 4.7 %collective-permute-start = (bf16[2,2,4,32,128]{4,3,2,1,0:T(8,128)(2,1)S(1)}, bf16[2,2,4,32,128]{4,3,2,1,0:T(8,128)(2,1)S(1)}, u32[]{:S(2)}, u32[]{:S(2)}) collective-permute-start(bf16[2,2,4,32,128]{4,3,2,1,0:T(8,128)(2,1)S(1)} %get-tuple-element.37), channel_id=1, source_target_pairs={{0,32},{32,64},{64,96},{96,128},{128,160},{160,192},{192,224},{224... | collective-permute-start | bytes 393224 | tf_op jit(solution)/shard_map/ppermute | solution.py:602
  7.9 0.4 collective-permute-done.1.xhi
  8.3 1.5 %collective-permute-done.xlo = bf16[2,2,4,32,128]{4,3,2,1,0:T(8,128)(2,1)S(1)} collective-permute-done((bf16[2,2,4,32,128]{4,3,2,1,0:T(8,128)(2,1)S(1)}, bf16[2,2,4,32,128]{4,3,2,1,0:T(8,128)(2,1)S(1)}, u32[]{:S(2)}, u32[]{:S(2)}) %collective-permute-start) | collective-permute-done | bytes 131104 | tf_op jit(solution)/shard_map/ppermute | solution.py:602
  9.8 6.1 %collective-permute-start.2 = (bf16[2,8,2,32,128]{4,3,2,1,0:T(8,128)(2,1)S(1)}, bf16[2,8,2,32,128]{4,3,2,1,0:T(8,128)(2,1)S(1)}, u32[]{:S(2)}, u32[]{:S(2)}) collective-permute-start(bf16[2,8,2,32,128]{4,3,2,1,0:T(8,128)(2,1)S(1)} %pad_maximum_fusion), channel_id=1, source_target_pairs={{0,4},{4,8},{8,12},{12,16},{16,20},{20,24},{24,28},{1,5},{5,9},{9,... | collective-permute-start | bytes 786440 | tf_op jit(solution)/shard_map/ppermute | solution.py:602
  16.0 4.7 %collective-permute-start.3 = (bf16[2,8,2,32,128]{4,3,2,1,0:T(8,128)(2,1)S(1)}, bf16[2,8,2,32,128]{4,3,2,1,0:T(8,128)(2,1)S(1)}, u32[]{:S(2)}, u32[]{:S(2)}) collective-permute-start(bf16[2,8,2,32,128]{4,3,2,1,0:T(8,128)(2,1)S(1)} %pad_maximum_fusion.1), channel_id=1, source_target_pairs={{4,0},{8,4},{12,8},{16,12},{20,16},{24,20},{28,24},{5,1},{9,5},{13... | collective-permute-start | bytes 786440 | tf_op jit(solution)/shard_map/ppermute | solution.py:607
  20.7 0.0 copy-start
  20.7 0.0 copy-start.4
  20.7 0.0 copy-start.5
  20.7 0.0 collective-permute-done.2.ylo
  20.8 6.4 %collective-permute-done.3.yhi = bf16[2,8,2,32,128]{4,3,2,1,0:T(8,128)(2,1)S(1)} collective-permute-done((bf16[2,8,2,32,128]{4,3,2,1,0:T(8,128)(2,1)S(1)}, bf16[2,8,2,32,128]{4,3,2,1,0:T(8,128)(2,1)S(1)}, u32[]{:S(2)}, u32[]{:S(2)}) %collective-permute-start.3) | collective-permute-done | bytes 262176 | tf_op jit(solution)/shard_map/ppermute | solution.py:607
  27.1 0.5 shard_map.135.face
  27.6 1.3 collective-permute-start.5
  28.9 4.0 %collective-permute-start.4 = (bf16[2,2,32,128]{3,2,1,0:T(8,128)(2,1)S(1)}, bf16[2,2,32,128]{3,2,1,0:T(8,128)(2,1)S(1)}, u32[]{:S(2)}, u32[]{:S(2)}) collective-permute-start(bf16[2,2,32,128]{3,2,1,0:T(8,128)(2,1)S(1)} %shard_map.135.face), channel_id=1, source_target_pairs={{0,1},{1,2},{2,3},{4,5},{5,6},{6,7},{8,9},{9,10},{10,11},{12,13},{... | collective-permute-start | bytes 98312 | tf_op jit(solution)/shard_map/ppermute | solution.py:602
  32.9 0.1 pad_add_fusion.place
  33.0 0.0 collective-permute-done.5.face_r
  33.0 0.9 collective-permute-done.4.face_l
  33.9 0.0 copy-done.1
  33.9 0.0 copy-done.2
  33.9 3.6 %shard_map.136 = (f32[19,32,768]{2,1,0:T(8,128)S(1)}, bf16[32,64]{1,0:T(8,128)(2,1)S(1)}) custom-call(s32[3]{0:T(128)S(1)} %pad_add_fusion.place, bf16[2,4,4,32,128]{4,3,2,1,0:T(8,128)(2,1)S(1)} %maximum_bitcast_fusion.own, bf16[2,2,4,32,128]{4,3,2,1,0:T(8,128)(2,1)S(1)} %collective-permute-done.xlo, ...), custom_call_target="tpu_custom_call" | custom-call | tf_op jit(solution)/shard_map/pallas_call | solution.py:633
  37.5 1.3 collective-permute-start.7
  38.8 0.1 pad_slice_fusion
  38.9 4.3 %collective-permute-start.6 = (bf16[8,64]{1,0:T(8,128)(2,1)S(1)}, bf16[8,64]{1,0:T(8,128)(2,1)S(1)}, u32[]{:S(2)}, u32[]{:S(2)}) collective-permute-start(bf16[8,64]{1,0:T(8,128)(2,1)S(1)} %get-tuple-element.43), channel_id=1, source_target_pairs={{0,1},{1,2},{2,3},{4,5},{5,6},{6,7},{8,9},{9,10},{10,11},{12,13},{... | collective-permute-start | bytes 3080 | tf_op jit(solution)/shard_map/ppermute | solution.py:602
  43.2 0.0 collective-permute-done.7
  43.2 0.1 fusion
  43.2 0.6 collective-permute-done.6
  43.9 0.1 fusion.1
  44.0 0.1 broadcast_in_dim.10
  44.0 33.3 %all_to_all.15 = bf16[64,24,128]{2,1,0:T(8,128)(2,1)S(1)} all-to-all(bf16[64,24,128]{2,1,0:T(8,128)(2,1)S(1)} %broadcast_in_dim.10), channel_id=1, replica_groups=mesh['gx_0'=8,'gx_1'=2,'gy_0'=4,'gy_1'=2,'gz'=4] {'gx_0','gx_1','gy_0'}, dimensions={0} | all-to-all | bytes 786432 | tf_op jit(solution)/shard_map/all_to_all | solution.py:652
  77.3 5.3 %collective-permute-start.8 = (bf16[16,4,24,128]{3,2,1,0:T(8,128)(2,1)S(1)}, bf16[16,4,24,128]{3,2,1,0:T(8,128)(2,1)S(1)}, u32[]{:S(2)}, u32[]{:S(2)}) collective-permute-start(bf16[16,4,24,128]{3,2,1,0:T(8,128)(2,1)S(1)} %bitcast.19), channel_id=1, source_target_pairs={{0,4},{4,0},{1,5},{5,1},{2,6},{6,2},{3,7},{7,3},{8,12},{12,8},{9,1... | collective-permute-start | bytes 1179656 | tf_op jit(solution)/shard_map/ppermute | solution.py:659
  82.6 1.1 collective-permute-done.8.recv_far
  83.8 0.0 copy-done
  83.8 0.0 copy-done.4
  83.8 0.0 copy-done.5
  83.8 0.0 copy-start.3
  83.8 22.8 %shard_map.137 = (bf16[4,4,32,128]{3,2,1,0:T(8,128)(2,1)S(1)}, bf16[4,4,32,128]{3,2,1,0:T(8,128)(2,1)S(1)}, bf16[16,80,128]{2,1,0:T(8,128)(2,1)S(1)}) custom-call(s32[3]{0:T(128)S(1)} %pad_add_fusion.place, bf16[16,4,24,128]{3,2,1,0:T(8,128)(2,1)S(1)} %bitcast.20, bf16[16,4,24,128]{3,2,1,0:T(8,128)(2,1)S(1)} %collective-permute-done.8.recv_far, ...), custom_call_target="tpu_custom_call" | custom-call | tf_op jit(solution)/shard_map/pallas_call | solution.py:663
  106.6 14.2 %all_to_all.16.recv = bf16[16,80,128]{2,1,0:T(8,128)(2,1)S(1)} all-to-all(bf16[16,80,128]{2,1,0:T(8,128)(2,1)S(1)} %get-tuple-element.21), channel_id=1, replica_groups=mesh['gx_0'=8,'gx_1'=2,'gy_0'=4,'gy_1'=2,'gz'=4] {'gx_0','gx_1'}, dimensions={0} | all-to-all | bytes 655360 | tf_op jit(solution)/shard_map/all_to_all | solution.py:708
  120.8 0.0 copy-done.3
  120.8 1.7 %shard_map.138 = bf16[32,16,128]{2,1,0:T(8,128)(2,1)} custom-call(s32[3]{0:T(128)S(1)} %pad_add_fusion.place, bf16[16,80,128]{2,1,0:T(8,128)(2,1)S(1)} %all_to_all.16.recv, bf16[512,512]{1,0:T(8,128)(2,1)S(1)} %copy-done.3), custom_call_target="tpu_custom_call" | custom-call | tf_op jit(solution)/shard_map/pallas_call | solution.py:709
  122.5 8.2 %all-to-all-start.2 = ((bf16[32,16,128]{2,1,0:T(8,128)(2,1)}), bf16[32,16,128]{2,1,0:T(8,128)(2,1)S(1)}, u32[]{:S(2)}, u32[]{:S(2)}) async-start(bf16[32,16,128]{2,1,0:T(8,128)(2,1)} %shard_map.138), calls=%async_computation.2 | async-start | bytes 262144 | tf_op jit(solution)/shard_map/all_to_all | solution.py:717
  130.8 0.7 copy.17
  131.5 0.7 copy.18
  132.2 9.7 %all-to-all-done.2.recv = bf16[32,16,128]{2,1,0:T(8,128)(2,1)S(1)} async-done(((bf16[32,16,128]{2,1,0:T(8,128)(2,1)}), bf16[32,16,128]{2,1,0:T(8,128)(2,1)S(1)}, u32[]{:S(2)}, u32[]{:S(2)}) %all-to-all-start.2) | async-done | bytes 131104 | tf_op jit(solution)/shard_map/all_to_all | solution.py:717
  141.9 0.8 shard_map.139
  (10 shorter events, 0.2 us)
Async XLA Ops:
  1.7 32.2 %copy-start.1 = (bf16[27,32,32]{2,1,0:T(8,128)(2,1)S(1)}, bf16[27,32,32]{2,1,0:T(8,128)(2,1)}, u32[]{:S(2)}) copy-start(bf16[27,32,32]{2,1,0:T(8,128)(2,1)} %w_fine_in_hbm.1) | copy-start | bytes 165892
  1.7 32.2 %copy-start.2 = (bf16[27,32,32]{2,1,0:T(8,128)(2,1)S(1)}, bf16[27,32,32]{2,1,0:T(8,128)(2,1)}, u32[]{:S(2)}) copy-start(bf16[27,32,32]{2,1,0:T(8,128)(2,1)} %w_fine_out_hbm.1) | copy-start | bytes 165892
  1.8 6.5 %collective-permute-start.1 = (bf16[2,2,4,32,128]{4,3,2,1,0:T(8,128)(2,1)S(1)}, bf16[2,2,4,32,128]{4,3,2,1,0:T(8,128)(2,1)S(1)}, u32[]{:S(2)}, u32[]{:S(2)}) collective-permute-start(bf16[2,2,4,32,128]{4,3,2,1,0:T(8,128)(2,1)S(1)} %get-tuple-element.36), channel_id=1, source_target_pairs={{32,0},{64,32},{96,64},{128,96},{160,128},{192,160},{224,192},{256... | collective-permute-start | bytes 393224 | tf_op jit(solution)/shard_map/ppermute | solution.py:607
  3.2 6.6 %collective-permute-start = (bf16[2,2,4,32,128]{4,3,2,1,0:T(8,128)(2,1)S(1)}, bf16[2,2,4,32,128]{4,3,2,1,0:T(8,128)(2,1)S(1)}, u32[]{:S(2)}, u32[]{:S(2)}) collective-permute-start(bf16[2,2,4,32,128]{4,3,2,1,0:T(8,128)(2,1)S(1)} %get-tuple-element.37), channel_id=1, source_target_pairs={{0,32},{32,64},{64,96},{96,128},{128,160},{160,192},{192,224},{224... | collective-permute-start | bytes 393224 | tf_op jit(solution)/shard_map/ppermute | solution.py:602
  9.8 10.9 %collective-permute-start.2 = (bf16[2,8,2,32,128]{4,3,2,1,0:T(8,128)(2,1)S(1)}, bf16[2,8,2,32,128]{4,3,2,1,0:T(8,128)(2,1)S(1)}, u32[]{:S(2)}, u32[]{:S(2)}) collective-permute-start(bf16[2,8,2,32,128]{4,3,2,1,0:T(8,128)(2,1)S(1)} %pad_maximum_fusion), channel_id=1, source_target_pairs={{0,4},{4,8},{8,12},{12,16},{16,20},{20,24},{24,28},{1,5},{5,9},{9,... | collective-permute-start | bytes 786440 | tf_op jit(solution)/shard_map/ppermute | solution.py:602
  16.0 11.2 %collective-permute-start.3 = (bf16[2,8,2,32,128]{4,3,2,1,0:T(8,128)(2,1)S(1)}, bf16[2,8,2,32,128]{4,3,2,1,0:T(8,128)(2,1)S(1)}, u32[]{:S(2)}, u32[]{:S(2)}) collective-permute-start(bf16[2,8,2,32,128]{4,3,2,1,0:T(8,128)(2,1)S(1)} %pad_maximum_fusion.1), channel_id=1, source_target_pairs={{4,0},{8,4},{12,8},{16,12},{20,16},{24,20},{28,24},{5,1},{9,5},{13... | collective-permute-start | bytes 786440 | tf_op jit(solution)/shard_map/ppermute | solution.py:607
  20.7 63.1 %copy-start = (bf16[27,128,128]{2,1,0:T(8,128)(2,1)S(1)}, bf16[27,128,128]{2,1,0:T(8,128)(2,1)}, u32[]{:S(2)}) copy-start(bf16[27,128,128]{2,1,0:T(8,128)(2,1)} %w_mid_hbm.1) | copy-start | bytes 2654212
  20.7 63.1 %copy-start.4 = (bf16[27,32,128]{2,1,0:T(8,128)(2,1)S(1)}, bf16[27,32,128]{2,1,0:T(8,128)(2,1)}, u32[]{:S(2)}) copy-start(bf16[27,32,128]{2,1,0:T(8,128)(2,1)} %w_in_hbm.1) | copy-start | bytes 663556
  20.7 63.0 %copy-start.5 = (bf16[128,32]{0,1:T(8,128)(2,1)S(1)}, bf16[128,32]{0,1:T(8,128)(2,1)}, u32[]{:S(2)}) copy-start(bf16[128,32]{0,1:T(8,128)(2,1)} %param.13) | copy-start | bytes 24580
  27.6 5.4 %collective-permute-start.5 = (bf16[2,2,32,128]{3,2,1,0:T(8,128)(2,1)S(1)}, bf16[2,2,32,128]{3,2,1,0:T(8,128)(2,1)S(1)}, u32[]{:S(2)}, u32[]{:S(2)}) collective-permute-start(bf16[2,2,32,128]{3,2,1,0:T(8,128)(2,1)S(1)} %shard_map.135.face), channel_id=1, source_target_pairs={{1,0},{2,1},{3,2},{5,4},{6,5},{7,6},{9,8},{10,9},{11,10},{13,12},{... | collective-permute-start | bytes 98312 | tf_op jit(solution)/shard_map/ppermute | solution.py:607
  28.9 5.0 %collective-permute-start.4 = (bf16[2,2,32,128]{3,2,1,0:T(8,128)(2,1)S(1)}, bf16[2,2,32,128]{3,2,1,0:T(8,128)(2,1)S(1)}, u32[]{:S(2)}, u32[]{:S(2)}) collective-permute-start(bf16[2,2,32,128]{3,2,1,0:T(8,128)(2,1)S(1)} %shard_map.135.face), channel_id=1, source_target_pairs={{0,1},{1,2},{2,3},{4,5},{5,6},{6,7},{8,9},{9,10},{10,11},{12,13},{... | collective-permute-start | bytes 98312 | tf_op jit(solution)/shard_map/ppermute | solution.py:602
  37.5 5.7 %collective-permute-start.7 = (bf16[8,64]{1,0:T(8,128)(2,1)S(1)}, bf16[8,64]{1,0:T(8,128)(2,1)S(1)}, u32[]{:S(2)}, u32[]{:S(2)}) collective-permute-start(bf16[8,64]{1,0:T(8,128)(2,1)S(1)} %get-tuple-element.42), channel_id=1, source_target_pairs={{1,0},{2,1},{3,2},{5,4},{6,5},{7,6},{9,8},{10,9},{11,10},{13,12},{... | collective-permute-start | bytes 3080 | tf_op jit(solution)/shard_map/ppermute | solution.py:607
  38.9 5.0 %collective-permute-start.6 = (bf16[8,64]{1,0:T(8,128)(2,1)S(1)}, bf16[8,64]{1,0:T(8,128)(2,1)S(1)}, u32[]{:S(2)}, u32[]{:S(2)}) collective-permute-start(bf16[8,64]{1,0:T(8,128)(2,1)S(1)} %get-tuple-element.43), channel_id=1, source_target_pairs={{0,1},{1,2},{2,3},{4,5},{5,6},{6,7},{8,9},{9,10},{10,11},{12,13},{... | collective-permute-start | bytes 3080 | tf_op jit(solution)/shard_map/ppermute | solution.py:602
  77.3 6.5 %collective-permute-start.8 = (bf16[16,4,24,128]{3,2,1,0:T(8,128)(2,1)S(1)}, bf16[16,4,24,128]{3,2,1,0:T(8,128)(2,1)S(1)}, u32[]{:S(2)}, u32[]{:S(2)}) collective-permute-start(bf16[16,4,24,128]{3,2,1,0:T(8,128)(2,1)S(1)} %bitcast.19), channel_id=1, source_target_pairs={{0,4},{4,0},{1,5},{5,1},{2,6},{6,2},{3,7},{7,3},{8,12},{12,8},{9,1... | collective-permute-start | bytes 1179656 | tf_op jit(solution)/shard_map/ppermute | solution.py:659
  83.8 37.0 %copy-start.3 = (bf16[512,512]{1,0:T(8,128)(2,1)S(1)}, bf16[512,512]{1,0:T(8,128)(2,1)}, u32[]{:S(2)}) copy-start(bf16[512,512]{1,0:T(8,128)(2,1)} %constant.27.clone.perm) | copy-start | bytes 1572868
  122.5 19.4 %all-to-all-start.2 = ((bf16[32,16,128]{2,1,0:T(8,128)(2,1)}), bf16[32,16,128]{2,1,0:T(8,128)(2,1)S(1)}, u32[]{:S(2)}, u32[]{:S(2)}) async-start(bf16[32,16,128]{2,1,0:T(8,128)(2,1)} %shard_map.138), calls=%async_computation.2 | async-start | bytes 262144 | tf_op jit(solution)/shard_map/all_to_all | solution.py:717

commit v4 on v3

--- a/solution.py
+++ b/solution.py
@@ -167,13 +167,17 @@
         edge_1 = jnp.where(lower, left_b, right_b)
         edge_2 = jnp.where(lower, swapped, right_a)
         edges = edge_sum(weight[...], jnp.concatenate([edge_0, edge_1, edge_2], axis=0).astype(BF))
-        for m in range(6):
-            acc[m] = jnp.zeros((32, 768), F32)
-        for xi in range(8):
+        def stack_plane(xi):
             for yi in range(8):
                 value = row(arr, xi, yi).astype(F32)
-                vbuf[:, yi * 128 : yi * 128 + 128] = stacked_row(value, edge_1, xi * 8 + yi, lane)
-            product = mm(weight[...], vbuf[...])
+                line = stacked_row(value, edge_1, xi * 8 + yi, lane)
+                vbuf[xi % 2, :, yi * 128 : yi * 128 + 128] = line
+
+        stack_plane(0)
+        for xi in range(8):
+            if xi < 7:
+                stack_plane(xi + 1)
+            product = mm(weight[...], vbuf[xi % 2])
             for a in range(3):
                 m = xi - a
                 if 0 <= m < 6:
@@ -182,7 +186,7 @@
                         at = (3 * a + b) * 32
                         piece = product[at : at + 32, b * 128 : b * 128 + 768]
                         part = piece if part is None else part + piece
-                    acc[m] = acc[m] + part
+                    acc[m] = part if a == 0 else acc[m] + part
         total = jnp.zeros((32, 128), F32)
         if arr == 0:
             x_at = lane % 64 // 8
@@ -294,7 +298,7 @@
     def stacked(value):
         return jnp.concatenate([row_roll(value, 1), value, row_roll(value, -1)], axis=1).astype(BF)
 
-    def unpack(plane, carry):
+    def unpack(plane):
         ok, at = inside(plane)
         valid = ones_where(ok)
         parts = []
@@ -308,9 +312,6 @@
         first = whole[:, :32]
         around = [row_roll(first, 1), first, row_roll(first, -1), jnp.zeros((rows, 32), F32)]
         p3[plane, body_rows, :] = jnp.concatenate(around, axis=1).astype(BF)
-        return carry
-
-    lax.fori_loop(0, 11, unpack, 0)
 
     for load in loads:
         load.wait()
@@ -333,19 +334,17 @@
         last = product(jnp.concatenate(end, axis=1), alone)
         return both[:rows, :128] + both[PITCH:, 128:] + last
 
-    def level_2(plane, carry):
+    def level_2(plane):
         ok, _ = inside(plane)
         mask = z_mask * ones_where(ok)
         z_2 = taps(p3, plane - 1, wp_in[:, :256], wp_in[:, 256:], mm)
         sigma, steep = slope_of(z_2)
         s2[plane - 1] = steep * mask
         c3[plane - 1, body_rows, :] = stacked(z_2 * sigma * mask)
-        return carry
-
-    lax.fori_loop(1, 10, level_2, 0)
+
     lift_64 = jnp.concatenate([jnp.zeros((32, 128), BF), w_lift[...]], axis=0)
 
-    def level_3(plane, carry):
+    def level_3(plane):
         ok, _ = inside(plane)
         mask = z_mask * ones_where(ok)
         z_3 = taps(c3, plane - 2, wp_mid[:, :256], wp_mid[:, 256:], mm)
@@ -353,16 +352,20 @@
         c2[plane - 2, body_rows, :] = (z_3 * sigma * mask).astype(BF)
         d_third = mm(raw[plane], lift_64)
         d3[plane - 2, body_rows, :] = stacked(d_third * steep)
-        return carry
-
-    lax.fori_loop(2, 9, level_3, 0)
-
-    def level_2_back(plane, carry):
+
+    def level_2_back(plane):
         total = taps(d3, plane - 3, bp_mid[:256, :], bp_mid[256:, :], mm_nt)
         e3[plane - 3, deep_rows, :] = stacked(total * s2[plane - 1])
-        return carry
-
-    lax.fori_loop(3, 8, level_2_back, 0)
+
+    for step in range(14):
+        if step < 11:
+            unpack(step)
+        if 1 <= step - 1 < 10:
+            level_2(step - 1)
+        if 2 <= step - 2 < 9:
+            level_3(step - 2)
+        if 3 <= step - 3 < 8:
+            level_2_back(step - 3)
 
     near = 3 * PITCH
     for x in range(3):
@@ -435,7 +438,7 @@
     join_e = (keep[18, :, 0:128] + spread_e[:32]).astype(BF).astype(F32)
     dz_e = (keep[18, :, 256:384] + spread_e[32:] * (1.0 / 64.0)) * keep[18, :, 128:256]
     dz_e = dz_e.astype(BF).astype(F32)
-    for m in range(6):
+    def stack_plane(m):
         for k in range(6):
             at = slice(k * 128, k * 128 + 128)
             over = spread[COARSE_OF[m], COARSE_OF[k]]
@@ -443,10 +446,12 @@
             v_join[m, :, at] = stacked_row(join, join_e, m * 8 + k, lane)
             dz = (keep[12 + m, :, at] + over[32:] * (1.0 / 64.0)) * keep[6 + m, :, at]
             v_dz[m, :, at] = stacked_row(dz.astype(BF).astype(F32), dz_e, m * 8 + k, lane)
-    for store, weight, result in ((v_join, w_o, out), (v_dz, w_g, g_in)):
-        for x in range(4):
-            acc[x] = jnp.zeros((32, 512), F32)
-        for m in range(6):
+
+    stack_plane(0)
+    for m in range(6):
+        if m < 5:
+            stack_plane(m + 1)
+        for kind, (store, weight) in enumerate(((v_join, w_o), (v_dz, w_g))):
             product = mm(weight[...], store[m])
             for a in range(3):
                 x = m - a
@@ -456,10 +461,14 @@
                         at = (3 * a + b) * 32
                         piece = product[at : at + 32, b * 128 : b * 128 + 512]
                         part = piece if part is None else part + piece
-                    acc[x] = acc[x] + part
-        for x in range(4):
-            for y in range(4):
-                result[x, y] = acc[x, :, y * 128 : y * 128 + 128].astype(BF)
+                    if a == 0:
+                        acc[kind, x] = part
+                    elif a == 1:
+                        acc[kind, x] = acc[kind, x] + part
+                    else:
+                        part = (acc[kind, x] + part).astype(BF)
+                        for y in range(4):
+                            (out, g_in)[kind][x, y] = part[:, y * 128 : y * 128 + 128]
     flat = [
         [jnp.concatenate([own[arr, x, y] for y in range(4)], axis=1) for x in range(4)]
         for arr in range(2)
@@ -476,12 +485,13 @@
             total_o = part_o if total_o is None else total_o + part_o
             total_i = part_i if total_i is None else total_i + part_i
         by_tap = [total_o[c * 32 : c * 32 + 32] for c in range(3)]
-        both = (jnp.concatenate(by_tap, axis=1) * scale, total_i * scale)
+        blank = jnp.zeros((32, 32), F32)
+        total_o = jnp.concatenate([*by_tap, blank], axis=1)
+        both = (total_o * scale, jnp.concatenate([total_i, blank], axis=1) * scale)
         for kind in range(2):
             to = base + (kind * 9 + ab) * i_fine
             for x in range(count_x):
-                mbuf[x, to : to + i_fine, 0:96] = both[kind][x * i_fine : (x + 1) * i_fine]
-                mbuf[x, to : to + i_fine, 96:128] = jnp.zeros((i_fine, 32), F32)
+                mbuf[x, to : to + i_fine, :] = both[kind][x * i_fine : (x + 1) * i_fine]
     used = base + 18 * i_fine
     for x in range(count_x):
         if used < mbuf.shape[1]:
@@ -636,7 +646,7 @@
             shape_of((19, 32, 768), F32),
             shape_of((32, 64), BF),
         ),
-        [pltpu.VMEM((6, 32, 768), F32), pltpu.VMEM((96, 1024), BF), taps, taps],
+        [pltpu.VMEM((6, 32, 768), F32), pltpu.VMEM((2, 96, 1024), BF), taps, taps],
         11,
         True,
         10,
@@ -683,7 +693,7 @@
             pltpu.VMEM((24, 64), F32),
             pltpu.VMEM((6, 96, 768), BF),
             pltpu.VMEM((6, 96, 768), BF),
-            pltpu.VMEM((4, 32, 512), F32),
+            pltpu.VMEM((2, 4, 32, 512), F32),
             taps,
             taps,
             pltpu.VMEM((count_x, message_rows(sizes), 128), F32),

time: 143 us -> 138 us (0.965)
  Pallas kernels: 29.4 us -> 24 us
    pallas_call x1, Pallas kernels: 22.8 us -> 17.4 us  [shards(): call(functools.partial(second, sizes, scale), (shape_of((4, 4, 32, 128),...]
where the time goes in v4:
time: 138 us; the launch traced here: 137 us
  blocking collectives  47.4 us (34%)
  starting transfers between devices  41.2 us (30%)
  Pallas kernels  24 us (17%)
  waiting for transfers between devices  20.9 us (15%)
  local copies, waits for them, and re-layouts  2.72 us (2%)
    all_to_all x1, blocking collectives, shards(): lax.all_to_all(jnp.broadcast_to(packed[None], (count_x * half_y, 24, 128)...  33.3 us
    ppermute x4, starting transfers between devices, from_below(): return lax.ppermute(value, axis, [(i, i + 1) for i in range(count - 1)])  19 us
    pallas_call x1, Pallas kernels, shards(): call(functools.partial(second, sizes, scale), (shape_of((4, 4, 32, 128),...  17.4 us
    all_to_all x1, blocking collectives, shards(): msg = lax.all_to_all(msg, GX, split_axis=0, concat_axis=0, tiled=True)  14.2 us
    all_to_all x1, waiting for transfers between devices, shards(): lax.all_to_all(msg, GY + ('gz',), split_axis=0, concat_axis=0, tiled=True)  9.71 us
    ppermute x4, starting transfers between devices, from_above(): return lax.ppermute(value, axis, [(i + 1, i) for i in range(count - 1)])  8.73 us
    all_to_all x1, starting transfers between devices, shards(): lax.all_to_all(msg, GY + ('gz',), split_axis=0, concat_axis=0, tiled=True)  8.29 us
    ppermute x4, waiting for transfers between devices, from_above(): return lax.ppermute(value, axis, [(i + 1, i) for i in range(count - 1)])  6.77 us
  transfers between devices with their start and end apart: 10, of which 7 were waited for; matrix products, arithmetic and copies ran while one was open for 1% of the time, Pallas kernels for 0%

profile of v4, /device:TPU:1, one launch (start us, length us, event | category | flops | bytes accessed | tf_op | source)
XLA Modules:
  0.0 137.4 jit_solution(566632150016266072)
XLA Ops:
  0.6 1.0 copy_bitcast_fusion
  1.7 0.0 copy-start.1
  1.7 0.0 copy-start.2
  1.8 1.4 %collective-permute-start.1 = (bf16[2,2,4,32,128]{4,3,2,1,0:T(8,128)(2,1)S(1)}, bf16[2,2,4,32,128]{4,3,2,1,0:T(8,128)(2,1)S(1)}, u32[]{:S(2)}, u32[]{:S(2)}) collective-permute-start(bf16[2,2,4,32,128]{4,3,2,1,0:T(8,128)(2,1)S(1)} %get-tuple-element.36), channel_id=1, source_target_pairs={{32,0},{64,32},{96,64},{128,96},{160,128},{192,160},{224,192},{256... | collective-permute-start | bytes 393224 | tf_op jit(solution)/shard_map/ppermute | solution.py:617
  3.2 4.7 %collective-permute-start = (bf16[2,2,4,32,128]{4,3,2,1,0:T(8,128)(2,1)S(1)}, bf16[2,2,4,32,128]{4,3,2,1,0:T(8,128)(2,1)S(1)}, u32[]{:S(2)}, u32[]{:S(2)}) collective-permute-start(bf16[2,2,4,32,128]{4,3,2,1,0:T(8,128)(2,1)S(1)} %get-tuple-element.37), channel_id=1, source_target_pairs={{0,32},{32,64},{64,96},{96,128},{128,160},{160,192},{192,224},{224... | collective-permute-start | bytes 393224 | tf_op jit(solution)/shard_map/ppermute | solution.py:612
  7.9 0.4 collective-permute-done.1.xhi
  8.3 1.5 %collective-permute-done.xlo = bf16[2,2,4,32,128]{4,3,2,1,0:T(8,128)(2,1)S(1)} collective-permute-done((bf16[2,2,4,32,128]{4,3,2,1,0:T(8,128)(2,1)S(1)}, bf16[2,2,4,32,128]{4,3,2,1,0:T(8,128)(2,1)S(1)}, u32[]{:S(2)}, u32[]{:S(2)}) %collective-permute-start) | collective-permute-done | bytes 131104 | tf_op jit(solution)/shard_map/ppermute | solution.py:612
  9.8 6.1 %collective-permute-start.2 = (bf16[2,8,2,32,128]{4,3,2,1,0:T(8,128)(2,1)S(1)}, bf16[2,8,2,32,128]{4,3,2,1,0:T(8,128)(2,1)S(1)}, u32[]{:S(2)}, u32[]{:S(2)}) collective-permute-start(bf16[2,8,2,32,128]{4,3,2,1,0:T(8,128)(2,1)S(1)} %pad_maximum_fusion), channel_id=1, source_target_pairs={{0,4},{4,8},{8,12},{12,16},{16,20},{20,24},{24,28},{1,5},{5,9},{9,... | collective-permute-start | bytes 786440 | tf_op jit(solution)/shard_map/ppermute | solution.py:612
  16.0 4.7 %collective-permute-start.3 = (bf16[2,8,2,32,128]{4,3,2,1,0:T(8,128)(2,1)S(1)}, bf16[2,8,2,32,128]{4,3,2,1,0:T(8,128)(2,1)S(1)}, u32[]{:S(2)}, u32[]{:S(2)}) collective-permute-start(bf16[2,8,2,32,128]{4,3,2,1,0:T(8,128)(2,1)S(1)} %pad_maximum_fusion.1), channel_id=1, source_target_pairs={{4,0},{8,4},{12,8},{16,12},{20,16},{24,20},{28,24},{5,1},{9,5},{13... | collective-permute-start | bytes 786440 | tf_op jit(solution)/shard_map/ppermute | solution.py:617
  20.7 0.0 copy-start
  20.7 0.0 copy-start.4
  20.7 0.0 copy-start.5
  20.7 0.0 collective-permute-done.2.ylo
  20.8 6.4 %collective-permute-done.3.yhi = bf16[2,8,2,32,128]{4,3,2,1,0:T(8,128)(2,1)S(1)} collective-permute-done((bf16[2,8,2,32,128]{4,3,2,1,0:T(8,128)(2,1)S(1)}, bf16[2,8,2,32,128]{4,3,2,1,0:T(8,128)(2,1)S(1)}, u32[]{:S(2)}, u32[]{:S(2)}) %collective-permute-start.3) | collective-permute-done | bytes 262176 | tf_op jit(solution)/shard_map/ppermute | solution.py:617
  27.1 0.5 shard_map.135.face
  27.6 1.3 collective-permute-start.5
  28.9 4.0 %collective-permute-start.4 = (bf16[2,2,32,128]{3,2,1,0:T(8,128)(2,1)S(1)}, bf16[2,2,32,128]{3,2,1,0:T(8,128)(2,1)S(1)}, u32[]{:S(2)}, u32[]{:S(2)}) collective-permute-start(bf16[2,2,32,128]{3,2,1,0:T(8,128)(2,1)S(1)} %shard_map.135.face), channel_id=1, source_target_pairs={{0,1},{1,2},{2,3},{4,5},{5,6},{6,7},{8,9},{9,10},{10,11},{12,13},{... | collective-permute-start | bytes 98312 | tf_op jit(solution)/shard_map/ppermute | solution.py:612
  32.9 0.1 pad_add_fusion.place
  33.0 0.0 collective-permute-done.5.face_r
  33.0 0.9 collective-permute-done.4.face_l
  33.9 0.0 copy-done.1
  33.9 0.0 copy-done.2
  33.9 3.6 %shard_map.136 = (f32[19,32,768]{2,1,0:T(8,128)S(1)}, bf16[32,64]{1,0:T(8,128)(2,1)S(1)}) custom-call(s32[3]{0:T(128)S(1)} %pad_add_fusion.place, bf16[2,4,4,32,128]{4,3,2,1,0:T(8,128)(2,1)S(1)} %maximum_bitcast_fusion.own, bf16[2,2,4,32,128]{4,3,2,1,0:T(8,128)(2,1)S(1)} %collective-permute-done.xlo, ...), custom_call_target="tpu_custom_call" | custom-call | tf_op jit(solution)/shard_map/pallas_call | solution.py:643
  37.5 1.3 collective-permute-start.7
  38.8 0.1 pad_slice_fusion
  38.9 4.3 %collective-permute-start.6 = (bf16[8,64]{1,0:T(8,128)(2,1)S(1)}, bf16[8,64]{1,0:T(8,128)(2,1)S(1)}, u32[]{:S(2)}, u32[]{:S(2)}) collective-permute-start(bf16[8,64]{1,0:T(8,128)(2,1)S(1)} %get-tuple-element.43), channel_id=1, source_target_pairs={{0,1},{1,2},{2,3},{4,5},{5,6},{6,7},{8,9},{9,10},{10,11},{12,13},{... | collective-permute-start | bytes 3080 | tf_op jit(solution)/shard_map/ppermute | solution.py:612
  43.2 0.0 collective-permute-done.7
  43.2 0.1 fusion
  43.3 0.6 collective-permute-done.6
  43.9 0.1 fusion.1
  44.0 0.1 broadcast_in_dim.10
  44.0 33.3 %all_to_all.15 = bf16[64,24,128]{2,1,0:T(8,128)(2,1)S(1)} all-to-all(bf16[64,24,128]{2,1,0:T(8,128)(2,1)S(1)} %broadcast_in_dim.10), channel_id=1, replica_groups=mesh['gx_0'=8,'gx_1'=2,'gy_0'=4,'gy_1'=2,'gz'=4] {'gx_0','gx_1','gy_0'}, dimensions={0} | all-to-all | bytes 786432 | tf_op jit(solution)/shard_map/all_to_all | solution.py:662
  77.3 5.1 %collective-permute-start.8 = (bf16[16,4,24,128]{3,2,1,0:T(8,128)(2,1)S(1)}, bf16[16,4,24,128]{3,2,1,0:T(8,128)(2,1)S(1)}, u32[]{:S(2)}, u32[]{:S(2)}) collective-permute-start(bf16[16,4,24,128]{3,2,1,0:T(8,128)(2,1)S(1)} %bitcast.19), channel_id=1, source_target_pairs={{0,4},{4,0},{1,5},{5,1},{2,6},{6,2},{3,7},{7,3},{8,12},{12,8},{9,1... | collective-permute-start | bytes 1179656 | tf_op jit(solution)/shard_map/ppermute | solution.py:669
  82.4 1.3 collective-permute-done.8.recv_far
  83.8 0.0 copy-done
  83.8 0.0 copy-done.4
  83.8 0.0 copy-done.5
  83.8 0.0 copy-start.3
  83.8 17.4 %shard_map.137 = (bf16[4,4,32,128]{3,2,1,0:T(8,128)(2,1)S(1)}, bf16[4,4,32,128]{3,2,1,0:T(8,128)(2,1)S(1)}, bf16[16,80,128]{2,1,0:T(8,128)(2,1)S(1)}) custom-call(s32[3]{0:T(128)S(1)} %pad_add_fusion.place, bf16[16,4,24,128]{3,2,1,0:T(8,128)(2,1)S(1)} %bitcast.20, bf16[16,4,24,128]{3,2,1,0:T(8,128)(2,1)S(1)} %collective-permute-done.8.recv_far, ...), custom_call_target="tpu_custom_call" | custom-call | tf_op jit(solution)/shard_map/pallas_call | solution.py:673
  101.2 14.2 %all_to_all.16.recv = bf16[16,80,128]{2,1,0:T(8,128)(2,1)S(1)} all-to-all(bf16[16,80,128]{2,1,0:T(8,128)(2,1)S(1)} %get-tuple-element.21), channel_id=1, replica_groups=mesh['gx_0'=8,'gx_1'=2,'gy_0'=4,'gy_1'=2,'gz'=4] {'gx_0','gx_1'}, dimensions={0} | all-to-all | bytes 655360 | tf_op jit(solution)/shard_map/all_to_all | solution.py:718
  115.3 0.0 copy-done.3
  115.3 1.7 %shard_map.138 = bf16[32,16,128]{2,1,0:T(8,128)(2,1)} custom-call(s32[3]{0:T(128)S(1)} %pad_add_fusion.place, bf16[16,80,128]{2,1,0:T(8,128)(2,1)S(1)} %all_to_all.16.recv, bf16[512,512]{1,0:T(8,128)(2,1)S(1)} %copy-done.3), custom_call_target="tpu_custom_call" | custom-call | tf_op jit(solution)/shard_map/pallas_call | solution.py:719
  117.1 8.3 %all-to-all-start.2 = ((bf16[32,16,128]{2,1,0:T(8,128)(2,1)}), bf16[32,16,128]{2,1,0:T(8,128)(2,1)S(1)}, u32[]{:S(2)}, u32[]{:S(2)}) async-start(bf16[32,16,128]{2,1,0:T(8,128)(2,1)} %shard_map.138), calls=%async_computation.2 | async-start | bytes 262144 | tf_op jit(solution)/shard_map/all_to_all | solution.py:727
  125.4 0.7 copy.17
  126.1 0.7 copy.18
  126.8 9.7 %all-to-all-done.2.recv = bf16[32,16,128]{2,1,0:T(8,128)(2,1)S(1)} async-done(((bf16[32,16,128]{2,1,0:T(8,128)(2,1)}), bf16[32,16,128]{2,1,0:T(8,128)(2,1)S(1)}, u32[]{:S(2)}, u32[]{:S(2)}) %all-to-all-start.2) | async-done | bytes 131104 | tf_op jit(solution)/shard_map/all_to_all | solution.py:727
  136.5 0.8 shard_map.139
  (10 shorter events, 0.2 us)
Async XLA Ops:
  1.7 32.2 %copy-start.1 = (bf16[27,32,32]{2,1,0:T(8,128)(2,1)S(1)}, bf16[27,32,32]{2,1,0:T(8,128)(2,1)}, u32[]{:S(2)}) copy-start(bf16[27,32,32]{2,1,0:T(8,128)(2,1)} %w_fine_in_hbm.1) | copy-start | bytes 165892
  1.7 32.2 %copy-start.2 = (bf16[27,32,32]{2,1,0:T(8,128)(2,1)S(1)}, bf16[27,32,32]{2,1,0:T(8,128)(2,1)}, u32[]{:S(2)}) copy-start(bf16[27,32,32]{2,1,0:T(8,128)(2,1)} %w_fine_out_hbm.1) | copy-start | bytes 165892
  1.8 6.5 %collective-permute-start.1 = (bf16[2,2,4,32,128]{4,3,2,1,0:T(8,128)(2,1)S(1)}, bf16[2,2,4,32,128]{4,3,2,1,0:T(8,128)(2,1)S(1)}, u32[]{:S(2)}, u32[]{:S(2)}) collective-permute-start(bf16[2,2,4,32,128]{4,3,2,1,0:T(8,128)(2,1)S(1)} %get-tuple-element.36), channel_id=1, source_target_pairs={{32,0},{64,32},{96,64},{128,96},{160,128},{192,160},{224,192},{256... | collective-permute-start | bytes 393224 | tf_op jit(solution)/shard_map/ppermute | solution.py:617
  3.2 6.6 %collective-permute-start = (bf16[2,2,4,32,128]{4,3,2,1,0:T(8,128)(2,1)S(1)}, bf16[2,2,4,32,128]{4,3,2,1,0:T(8,128)(2,1)S(1)}, u32[]{:S(2)}, u32[]{:S(2)}) collective-permute-start(bf16[2,2,4,32,128]{4,3,2,1,0:T(8,128)(2,1)S(1)} %get-tuple-element.37), channel_id=1, source_target_pairs={{0,32},{32,64},{64,96},{96,128},{128,160},{160,192},{192,224},{224... | collective-permute-start | bytes 393224 | tf_op jit(solution)/shard_map/ppermute | solution.py:612
  9.8 10.9 %collective-permute-start.2 = (bf16[2,8,2,32,128]{4,3,2,1,0:T(8,128)(2,1)S(1)}, bf16[2,8,2,32,128]{4,3,2,1,0:T(8,128)(2,1)S(1)}, u32[]{:S(2)}, u32[]{:S(2)}) collective-permute-start(bf16[2,8,2,32,128]{4,3,2,1,0:T(8,128)(2,1)S(1)} %pad_maximum_fusion), channel_id=1, source_target_pairs={{0,4},{4,8},{8,12},{12,16},{16,20},{20,24},{24,28},{1,5},{5,9},{9,... | collective-permute-start | bytes 786440 | tf_op jit(solution)/shard_map/ppermute | solution.py:612
  16.0 11.2 %collective-permute-start.3 = (bf16[2,8,2,32,128]{4,3,2,1,0:T(8,128)(2,1)S(1)}, bf16[2,8,2,32,128]{4,3,2,1,0:T(8,128)(2,1)S(1)}, u32[]{:S(2)}, u32[]{:S(2)}) collective-permute-start(bf16[2,8,2,32,128]{4,3,2,1,0:T(8,128)(2,1)S(1)} %pad_maximum_fusion.1), channel_id=1, source_target_pairs={{4,0},{8,4},{12,8},{16,12},{20,16},{24,20},{28,24},{5,1},{9,5},{13... | collective-permute-start | bytes 786440 | tf_op jit(solution)/shard_map/ppermute | solution.py:617
  20.7 63.1 %copy-start = (bf16[27,128,128]{2,1,0:T(8,128)(2,1)S(1)}, bf16[27,128,128]{2,1,0:T(8,128)(2,1)}, u32[]{:S(2)}) copy-start(bf16[27,128,128]{2,1,0:T(8,128)(2,1)} %w_mid_hbm.1) | copy-start | bytes 2654212
  20.7 63.1 %copy-start.4 = (bf16[27,32,128]{2,1,0:T(8,128)(2,1)S(1)}, bf16[27,32,128]{2,1,0:T(8,128)(2,1)}, u32[]{:S(2)}) copy-start(bf16[27,32,128]{2,1,0:T(8,128)(2,1)} %w_in_hbm.1) | copy-start | bytes 663556
  20.7 63.0 %copy-start.5 = (bf16[128,32]{0,1:T(8,128)(2,1)S(1)}, bf16[128,32]{0,1:T(8,128)(2,1)}, u32[]{:S(2)}) copy-start(bf16[128,32]{0,1:T(8,128)(2,1)} %param.13) | copy-start | bytes 24580
  27.6 5.4 %collective-permute-start.5 = (bf16[2,2,32,128]{3,2,1,0:T(8,128)(2,1)S(1)}, bf16[2,2,32,128]{3,2,1,0:T(8,128)(2,1)S(1)}, u32[]{:S(2)}, u32[]{:S(2)}) collective-permute-start(bf16[2,2,32,128]{3,2,1,0:T(8,128)(2,1)S(1)} %shard_map.135.face), channel_id=1, source_target_pairs={{1,0},{2,1},{3,2},{5,4},{6,5},{7,6},{9,8},{10,9},{11,10},{13,12},{... | collective-permute-start | bytes 98312 | tf_op jit(solution)/shard_map/ppermute | solution.py:617
  28.9 5.0 %collective-permute-start.4 = (bf16[2,2,32,128]{3,2,1,0:T(8,128)(2,1)S(1)}, bf16[2,2,32,128]{3,2,1,0:T(8,128)(2,1)S(1)}, u32[]{:S(2)}, u32[]{:S(2)}) collective-permute-start(bf16[2,2,32,128]{3,2,1,0:T(8,128)(2,1)S(1)} %shard_map.135.face), channel_id=1, source_target_pairs={{0,1},{1,2},{2,3},{4,5},{5,6},{6,7},{8,9},{9,10},{10,11},{12,13},{... | collective-permute-start | bytes 98312 | tf_op jit(solution)/shard_map/ppermute | solution.py:612
  37.5 5.7 %collective-permute-start.7 = (bf16[8,64]{1,0:T(8,128)(2,1)S(1)}, bf16[8,64]{1,0:T(8,128)(2,1)S(1)}, u32[]{:S(2)}, u32[]{:S(2)}) collective-permute-start(bf16[8,64]{1,0:T(8,128)(2,1)S(1)} %get-tuple-element.42), channel_id=1, source_target_pairs={{1,0},{2,1},{3,2},{5,4},{6,5},{7,6},{9,8},{10,9},{11,10},{13,12},{... | collective-permute-start | bytes 3080 | tf_op jit(solution)/shard_map/ppermute | solution.py:617
  38.9 5.0 %collective-permute-start.6 = (bf16[8,64]{1,0:T(8,128)(2,1)S(1)}, bf16[8,64]{1,0:T(8,128)(2,1)S(1)}, u32[]{:S(2)}, u32[]{:S(2)}) collective-permute-start(bf16[8,64]{1,0:T(8,128)(2,1)S(1)} %get-tuple-element.43), channel_id=1, source_target_pairs={{0,1},{1,2},{2,3},{4,5},{5,6},{6,7},{8,9},{9,10},{10,11},{12,13},{... | collective-permute-start | bytes 3080 | tf_op jit(solution)/shard_map/ppermute | solution.py:612
  77.3 6.5 %collective-permute-start.8 = (bf16[16,4,24,128]{3,2,1,0:T(8,128)(2,1)S(1)}, bf16[16,4,24,128]{3,2,1,0:T(8,128)(2,1)S(1)}, u32[]{:S(2)}, u32[]{:S(2)}) collective-permute-start(bf16[16,4,24,128]{3,2,1,0:T(8,128)(2,1)S(1)} %bitcast.19), channel_id=1, source_target_pairs={{0,4},{4,0},{1,5},{5,1},{2,6},{6,2},{3,7},{7,3},{8,12},{12,8},{9,1... | collective-permute-start | bytes 1179656 | tf_op jit(solution)/shard_map/ppermute | solution.py:669
  83.8 31.6 %copy-start.3 = (bf16[512,512]{1,0:T(8,128)(2,1)S(1)}, bf16[512,512]{1,0:T(8,128)(2,1)}, u32[]{:S(2)}) copy-start(bf16[512,512]{1,0:T(8,128)(2,1)} %constant.27.clone.perm) | copy-start | bytes 1572868
  117.1 19.5 %all-to-all-start.2 = ((bf16[32,16,128]{2,1,0:T(8,128)(2,1)}), bf16[32,16,128]{2,1,0:T(8,128)(2,1)S(1)}, u32[]{:S(2)}, u32[]{:S(2)}) async-start(bf16[32,16,128]{2,1,0:T(8,128)(2,1)} %shard_map.138), calls=%async_computation.2 | async-start | bytes 262144 | tf_op jit(solution)/shard_map/all_to_all | solution.py:727

commit v5 on v4

--- a/solution.py
+++ b/solution.py
@@ -515,14 +515,6 @@
     return jnp.asarray(perm, BF)
 
 
-def split_three(value):
-    high = value.astype(BF)
-    rest = value - high.astype(F32)
-    mid = rest.astype(BF)
-    low = (rest - mid.astype(F32)).astype(BF)
-    return high, mid, low
-
-
 def regroup(sizes, place, recv, perm, out, buf, line):
     count_x, count_y, count_z = sizes
     gy = place[1]
@@ -539,10 +531,7 @@
     padded = -(-count // 16) * 16
     blank = jnp.zeros((padded - count, tiles * 128), F32)
     coarse = jnp.concatenate([mid, low, blank], axis=0)
-    moved = None
-    for part in split_three(coarse):
-        term = mm(part, perm[...])
-        moved = term if moved is None else moved + term
+    moved = mm(coarse.astype(BF), perm[...])
     base = tiles * (i_mid + i_fine)
     fine = total[base : base + 18 * i_fine]
     fine = jnp.concatenate([fine, jnp.zeros((128 - 18 * i_fine, 128), F32)], axis=0)
@@ -712,9 +701,6 @@
         place, recv, recv_far, own, keep,
         w_coarse_in, w_coarse_mid, w_lift.T, w_fine_in, w_fine_out,
     )
-    out = out.transpose(2, 0, 1, 3)
-    grad_input = grad_input.transpose(2, 0, 1, 3)
-
     msg = lax.all_to_all(msg, GX, split_axis=0, concat_axis=0, tiled=True)
     msg = call(
         functools.partial(regroup, sizes),
@@ -725,6 +711,9 @@
         6,
     )(place, msg, gz_perm(sizes))
     msg = lax.all_to_all(msg, GY + ("gz",), split_axis=0, concat_axis=0, tiled=True)
+    out, grad_input, msg = lax.optimization_barrier((out, grad_input, msg))
+    out = out.transpose(2, 0, 1, 3)
+    grad_input = grad_input.transpose(2, 0, 1, 3)
     i_mid, i_fine = 128 // count_x, 32 // count_x
     o_mid, o_fine = 128 // (count_y * count_z), 32 // (count_y * count_z)
     grads = call(

time: 138 us -> 138 us (level)
  blocking collectives: 47.4 us -> 66.7 us
  waiting for transfers between devices: 20.9 us -> 11.2 us
  starting transfers between devices: 41.2 us -> 32.9 us
    all_to_all x0 -> x1, blocking collectives: none -> 19.2 us  [shards(): lax.all_to_all(msg, GY + ('gz',), split_axis=0, concat_axis=0, tiled=True)]
    all_to_all x1 -> x0, waiting for transfers between devices: 9.71 us -> none  [shards(): lax.all_to_all(msg, GY + ('gz',), split_axis=0, concat_axis=0, tiled=True)]
    all_to_all x1 -> x0, starting transfers between devices: 8.29 us -> none  [shards(): lax.all_to_all(msg, GY + ('gz',), split_axis=0, concat_axis=0, tiled=True)]
  transfers between devices with their start and end apart: 10 -> 9, of which waited for: 7 -> 6; matrix products, arithmetic and copies ran while one was open for 1% -> 0% of each run, Pallas kernels for 0% -> 0%
where the time goes in v5:
time: 138 us
  blocking collectives  66.7 us (48%)
  starting transfers between devices  32.9 us (24%)
  Pallas kernels  23.2 us (17%)
  waiting for transfers between devices  11.2 us (8%)
  local copies, waits for them, and re-layouts  2.72 us (2%)
    all_to_all x1, blocking collectives, shards(): lax.all_to_all(jnp.broadcast_to(packed[None], (count_x * half_y, 24, 128)...  33.3 us
    all_to_all x1, blocking collectives, shards(): lax.all_to_all(msg, GY + ('gz',), split_axis=0, concat_axis=0, tiled=True)  19.2 us
    ppermute x4, starting transfers between devices, from_below(): return lax.ppermute(value, axis, [(i, i + 1) for i in range(count - 1)])  19 us
    pallas_call x1, Pallas kernels, shards(): call(functools.partial(second, sizes, scale), (shape_of((4, 4, 32, 128),...  17.4 us
    all_to_all x1, blocking collectives, shards(): msg = lax.all_to_all(msg, GX, split_axis=0, concat_axis=0, tiled=True)  14.2 us
    ppermute x4, starting transfers between devices, from_above(): return lax.ppermute(value, axis, [(i + 1, i) for i in range(count - 1)])  8.73 us
    ppermute x4, waiting for transfers between devices, from_above(): return lax.ppermute(value, axis, [(i + 1, i) for i in range(count - 1)])  6.77 us
    ppermute x1, starting transfers between devices, shards(): recv_far = lax.ppermute(recv, 'gy_1', [(0, 1), (1, 0)])  5.14 us
  transfers between devices with their start and end apart: 9, of which 6 were waited for; matrix products, arithmetic and copies ran while one was open for 0% of the time, Pallas kernels for 0%

profile of v5, /device:TPU:1, one launch (start us, length us, event | category | flops | bytes accessed | tf_op | source)
XLA Modules:
  0.0 137.8 jit_solution(8826939492927590483)
XLA Ops:
  0.6 1.0 copy_bitcast_fusion
  1.7 0.0 copy-start.1
  1.7 0.0 copy-start.2
  1.8 1.4 %collective-permute-start.1 = (bf16[2,2,4,32,128]{4,3,2,1,0:T(8,128)(2,1)S(1)}, bf16[2,2,4,32,128]{4,3,2,1,0:T(8,128)(2,1)S(1)}, u32[]{:S(2)}, u32[]{:S(2)}) collective-permute-start(bf16[2,2,4,32,128]{4,3,2,1,0:T(8,128)(2,1)S(1)} %get-tuple-element.42), channel_id=1, source_target_pairs={{32,0},{64,32},{96,64},{128,96},{160,128},{192,160},{224,192},{256... | collective-permute-start | bytes 393224 | tf_op jit(solution)/shard_map/ppermute | solution.py:606
  3.2 4.7 %collective-permute-start = (bf16[2,2,4,32,128]{4,3,2,1,0:T(8,128)(2,1)S(1)}, bf16[2,2,4,32,128]{4,3,2,1,0:T(8,128)(2,1)S(1)}, u32[]{:S(2)}, u32[]{:S(2)}) collective-permute-start(bf16[2,2,4,32,128]{4,3,2,1,0:T(8,128)(2,1)S(1)} %get-tuple-element.43), channel_id=1, source_target_pairs={{0,32},{32,64},{64,96},{96,128},{128,160},{160,192},{192,224},{224... | collective-permute-start | bytes 393224 | tf_op jit(solution)/shard_map/ppermute | solution.py:601
  7.9 0.4 collective-permute-done.1.xhi
  8.3 1.5 %collective-permute-done.xlo = bf16[2,2,4,32,128]{4,3,2,1,0:T(8,128)(2,1)S(1)} collective-permute-done((bf16[2,2,4,32,128]{4,3,2,1,0:T(8,128)(2,1)S(1)}, bf16[2,2,4,32,128]{4,3,2,1,0:T(8,128)(2,1)S(1)}, u32[]{:S(2)}, u32[]{:S(2)}) %collective-permute-start) | collective-permute-done | bytes 131104 | tf_op jit(solution)/shard_map/ppermute | solution.py:601
  9.8 6.1 %collective-permute-start.2 = (bf16[2,8,2,32,128]{4,3,2,1,0:T(8,128)(2,1)S(1)}, bf16[2,8,2,32,128]{4,3,2,1,0:T(8,128)(2,1)S(1)}, u32[]{:S(2)}, u32[]{:S(2)}) collective-permute-start(bf16[2,8,2,32,128]{4,3,2,1,0:T(8,128)(2,1)S(1)} %pad_maximum_fusion), channel_id=1, source_target_pairs={{0,4},{4,8},{8,12},{12,16},{16,20},{20,24},{24,28},{1,5},{5,9},{9,... | collective-permute-start | bytes 786440 | tf_op jit(solution)/shard_map/ppermute | solution.py:601
  16.0 4.7 %collective-permute-start.3 = (bf16[2,8,2,32,128]{4,3,2,1,0:T(8,128)(2,1)S(1)}, bf16[2,8,2,32,128]{4,3,2,1,0:T(8,128)(2,1)S(1)}, u32[]{:S(2)}, u32[]{:S(2)}) collective-permute-start(bf16[2,8,2,32,128]{4,3,2,1,0:T(8,128)(2,1)S(1)} %pad_maximum_fusion.1), channel_id=1, source_target_pairs={{4,0},{8,4},{12,8},{16,12},{20,16},{24,20},{28,24},{5,1},{9,5},{13... | collective-permute-start | bytes 786440 | tf_op jit(solution)/shard_map/ppermute | solution.py:606
  20.7 0.0 copy-start
  20.7 0.0 copy-start.4
  20.7 0.0 copy-start.5
  20.7 0.0 collective-permute-done.2.ylo
  20.8 6.4 %collective-permute-done.3.yhi = bf16[2,8,2,32,128]{4,3,2,1,0:T(8,128)(2,1)S(1)} collective-permute-done((bf16[2,8,2,32,128]{4,3,2,1,0:T(8,128)(2,1)S(1)}, bf16[2,8,2,32,128]{4,3,2,1,0:T(8,128)(2,1)S(1)}, u32[]{:S(2)}, u32[]{:S(2)}) %collective-permute-start.3) | collective-permute-done | bytes 262176 | tf_op jit(solution)/shard_map/ppermute | solution.py:606
  27.1 0.5 shard_map.135.face
  27.6 1.3 collective-permute-start.5
  28.9 4.0 %collective-permute-start.4 = (bf16[2,2,32,128]{3,2,1,0:T(8,128)(2,1)S(1)}, bf16[2,2,32,128]{3,2,1,0:T(8,128)(2,1)S(1)}, u32[]{:S(2)}, u32[]{:S(2)}) collective-permute-start(bf16[2,2,32,128]{3,2,1,0:T(8,128)(2,1)S(1)} %shard_map.135.face), channel_id=1, source_target_pairs={{0,1},{1,2},{2,3},{4,5},{5,6},{6,7},{8,9},{9,10},{10,11},{12,13},{... | collective-permute-start | bytes 98312 | tf_op jit(solution)/shard_map/ppermute | solution.py:601
  32.9 0.1 pad_add_fusion.place
  33.0 0.0 collective-permute-done.5.face_r
  33.0 0.9 collective-permute-done.4.face_l
  33.9 0.0 copy-done.1
  33.9 0.0 copy-done.2
  33.9 3.6 %shard_map.136 = (f32[19,32,768]{2,1,0:T(8,128)S(1)}, bf16[32,64]{1,0:T(8,128)(2,1)S(1)}) custom-call(s32[3]{0:T(128)S(1)} %pad_add_fusion.place, bf16[2,4,4,32,128]{4,3,2,1,0:T(8,128)(2,1)S(1)} %maximum_bitcast_fusion.own, bf16[2,2,4,32,128]{4,3,2,1,0:T(8,128)(2,1)S(1)} %collective-permute-done.xlo, ...), custom_call_target="tpu_custom_call" | custom-call | tf_op jit(solution)/shard_map/pallas_call | solution.py:632
  37.5 1.3 collective-permute-start.7
  38.8 0.1 pad_slice_fusion
  38.9 4.3 %collective-permute-start.6 = (bf16[8,64]{1,0:T(8,128)(2,1)S(1)}, bf16[8,64]{1,0:T(8,128)(2,1)S(1)}, u32[]{:S(2)}, u32[]{:S(2)}) collective-permute-start(bf16[8,64]{1,0:T(8,128)(2,1)S(1)} %get-tuple-element.49), channel_id=1, source_target_pairs={{0,1},{1,2},{2,3},{4,5},{5,6},{6,7},{8,9},{9,10},{10,11},{12,13},{... | collective-permute-start | bytes 3080 | tf_op jit(solution)/shard_map/ppermute | solution.py:601
  43.2 0.0 collective-permute-done.7
  43.2 0.1 fusion
  43.3 0.6 collective-permute-done.6
  43.9 0.1 fusion.1
  44.0 0.1 broadcast_in_dim.10
  44.0 33.3 %all_to_all.15 = bf16[64,24,128]{2,1,0:T(8,128)(2,1)S(1)} all-to-all(bf16[64,24,128]{2,1,0:T(8,128)(2,1)S(1)} %broadcast_in_dim.10), channel_id=1, replica_groups=mesh['gx_0'=8,'gx_1'=2,'gy_0'=4,'gy_1'=2,'gz'=4] {'gx_0','gx_1','gy_0'}, dimensions={0} | all-to-all | bytes 786432 | tf_op jit(solution)/shard_map/all_to_all | solution.py:651
  77.3 5.1 %collective-permute-start.8 = (bf16[16,4,24,128]{3,2,1,0:T(8,128)(2,1)S(1)}, bf16[16,4,24,128]{3,2,1,0:T(8,128)(2,1)S(1)}, u32[]{:S(2)}, u32[]{:S(2)}) collective-permute-start(bf16[16,4,24,128]{3,2,1,0:T(8,128)(2,1)S(1)} %bitcast.19), channel_id=1, source_target_pairs={{0,4},{4,0},{1,5},{5,1},{2,6},{6,2},{3,7},{7,3},{8,12},{12,8},{9,1... | collective-permute-start | bytes 1179656 | tf_op jit(solution)/shard_map/ppermute | solution.py:658
  82.4 1.3 collective-permute-done.8.recv_far
  83.8 0.0 copy-done
  83.8 0.0 copy-done.4
  83.8 0.0 copy-done.5
  83.8 0.0 copy-start.3
  83.8 17.4 %shard_map.137 = (bf16[4,4,32,128]{3,2,1,0:T(8,128)(2,1)S(1)}, bf16[4,4,32,128]{3,2,1,0:T(8,128)(2,1)S(1)}, bf16[16,80,128]{2,1,0:T(8,128)(2,1)S(1)}) custom-call(s32[3]{0:T(128)S(1)} %pad_add_fusion.place, bf16[16,4,24,128]{3,2,1,0:T(8,128)(2,1)S(1)} %bitcast.20, bf16[16,4,24,128]{3,2,1,0:T(8,128)(2,1)S(1)} %collective-permute-done.8.recv_far, ...), custom_call_target="tpu_custom_call" | custom-call | tf_op jit(solution)/shard_map/pallas_call | solution.py:662
  101.2 14.2 %all_to_all.16.recv = bf16[16,80,128]{2,1,0:T(8,128)(2,1)S(1)} all-to-all(bf16[16,80,128]{2,1,0:T(8,128)(2,1)S(1)} %get-tuple-element.24), channel_id=1, replica_groups=mesh['gx_0'=8,'gx_1'=2,'gy_0'=4,'gy_1'=2,'gz'=4] {'gx_0','gx_1'}, dimensions={0} | all-to-all | bytes 655360 | tf_op jit(solution)/shard_map/all_to_all | solution.py:704
  115.3 0.0 copy-done.3
  115.3 0.9 shard_map.138
  116.3 19.2 %all_to_all.17.recv = bf16[32,16,128]{2,1,0:T(8,128)(2,1)S(1)} all-to-all(bf16[32,16,128]{2,1,0:T(8,128)(2,1)S(1)} %shard_map.138), channel_id=1, replica_groups=mesh['gx_0'=8,'gx_1'=2,'gy_0'=4,'gy_1'=2,'gz'=4] {'gy_0','gy_1','gz'}, dimensions={0} | all-to-all | bytes 262144 | tf_op jit(solution)/shard_map/all_to_all | solution.py:713
  135.5 0.7 copy.17
  136.3 0.7 copy.18
  137.0 0.8 shard_map.139
  (10 shorter events, 0.2 us)
Async XLA Ops:
  1.7 32.2 %copy-start.1 = (bf16[27,32,32]{2,1,0:T(8,128)(2,1)S(1)}, bf16[27,32,32]{2,1,0:T(8,128)(2,1)}, u32[]{:S(2)}) copy-start(bf16[27,32,32]{2,1,0:T(8,128)(2,1)} %w_fine_in_hbm.1) | copy-start | bytes 165892
  1.7 32.2 %copy-start.2 = (bf16[27,32,32]{2,1,0:T(8,128)(2,1)S(1)}, bf16[27,32,32]{2,1,0:T(8,128)(2,1)}, u32[]{:S(2)}) copy-start(bf16[27,32,32]{2,1,0:T(8,128)(2,1)} %w_fine_out_hbm.1) | copy-start | bytes 165892
  1.8 6.5 %collective-permute-start.1 = (bf16[2,2,4,32,128]{4,3,2,1,0:T(8,128)(2,1)S(1)}, bf16[2,2,4,32,128]{4,3,2,1,0:T(8,128)(2,1)S(1)}, u32[]{:S(2)}, u32[]{:S(2)}) collective-permute-start(bf16[2,2,4,32,128]{4,3,2,1,0:T(8,128)(2,1)S(1)} %get-tuple-element.42), channel_id=1, source_target_pairs={{32,0},{64,32},{96,64},{128,96},{160,128},{192,160},{224,192},{256... | collective-permute-start | bytes 393224 | tf_op jit(solution)/shard_map/ppermute | solution.py:606
  3.2 6.6 %collective-permute-start = (bf16[2,2,4,32,128]{4,3,2,1,0:T(8,128)(2,1)S(1)}, bf16[2,2,4,32,128]{4,3,2,1,0:T(8,128)(2,1)S(1)}, u32[]{:S(2)}, u32[]{:S(2)}) collective-permute-start(bf16[2,2,4,32,128]{4,3,2,1,0:T(8,128)(2,1)S(1)} %get-tuple-element.43), channel_id=1, source_target_pairs={{0,32},{32,64},{64,96},{96,128},{128,160},{160,192},{192,224},{224... | collective-permute-start | bytes 393224 | tf_op jit(solution)/shard_map/ppermute | solution.py:601
  9.8 10.9 %collective-permute-start.2 = (bf16[2,8,2,32,128]{4,3,2,1,0:T(8,128)(2,1)S(1)}, bf16[2,8,2,32,128]{4,3,2,1,0:T(8,128)(2,1)S(1)}, u32[]{:S(2)}, u32[]{:S(2)}) collective-permute-start(bf16[2,8,2,32,128]{4,3,2,1,0:T(8,128)(2,1)S(1)} %pad_maximum_fusion), channel_id=1, source_target_pairs={{0,4},{4,8},{8,12},{12,16},{16,20},{20,24},{24,28},{1,5},{5,9},{9,... | collective-permute-start | bytes 786440 | tf_op jit(solution)/shard_map/ppermute | solution.py:601
  16.0 11.2 %collective-permute-start.3 = (bf16[2,8,2,32,128]{4,3,2,1,0:T(8,128)(2,1)S(1)}, bf16[2,8,2,32,128]{4,3,2,1,0:T(8,128)(2,1)S(1)}, u32[]{:S(2)}, u32[]{:S(2)}) collective-permute-start(bf16[2,8,2,32,128]{4,3,2,1,0:T(8,128)(2,1)S(1)} %pad_maximum_fusion.1), channel_id=1, source_target_pairs={{4,0},{8,4},{12,8},{16,12},{20,16},{24,20},{28,24},{5,1},{9,5},{13... | collective-permute-start | bytes 786440 | tf_op jit(solution)/shard_map/ppermute | solution.py:606
  20.7 63.1 %copy-start = (bf16[27,128,128]{2,1,0:T(8,128)(2,1)S(1)}, bf16[27,128,128]{2,1,0:T(8,128)(2,1)}, u32[]{:S(2)}) copy-start(bf16[27,128,128]{2,1,0:T(8,128)(2,1)} %w_mid_hbm.1) | copy-start | bytes 2654212
  20.7 63.1 %copy-start.4 = (bf16[27,32,128]{2,1,0:T(8,128)(2,1)S(1)}, bf16[27,32,128]{2,1,0:T(8,128)(2,1)}, u32[]{:S(2)}) copy-start(bf16[27,32,128]{2,1,0:T(8,128)(2,1)} %w_in_hbm.1) | copy-start | bytes 663556
  20.7 63.0 %copy-start.5 = (bf16[128,32]{0,1:T(8,128)(2,1)S(1)}, bf16[128,32]{0,1:T(8,128)(2,1)}, u32[]{:S(2)}) copy-start(bf16[128,32]{0,1:T(8,128)(2,1)} %param.13) | copy-start | bytes 24580
  27.6 5.4 %collective-permute-start.5 = (bf16[2,2,32,128]{3,2,1,0:T(8,128)(2,1)S(1)}, bf16[2,2,32,128]{3,2,1,0:T(8,128)(2,1)S(1)}, u32[]{:S(2)}, u32[]{:S(2)}) collective-permute-start(bf16[2,2,32,128]{3,2,1,0:T(8,128)(2,1)S(1)} %shard_map.135.face), channel_id=1, source_target_pairs={{1,0},{2,1},{3,2},{5,4},{6,5},{7,6},{9,8},{10,9},{11,10},{13,12},{... | collective-permute-start | bytes 98312 | tf_op jit(solution)/shard_map/ppermute | solution.py:606
  28.9 5.0 %collective-permute-start.4 = (bf16[2,2,32,128]{3,2,1,0:T(8,128)(2,1)S(1)}, bf16[2,2,32,128]{3,2,1,0:T(8,128)(2,1)S(1)}, u32[]{:S(2)}, u32[]{:S(2)}) collective-permute-start(bf16[2,2,32,128]{3,2,1,0:T(8,128)(2,1)S(1)} %shard_map.135.face), channel_id=1, source_target_pairs={{0,1},{1,2},{2,3},{4,5},{5,6},{6,7},{8,9},{9,10},{10,11},{12,13},{... | collective-permute-start | bytes 98312 | tf_op jit(solution)/shard_map/ppermute | solution.py:601
  37.5 5.7 %collective-permute-start.7 = (bf16[8,64]{1,0:T(8,128)(2,1)S(1)}, bf16[8,64]{1,0:T(8,128)(2,1)S(1)}, u32[]{:S(2)}, u32[]{:S(2)}) collective-permute-start(bf16[8,64]{1,0:T(8,128)(2,1)S(1)} %get-tuple-element.48), channel_id=1, source_target_pairs={{1,0},{2,1},{3,2},{5,4},{6,5},{7,6},{9,8},{10,9},{11,10},{13,12},{... | collective-permute-start | bytes 3080 | tf_op jit(solution)/shard_map/ppermute | solution.py:606
  38.9 5.0 %collective-permute-start.6 = (bf16[8,64]{1,0:T(8,128)(2,1)S(1)}, bf16[8,64]{1,0:T(8,128)(2,1)S(1)}, u32[]{:S(2)}, u32[]{:S(2)}) collective-permute-start(bf16[8,64]{1,0:T(8,128)(2,1)S(1)} %get-tuple-element.49), channel_id=1, source_target_pairs={{0,1},{1,2},{2,3},{4,5},{5,6},{6,7},{8,9},{9,10},{10,11},{12,13},{... | collective-permute-start | bytes 3080 | tf_op jit(solution)/shard_map/ppermute | solution.py:601
  77.3 6.5 %collective-permute-start.8 = (bf16[16,4,24,128]{3,2,1,0:T(8,128)(2,1)S(1)}, bf16[16,4,24,128]{3,2,1,0:T(8,128)(2,1)S(1)}, u32[]{:S(2)}, u32[]{:S(2)}) collective-permute-start(bf16[16,4,24,128]{3,2,1,0:T(8,128)(2,1)S(1)} %bitcast.19), channel_id=1, source_target_pairs={{0,4},{4,0},{1,5},{5,1},{2,6},{6,2},{3,7},{7,3},{8,12},{12,8},{9,1... | collective-permute-start | bytes 1179656 | tf_op jit(solution)/shard_map/ppermute | solution.py:658
  83.8 31.6 %copy-start.3 = (bf16[512,512]{1,0:T(8,128)(2,1)S(1)}, bf16[512,512]{1,0:T(8,128)(2,1)}, u32[]{:S(2)}) copy-start(bf16[512,512]{1,0:T(8,128)(2,1)} %constant.27.clone.perm) | copy-start | bytes 1572868

commit v6 on v5

--- a/solution.py
+++ b/solution.py
@@ -313,19 +313,23 @@
         around = [row_roll(first, 1), first, row_roll(first, -1), jnp.zeros((rows, 32), F32)]
         p3[plane, body_rows, :] = jnp.concatenate(around, axis=1).astype(BF)
 
-    for load in loads:
-        load.wait()
-    wp_in[...] = jnp.zeros(wp_in.shape, BF)
-    for a in range(3):
-        for b in range(3):
-            for c in range(3):
-                tap = 9 * a + 3 * b + c
-                side = slice(b * 128, b * 128 + 128)
-                deep = slice(a * 384 + c * 128, a * 384 + c * 128 + 128)
-                wp_in[a * 128 + c * 32 : a * 128 + c * 32 + 32, side] = w_in[tap]
-                wp_mid[deep, side] = w_mid[tap]
-                bp_mid[side, deep] = w_mid[26 - tap]
-                b_in[3 * a + b, :, c * 128 : c * 128 + 128] = w_in[26 - tap]
+    tap_list = [(a, b, c) for a in range(3) for b in range(3) for c in range(3)]
+
+    def weights_in():
+        loads[0].wait()
+        wp_in[...] = jnp.zeros(wp_in.shape, BF)
+        for tap, (a, b, c) in enumerate(tap_list):
+            deep = a * 128 + c * 32
+            wp_in[deep : deep + 32, b * 128 : b * 128 + 128] = w_in[tap]
+            b_in[3 * a + b, :, c * 128 : c * 128 + 128] = w_in[26 - tap]
+
+    def weights_mid():
+        loads[1].wait()
+        for tap, (a, b, c) in enumerate(tap_list):
+            side = slice(b * 128, b * 128 + 128)
+            deep = slice(a * 384 + c * 128, a * 384 + c * 128 + 128)
+            wp_mid[deep, side] = w_mid[tap]
+            bp_mid[side, deep] = w_mid[26 - tap]
 
     def taps(store, first, pair, alone, product):
         top = [store[first + a, 0 : rows + PITCH, :] for a in range(3)]
@@ -342,14 +346,13 @@
         s2[plane - 1] = steep * mask
         c3[plane - 1, body_rows, :] = stacked(z_2 * sigma * mask)
 
-    lift_64 = jnp.concatenate([jnp.zeros((32, 128), BF), w_lift[...]], axis=0)
-
     def level_3(plane):
         ok, _ = inside(plane)
         mask = z_mask * ones_where(ok)
         z_3 = taps(c3, plane - 2, wp_mid[:, :256], wp_mid[:, 256:], mm)
         sigma, steep = slope_of(z_3)
         c2[plane - 2, body_rows, :] = (z_3 * sigma * mask).astype(BF)
+        lift_64 = jnp.concatenate([jnp.zeros((32, 128), BF), w_lift[...]], axis=0)
         d_third = mm(raw[plane], lift_64)
         d3[plane - 2, body_rows, :] = stacked(d_third * steep)
 
@@ -360,6 +363,11 @@
     for step in range(14):
         if step < 11:
             unpack(step)
+        if step == 1:
+            weights_in()
+        if step == 3:
+            weights_mid()
+            loads[2].wait()
         if 1 <= step - 1 < 10:
             level_2(step - 1)
         if 2 <= step - 2 < 9:
@@ -411,6 +419,8 @@
             to = tiles * i_mid + tile * i_fine
             mbuf[x, to : to + i_fine, :] = g_coarse[x * i_fine : (x + 1) * i_fine, at]
 
+    loads[3].wait()
+    loads[4].wait()
     forward_taps(w_fine_out, w_o)
     backward_taps(w_fine_in, w_g)
     lane = iota((32, 128), 1)
@@ -701,6 +711,9 @@
         place, recv, recv_far, own, keep,
         w_coarse_in, w_coarse_mid, w_lift.T, w_fine_in, w_fine_out,
     )
+    out = out.transpose(2, 0, 1, 3)
+    grad_input = grad_input.transpose(2, 0, 1, 3)
+
     msg = lax.all_to_all(msg, GX, split_axis=0, concat_axis=0, tiled=True)
     msg = call(
         functools.partial(regroup, sizes),
@@ -711,9 +724,6 @@
         6,
     )(place, msg, gz_perm(sizes))
     msg = lax.all_to_all(msg, GY + ("gz",), split_axis=0, concat_axis=0, tiled=True)
-    out, grad_input, msg = lax.optimization_barrier((out, grad_input, msg))
-    out = out.transpose(2, 0, 1, 3)
-    grad_input = grad_input.transpose(2, 0, 1, 3)
     i_mid, i_fine = 128 // count_x, 32 // count_x
     o_mid, o_fine = 128 // (count_y * count_z), 32 // (count_y * count_z)
     grads = call(

time: 138 us -> 138 us (level)
  blocking collectives: 66.7 us -> 47.4 us
  waiting for transfers between devices: 11.2 us -> 20.9 us
  starting transfers between devices: 32.9 us -> 41.1 us
    all_to_all x1 -> x0, blocking collectives: 19.2 us -> none  [shards(): lax.all_to_all(msg, GY + ('gz',), split_axis=0, concat_axis=0, tiled=True)]
    all_to_all x0 -> x1, waiting for transfers between devices: none -> 9.71 us  [shards(): lax.all_to_all(msg, GY + ('gz',), split_axis=0, concat_axis=0, tiled=True)]
    all_to_all x0 -> x1, starting transfers between devices: none -> 8.27 us  [shards(): lax.all_to_all(msg, GY + ('gz',), split_axis=0, concat_axis=0, tiled=True)]
  transfers between devices with their start and end apart: 9 -> 10, of which waited for: 6 -> 7; matrix products, arithmetic and copies ran while one was open for 0% -> 1% of each run, Pallas kernels for 0% -> 0%
where the time goes in v6:
time: 138 us
  blocking collectives  47.4 us (34%)
  starting transfers between devices  41.1 us (30%)
  Pallas kernels  24.2 us (18%)
  waiting for transfers between devices  20.9 us (15%)
  local copies, waits for them, and re-layouts  2.72 us (2%)
    all_to_all x1, blocking collectives, shards(): lax.all_to_all(jnp.broadcast_to(packed[None], (count_x * half_y, 24, 128)...  33.3 us
    ppermute x4, starting transfers between devices, from_below(): return lax.ppermute(value, axis, [(i, i + 1) for i in range(count - 1)])  19 us
    pallas_call x1, Pallas kernels, shards(): call(functools.partial(second, sizes, scale), (shape_of((4, 4, 32, 128),...  17.7 us
    all_to_all x1, blocking collectives, shards(): msg = lax.all_to_all(msg, GX, split_axis=0, concat_axis=0, tiled=True)  14.2 us
    all_to_all x1, waiting for transfers between devices, shards(): lax.all_to_all(msg, GY + ('gz',), split_axis=0, concat_axis=0, tiled=True)  9.71 us
    ppermute x4, starting transfers between devices, from_above(): return lax.ppermute(value, axis, [(i + 1, i) for i in range(count - 1)])  8.73 us
    all_to_all x1, starting transfers between devices, shards(): lax.all_to_all(msg, GY + ('gz',), split_axis=0, concat_axis=0, tiled=True)  8.27 us
    ppermute x4, waiting for transfers between devices, from_above(): return lax.ppermute(value, axis, [(i + 1, i) for i in range(count - 1)])  6.77 us
  transfers between devices with their start and end apart: 10, of which 7 were waited for; matrix products, arithmetic and copies ran while one was open for 1% of the time, Pallas kernels for 0%

profile of v6, /device:TPU:1, one launch (start us, length us, event | category | flops | bytes accessed | tf_op | source)
XLA Modules:
  0.0 137.6 jit_solution(9723482889316184995)
XLA Ops:
  0.6 1.0 copy_bitcast_fusion
  1.7 0.0 copy-start.1
  1.7 0.0 copy-start.2
  1.8 1.4 %collective-permute-start.1 = (bf16[2,2,4,32,128]{4,3,2,1,0:T(8,128)(2,1)S(1)}, bf16[2,2,4,32,128]{4,3,2,1,0:T(8,128)(2,1)S(1)}, u32[]{:S(2)}, u32[]{:S(2)}) collective-permute-start(bf16[2,2,4,32,128]{4,3,2,1,0:T(8,128)(2,1)S(1)} %get-tuple-element.36), channel_id=1, source_target_pairs={{32,0},{64,32},{96,64},{128,96},{160,128},{192,160},{224,192},{256... | collective-permute-start | bytes 393224 | tf_op jit(solution)/shard_map/ppermute | solution.py:616
  3.2 4.7 %collective-permute-start = (bf16[2,2,4,32,128]{4,3,2,1,0:T(8,128)(2,1)S(1)}, bf16[2,2,4,32,128]{4,3,2,1,0:T(8,128)(2,1)S(1)}, u32[]{:S(2)}, u32[]{:S(2)}) collective-permute-start(bf16[2,2,4,32,128]{4,3,2,1,0:T(8,128)(2,1)S(1)} %get-tuple-element.37), channel_id=1, source_target_pairs={{0,32},{32,64},{64,96},{96,128},{128,160},{160,192},{192,224},{224... | collective-permute-start | bytes 393224 | tf_op jit(solution)/shard_map/ppermute | solution.py:611
  7.9 0.4 collective-permute-done.1.xhi
  8.3 1.5 %collective-permute-done.xlo = bf16[2,2,4,32,128]{4,3,2,1,0:T(8,128)(2,1)S(1)} collective-permute-done((bf16[2,2,4,32,128]{4,3,2,1,0:T(8,128)(2,1)S(1)}, bf16[2,2,4,32,128]{4,3,2,1,0:T(8,128)(2,1)S(1)}, u32[]{:S(2)}, u32[]{:S(2)}) %collective-permute-start) | collective-permute-done | bytes 131104 | tf_op jit(solution)/shard_map/ppermute | solution.py:611
  9.8 6.1 %collective-permute-start.2 = (bf16[2,8,2,32,128]{4,3,2,1,0:T(8,128)(2,1)S(1)}, bf16[2,8,2,32,128]{4,3,2,1,0:T(8,128)(2,1)S(1)}, u32[]{:S(2)}, u32[]{:S(2)}) collective-permute-start(bf16[2,8,2,32,128]{4,3,2,1,0:T(8,128)(2,1)S(1)} %pad_maximum_fusion), channel_id=1, source_target_pairs={{0,4},{4,8},{8,12},{12,16},{16,20},{20,24},{24,28},{1,5},{5,9},{9,... | collective-permute-start | bytes 786440 | tf_op jit(solution)/shard_map/ppermute | solution.py:611
  16.0 4.7 %collective-permute-start.3 = (bf16[2,8,2,32,128]{4,3,2,1,0:T(8,128)(2,1)S(1)}, bf16[2,8,2,32,128]{4,3,2,1,0:T(8,128)(2,1)S(1)}, u32[]{:S(2)}, u32[]{:S(2)}) collective-permute-start(bf16[2,8,2,32,128]{4,3,2,1,0:T(8,128)(2,1)S(1)} %pad_maximum_fusion.1), channel_id=1, source_target_pairs={{4,0},{8,4},{12,8},{16,12},{20,16},{24,20},{28,24},{5,1},{9,5},{13... | collective-permute-start | bytes 786440 | tf_op jit(solution)/shard_map/ppermute | solution.py:616
  20.7 0.0 copy-start
  20.7 0.0 copy-start.4
  20.7 0.0 copy-start.5
  20.7 0.0 collective-permute-done.2.ylo
  20.8 6.4 %collective-permute-done.3.yhi = bf16[2,8,2,32,128]{4,3,2,1,0:T(8,128)(2,1)S(1)} collective-permute-done((bf16[2,8,2,32,128]{4,3,2,1,0:T(8,128)(2,1)S(1)}, bf16[2,8,2,32,128]{4,3,2,1,0:T(8,128)(2,1)S(1)}, u32[]{:S(2)}, u32[]{:S(2)}) %collective-permute-start.3) | collective-permute-done | bytes 262176 | tf_op jit(solution)/shard_map/ppermute | solution.py:616
  27.1 0.5 shard_map.135.face
  27.6 1.3 collective-permute-start.5
  28.9 4.0 %collective-permute-start.4 = (bf16[2,2,32,128]{3,2,1,0:T(8,128)(2,1)S(1)}, bf16[2,2,32,128]{3,2,1,0:T(8,128)(2,1)S(1)}, u32[]{:S(2)}, u32[]{:S(2)}) collective-permute-start(bf16[2,2,32,128]{3,2,1,0:T(8,128)(2,1)S(1)} %shard_map.135.face), channel_id=1, source_target_pairs={{0,1},{1,2},{2,3},{4,5},{5,6},{6,7},{8,9},{9,10},{10,11},{12,13},{... | collective-permute-start | bytes 98312 | tf_op jit(solution)/shard_map/ppermute | solution.py:611
  32.9 0.1 pad_add_fusion.place
  33.0 0.0 collective-permute-done.5.face_r
  33.0 0.9 collective-permute-done.4.face_l
  33.9 0.0 copy-done.1
  33.9 0.0 copy-done.2
  33.9 3.6 %shard_map.136 = (f32[19,32,768]{2,1,0:T(8,128)S(1)}, bf16[32,64]{1,0:T(8,128)(2,1)S(1)}) custom-call(s32[3]{0:T(128)S(1)} %pad_add_fusion.place, bf16[2,4,4,32,128]{4,3,2,1,0:T(8,128)(2,1)S(1)} %maximum_bitcast_fusion.own, bf16[2,2,4,32,128]{4,3,2,1,0:T(8,128)(2,1)S(1)} %collective-permute-done.xlo, ...), custom_call_target="tpu_custom_call" | custom-call | tf_op jit(solution)/shard_map/pallas_call | solution.py:642
  37.5 1.3 collective-permute-start.7
  38.8 0.1 pad_slice_fusion
  38.9 4.3 %collective-permute-start.6 = (bf16[8,64]{1,0:T(8,128)(2,1)S(1)}, bf16[8,64]{1,0:T(8,128)(2,1)S(1)}, u32[]{:S(2)}, u32[]{:S(2)}) collective-permute-start(bf16[8,64]{1,0:T(8,128)(2,1)S(1)} %get-tuple-element.43), channel_id=1, source_target_pairs={{0,1},{1,2},{2,3},{4,5},{5,6},{6,7},{8,9},{9,10},{10,11},{12,13},{... | collective-permute-start | bytes 3080 | tf_op jit(solution)/shard_map/ppermute | solution.py:611
  43.2 0.0 collective-permute-done.7
  43.2 0.1 fusion
  43.3 0.6 collective-permute-done.6
  43.9 0.1 fusion.1
  44.0 0.1 broadcast_in_dim.10
  44.0 33.3 %all_to_all.15 = bf16[64,24,128]{2,1,0:T(8,128)(2,1)S(1)} all-to-all(bf16[64,24,128]{2,1,0:T(8,128)(2,1)S(1)} %broadcast_in_dim.10), channel_id=1, replica_groups=mesh['gx_0'=8,'gx_1'=2,'gy_0'=4,'gy_1'=2,'gz'=4] {'gx_0','gx_1','gy_0'}, dimensions={0} | all-to-all | bytes 786432 | tf_op jit(solution)/shard_map/all_to_all | solution.py:661
  77.3 5.1 %collective-permute-start.8 = (bf16[16,4,24,128]{3,2,1,0:T(8,128)(2,1)S(1)}, bf16[16,4,24,128]{3,2,1,0:T(8,128)(2,1)S(1)}, u32[]{:S(2)}, u32[]{:S(2)}) collective-permute-start(bf16[16,4,24,128]{3,2,1,0:T(8,128)(2,1)S(1)} %bitcast.19), channel_id=1, source_target_pairs={{0,4},{4,0},{1,5},{5,1},{2,6},{6,2},{3,7},{7,3},{8,12},{12,8},{9,1... | collective-permute-start | bytes 1179656 | tf_op jit(solution)/shard_map/ppermute | solution.py:668
  82.4 1.3 collective-permute-done.8.recv_far
  83.8 0.0 copy-done
  83.8 0.0 copy-done.4
  83.8 0.0 copy-done.5
  83.8 0.0 copy-start.3
  83.8 17.7 %shard_map.137 = (bf16[4,4,32,128]{3,2,1,0:T(8,128)(2,1)S(1)}, bf16[4,4,32,128]{3,2,1,0:T(8,128)(2,1)S(1)}, bf16[16,80,128]{2,1,0:T(8,128)(2,1)S(1)}) custom-call(s32[3]{0:T(128)S(1)} %pad_add_fusion.place, bf16[16,4,24,128]{3,2,1,0:T(8,128)(2,1)S(1)} %bitcast.20, bf16[16,4,24,128]{3,2,1,0:T(8,128)(2,1)S(1)} %collective-permute-done.8.recv_far, ...), custom_call_target="tpu_custom_call" | custom-call | tf_op jit(solution)/shard_map/pallas_call | solution.py:672
  101.5 14.2 %all_to_all.16.recv = bf16[16,80,128]{2,1,0:T(8,128)(2,1)S(1)} all-to-all(bf16[16,80,128]{2,1,0:T(8,128)(2,1)S(1)} %get-tuple-element.21), channel_id=1, replica_groups=mesh['gx_0'=8,'gx_1'=2,'gy_0'=4,'gy_1'=2,'gz'=4] {'gx_0','gx_1'}, dimensions={0} | all-to-all | bytes 655360 | tf_op jit(solution)/shard_map/all_to_all | solution.py:717
  115.7 0.0 copy-done.3
  115.7 1.6 %shard_map.138 = bf16[32,16,128]{2,1,0:T(8,128)(2,1)} custom-call(s32[3]{0:T(128)S(1)} %pad_add_fusion.place, bf16[16,80,128]{2,1,0:T(8,128)(2,1)S(1)} %all_to_all.16.recv, bf16[512,512]{1,0:T(8,128)(2,1)S(1)} %copy-done.3), custom_call_target="tpu_custom_call" | custom-call | tf_op jit(solution)/shard_map/pallas_call | solution.py:718
  117.3 8.3 %all-to-all-start.2 = ((bf16[32,16,128]{2,1,0:T(8,128)(2,1)}), bf16[32,16,128]{2,1,0:T(8,128)(2,1)S(1)}, u32[]{:S(2)}, u32[]{:S(2)}) async-start(bf16[32,16,128]{2,1,0:T(8,128)(2,1)} %shard_map.138), calls=%async_computation.2 | async-start | bytes 262144 | tf_op jit(solution)/shard_map/all_to_all | solution.py:726
  125.5 0.7 copy.17
  126.3 0.7 copy.18
  127.0 9.7 %all-to-all-done.2.recv = bf16[32,16,128]{2,1,0:T(8,128)(2,1)S(1)} async-done(((bf16[32,16,128]{2,1,0:T(8,128)(2,1)}), bf16[32,16,128]{2,1,0:T(8,128)(2,1)S(1)}, u32[]{:S(2)}, u32[]{:S(2)}) %all-to-all-start.2) | async-done | bytes 131104 | tf_op jit(solution)/shard_map/all_to_all | solution.py:726
  136.7 0.8 shard_map.139
  (10 shorter events, 0.2 us)
Async XLA Ops:
  1.7 32.2 %copy-start.1 = (bf16[27,32,32]{2,1,0:T(8,128)(2,1)S(1)}, bf16[27,32,32]{2,1,0:T(8,128)(2,1)}, u32[]{:S(2)}) copy-start(bf16[27,32,32]{2,1,0:T(8,128)(2,1)} %w_fine_in_hbm.1) | copy-start | bytes 165892
  1.7 32.2 %copy-start.2 = (bf16[27,32,32]{2,1,0:T(8,128)(2,1)S(1)}, bf16[27,32,32]{2,1,0:T(8,128)(2,1)}, u32[]{:S(2)}) copy-start(bf16[27,32,32]{2,1,0:T(8,128)(2,1)} %w_fine_out_hbm.1) | copy-start | bytes 165892
  1.8 6.5 %collective-permute-start.1 = (bf16[2,2,4,32,128]{4,3,2,1,0:T(8,128)(2,1)S(1)}, bf16[2,2,4,32,128]{4,3,2,1,0:T(8,128)(2,1)S(1)}, u32[]{:S(2)}, u32[]{:S(2)}) collective-permute-start(bf16[2,2,4,32,128]{4,3,2,1,0:T(8,128)(2,1)S(1)} %get-tuple-element.36), channel_id=1, source_target_pairs={{32,0},{64,32},{96,64},{128,96},{160,128},{192,160},{224,192},{256... | collective-permute-start | bytes 393224 | tf_op jit(solution)/shard_map/ppermute | solution.py:616
  3.2 6.6 %collective-permute-start = (bf16[2,2,4,32,128]{4,3,2,1,0:T(8,128)(2,1)S(1)}, bf16[2,2,4,32,128]{4,3,2,1,0:T(8,128)(2,1)S(1)}, u32[]{:S(2)}, u32[]{:S(2)}) collective-permute-start(bf16[2,2,4,32,128]{4,3,2,1,0:T(8,128)(2,1)S(1)} %get-tuple-element.37), channel_id=1, source_target_pairs={{0,32},{32,64},{64,96},{96,128},{128,160},{160,192},{192,224},{224... | collective-permute-start | bytes 393224 | tf_op jit(solution)/shard_map/ppermute | solution.py:611
  9.8 10.9 %collective-permute-start.2 = (bf16[2,8,2,32,128]{4,3,2,1,0:T(8,128)(2,1)S(1)}, bf16[2,8,2,32,128]{4,3,2,1,0:T(8,128)(2,1)S(1)}, u32[]{:S(2)}, u32[]{:S(2)}) collective-permute-start(bf16[2,8,2,32,128]{4,3,2,1,0:T(8,128)(2,1)S(1)} %pad_maximum_fusion), channel_id=1, source_target_pairs={{0,4},{4,8},{8,12},{12,16},{16,20},{20,24},{24,28},{1,5},{5,9},{9,... | collective-permute-start | bytes 786440 | tf_op jit(solution)/shard_map/ppermute | solution.py:611
  16.0 11.2 %collective-permute-start.3 = (bf16[2,8,2,32,128]{4,3,2,1,0:T(8,128)(2,1)S(1)}, bf16[2,8,2,32,128]{4,3,2,1,0:T(8,128)(2,1)S(1)}, u32[]{:S(2)}, u32[]{:S(2)}) collective-permute-start(bf16[2,8,2,32,128]{4,3,2,1,0:T(8,128)(2,1)S(1)} %pad_maximum_fusion.1), channel_id=1, source_target_pairs={{4,0},{8,4},{12,8},{16,12},{20,16},{24,20},{28,24},{5,1},{9,5},{13... | collective-permute-start | bytes 786440 | tf_op jit(solution)/shard_map/ppermute | solution.py:616
  20.7 63.1 %copy-start = (bf16[27,128,128]{2,1,0:T(8,128)(2,1)S(1)}, bf16[27,128,128]{2,1,0:T(8,128)(2,1)}, u32[]{:S(2)}) copy-start(bf16[27,128,128]{2,1,0:T(8,128)(2,1)} %w_mid_hbm.1) | copy-start | bytes 2654212
  20.7 63.1 %copy-start.4 = (bf16[27,32,128]{2,1,0:T(8,128)(2,1)S(1)}, bf16[27,32,128]{2,1,0:T(8,128)(2,1)}, u32[]{:S(2)}) copy-start(bf16[27,32,128]{2,1,0:T(8,128)(2,1)} %w_in_hbm.1) | copy-start | bytes 663556
  20.7 63.0 %copy-start.5 = (bf16[128,32]{0,1:T(8,128)(2,1)S(1)}, bf16[128,32]{0,1:T(8,128)(2,1)}, u32[]{:S(2)}) copy-start(bf16[128,32]{0,1:T(8,128)(2,1)} %param.13) | copy-start | bytes 24580
  27.6 5.4 %collective-permute-start.5 = (bf16[2,2,32,128]{3,2,1,0:T(8,128)(2,1)S(1)}, bf16[2,2,32,128]{3,2,1,0:T(8,128)(2,1)S(1)}, u32[]{:S(2)}, u32[]{:S(2)}) collective-permute-start(bf16[2,2,32,128]{3,2,1,0:T(8,128)(2,1)S(1)} %shard_map.135.face), channel_id=1, source_target_pairs={{1,0},{2,1},{3,2},{5,4},{6,5},{7,6},{9,8},{10,9},{11,10},{13,12},{... | collective-permute-start | bytes 98312 | tf_op jit(solution)/shard_map/ppermute | solution.py:616
  28.9 5.0 %collective-permute-start.4 = (bf16[2,2,32,128]{3,2,1,0:T(8,128)(2,1)S(1)}, bf16[2,2,32,128]{3,2,1,0:T(8,128)(2,1)S(1)}, u32[]{:S(2)}, u32[]{:S(2)}) collective-permute-start(bf16[2,2,32,128]{3,2,1,0:T(8,128)(2,1)S(1)} %shard_map.135.face), channel_id=1, source_target_pairs={{0,1},{1,2},{2,3},{4,5},{5,6},{6,7},{8,9},{9,10},{10,11},{12,13},{... | collective-permute-start | bytes 98312 | tf_op jit(solution)/shard_map/ppermute | solution.py:611
  37.5 5.7 %collective-permute-start.7 = (bf16[8,64]{1,0:T(8,128)(2,1)S(1)}, bf16[8,64]{1,0:T(8,128)(2,1)S(1)}, u32[]{:S(2)}, u32[]{:S(2)}) collective-permute-start(bf16[8,64]{1,0:T(8,128)(2,1)S(1)} %get-tuple-element.42), channel_id=1, source_target_pairs={{1,0},{2,1},{3,2},{5,4},{6,5},{7,6},{9,8},{10,9},{11,10},{13,12},{... | collective-permute-start | bytes 3080 | tf_op jit(solution)/shard_map/ppermute | solution.py:616
  38.9 5.0 %collective-permute-start.6 = (bf16[8,64]{1,0:T(8,128)(2,1)S(1)}, bf16[8,64]{1,0:T(8,128)(2,1)S(1)}, u32[]{:S(2)}, u32[]{:S(2)}) collective-permute-start(bf16[8,64]{1,0:T(8,128)(2,1)S(1)} %get-tuple-element.43), channel_id=1, source_target_pairs={{0,1},{1,2},{2,3},{4,5},{5,6},{6,7},{8,9},{9,10},{10,11},{12,13},{... | collective-permute-start | bytes 3080 | tf_op jit(solution)/shard_map/ppermute | solution.py:611
  77.3 6.5 %collective-permute-start.8 = (bf16[16,4,24,128]{3,2,1,0:T(8,128)(2,1)S(1)}, bf16[16,4,24,128]{3,2,1,0:T(8,128)(2,1)S(1)}, u32[]{:S(2)}, u32[]{:S(2)}) collective-permute-start(bf16[16,4,24,128]{3,2,1,0:T(8,128)(2,1)S(1)} %bitcast.19), channel_id=1, source_target_pairs={{0,4},{4,0},{1,5},{5,1},{2,6},{6,2},{3,7},{7,3},{8,12},{12,8},{9,1... | collective-permute-start | bytes 1179656 | tf_op jit(solution)/shard_map/ppermute | solution.py:668
  83.8 31.9 %copy-start.3 = (bf16[512,512]{1,0:T(8,128)(2,1)S(1)}, bf16[512,512]{1,0:T(8,128)(2,1)}, u32[]{:S(2)}) copy-start(bf16[512,512]{1,0:T(8,128)(2,1)} %constant.27.clone.perm) | copy-start | bytes 1572868
  117.3 19.4 %all-to-all-start.2 = ((bf16[32,16,128]{2,1,0:T(8,128)(2,1)}), bf16[32,16,128]{2,1,0:T(8,128)(2,1)S(1)}, u32[]{:S(2)}, u32[]{:S(2)}) async-start(bf16[32,16,128]{2,1,0:T(8,128)(2,1)} %shard_map.138), calls=%async_computation.2 | async-start | bytes 262144 | tf_op jit(solution)/shard_map/all_to_all | solution.py:726
